TPU v7x, 32 devices: a whole 2x2x4 slice. The times are simulated.
32 devices in a mesh: groups: 2 (over x), owner: 8 (over z, y), slab: 2 (over core).
Axes of the slice: x: 2, y: 2, z: 4, core: 2. Of those that a mesh axis runs over, the one named last changes fastest.
Arguments:
- queries: bfloat16 [16, 4, 112, 2560], P(('groups', 'owner'), 'slab'), parts along dimension 0, may hold values from -40 to 40
- key_value: bfloat16 [2, 16, 4, 112, 2560], P(None, ('groups', 'owner'), 'slab'), parts along dimension 1, may hold values from -8 to 8
- keep: int32 [8], P('groups'), parts along dimension 0, may hold values 0 or 1
- windows: int32 [8, 3], P('groups'), parts along dimension 0, may hold values from 0 to 7, as said below
- gate: float32 [8, 5120], P('groups'), parts along dimension 0, may hold values from -1.5 to 1.5
- out_weight: bfloat16 [2560, 5120], P('owner'), may hold values from -0.125 to 0.125
Outputs:
- output: bfloat16 [16, 4, 112, 5120], P(('groups', 'owner'), 'slab'), parts along dimension 0
There are 2 independent parts, one for each index of `groups`. A program takes and returns all parts, laid end to end along the dimension named above; an argument that names none is the same for every part. Nothing has to cross between parts.
Inputs may be any that keep to these rules, and one draw needn't show every extreme that they name: `windows`: column 0 runs from 0 to 1, column 1 from 1 to 4, column 2 from 1 to 7; the first request takes the largest value of each column.
All inputs are finite; a program needn't handle non-finite values.
Results may differ from a plain program's by a relative error of at most 0.0057.
Values may be sent and summed in bfloat16 or wider, within the bound.
No kernel may reach another device: no remote copies, remote signals or barrier semaphores. Data moves between devices by JAX's collectives and lax.ppermute only.
A program may use at most 128 MiB of HBM per device.

v0:
```python
import functools
import math

import jax
import jax.numpy as jnp
import numpy as np
from jax import lax
from jax.experimental import pallas as pl
from jax.experimental.pallas import tpu as pltpu
from jax.sharding import PartitionSpec as P

HEAD_DIM = 128
WB = 14
HALO = 1
LANES = 128
NEG_LARGE = -1e30
PARTS = 2
FLIGHT = 2
MIB = 1024 * 1024
ANYWHERE = pl.BlockSpec(memory_space=pl.ANY)
IN_HBM = pl.BlockSpec(memory_space=pltpu.HBM)
IN_VMEM = pl.BlockSpec(memory_space=pltpu.VMEM)
IN_SMEM = pl.BlockSpec(memory_space=pltpu.SMEM)


def ring_order(count):
    width = max(w for w in range(1, count + 1) if count % w == 0 and w * w <= count)
    height = count // width
    if width == 1 or height % 2:
        return list(range(count))
    order = []
    for row in range(height):
        columns = range(1, width) if row % 2 == 0 else range(width - 1, 0, -1)
        order += [row * width + column for column in columns]
    return order + [row * width for row in range(height - 1, -1, -1)]


def piece_widths(half_width):
    tiles = half_width // (2 * LANES)
    late = 3 * tiles // 10
    return [count * LANES for count in (tiles - late, late) if count]


def swap(value, axes):
    count = math.prod(lax.axis_size(axis) for axis in axes)
    return lax.ppermute(value, axes, [(i, count - 1 - i) for i in range(count)])


def after(value, *others):
    return lax.optimization_barrier((value,) + others)[0]


def run_copies(copies):
    for copy in copies:
        copy.start()
    for copy in copies:
        copy.wait()


def cut_kernel(first, total, with_border, weight_ref, key_value_ref, *refs):
    out_refs, done = refs[:-1], refs[-1]
    slab = lax.axis_index("slab")
    width = out_refs[0].shape[1]
    sources = []
    for strip in range(2):
        column = lax.axis_index("groups") * total + first + (1 - slab if strip else slab) * width
        sources.append(weight_ref.at[:, pl.ds(pl.multiple_of(column, LANES), width)])
    if with_border:
        frames_here = key_value_ref.shape[2]
        frame = jnp.where(slab == 0, frames_here - HALO, 0)
        width = out_refs[-1].shape[3]
        for part in range(PARTS):
            sources.append(key_value_ref.at[:, 0, pl.ds(frame, HALO), :, part * width : (part + 1) * width])
    run_copies([pltpu.make_async_copy(s, t, done.at[i]) for i, (s, t) in enumerate(zip(sources, out_refs))])


def cut(out_weight, key_value, width, first, total, with_border):
    depth = out_weight.shape[0]
    kinds, _, _, spots, features = key_value.shape
    shapes = [(depth, width)] * 2
    shapes += [(kinds, HALO, spots, features // PARTS)] * PARTS if with_border else []
    out_weight = pltpu.with_memory_space_constraint(out_weight, pltpu.HBM)
    key_value = pltpu.with_memory_space_constraint(key_value, pltpu.HBM)
    outs = pl.pallas_call(
        functools.partial(cut_kernel, first, total, with_border),
        out_shape=[jax.ShapeDtypeStruct(shape, jnp.bfloat16) for shape in shapes],
        in_specs=[IN_HBM] * 2,
        out_specs=[IN_VMEM] * len(shapes),
        scratch_shapes=[pltpu.SemaphoreType.DMA((len(shapes),))],
        compiler_params=pltpu.CompilerParams(vmem_limit_bytes=4 * MIB),
        cost_estimate=pl.CostEstimate(flops=0, bytes_accessed=8 * depth * width, transcendentals=0),
        name="cut",
    )(out_weight, key_value)
    return outs[:2], [edge.reshape(kinds, HALO * spots, features // PARTS) for edge in outs[2:]]


def scale_kernel(keep_ref, gate_ref, out_ref):
    owner = lax.axis_index("owner")
    factor = jnp.where(owner % 2 == 1, keep_ref[owner // 2], 1).astype(jnp.float32)
    out_ref[...] = gate_ref[pl.ds(owner // 2, 1), :] * factor


def scale_gate(keep, gate):
    return pl.pallas_call(
        scale_kernel,
        out_shape=jax.ShapeDtypeStruct((1, gate.shape[1]), jnp.float32),
        in_specs=[IN_SMEM, IN_VMEM],
        out_specs=IN_VMEM,
        compiler_params=pltpu.CompilerParams(vmem_limit_bytes=MIB),
        name="scale_gate",
    )(keep, gate)


def token_place(count, dim, spots, first_frame):
    shape = (count, 1) if dim == 0 else (1, count)
    token = lax.broadcasted_iota(jnp.int32, shape, dim).astype(jnp.float32)
    frame = jnp.floor((token + 0.5) * (1.0 / spots))
    spot = token - frame * spots
    row = jnp.floor((spot + 0.5) * (1.0 / WB))
    return frame + first_frame, row, spot - row * WB


def attend_kernel(spots, windows_ref, q_ref, k_ref, v_ref, k_halo_ref, v_halo_ref, *refs):
    out_ref, bias = refs[-2:]
    rows = q_ref.shape[0]
    halo_rows = k_halo_ref.shape[0]
    keys = bias.shape[1]
    frames_here = rows // spots

    @pl.when(pl.program_id(0) == 0)
    def _():
        request = lax.axis_index("owner") // 2
        halo_frame = jnp.where(lax.axis_index("slab") == 0, 0, -HALO - frames_here).astype(jnp.float32)
        query = token_place(rows, 0, spots, 0.0)
        key = token_place(keys, 1, spots, 0.0)
        index = lax.broadcasted_iota(jnp.int32, (1, keys), 1)
        frame = jnp.where(index < rows, key[0], key[0] + halo_frame)
        frame = jnp.where(index < rows + halo_rows, frame, -NEG_LARGE)
        allowed = None
        for part, place in enumerate((frame, key[1], key[2])):
            near = jnp.abs(query[part] - place) <= windows_ref[request, part].astype(jnp.float32)
            allowed = near if allowed is None else allowed & near
        bias[...] = jnp.where(allowed, 0.0, NEG_LARGE)

    scale = math.log2(math.e) / math.sqrt(HEAD_DIM)
    pad = jnp.zeros((keys - rows - halo_rows, HEAD_DIM), jnp.bfloat16)
    ones = jnp.ones((keys, HEAD_DIM), jnp.bfloat16)
    for head in range(q_ref.shape[1] // HEAD_DIM):
        at = slice(head * HEAD_DIM, (head + 1) * HEAD_DIM)
        key = jnp.concatenate([k_ref[:, at], k_halo_ref[:, at], pad], axis=0)
        value = jnp.concatenate([v_ref[:, at], v_halo_ref[:, at], pad], axis=0)
        value = jnp.concatenate([value, ones], axis=1)
        score = lax.dot_general(q_ref[:, at], key, (((1,), (1,)), ((), ())), preferred_element_type=jnp.float32)
        score = score * scale + bias[...]
        weight = jnp.exp2(score - jnp.max(score, axis=1, keepdims=True)).astype(jnp.bfloat16)
        mixture = jnp.dot(weight, value, preferred_element_type=jnp.float32)
        out_ref[:, at] = (mixture[:, :HEAD_DIM] / mixture[:, HEAD_DIM:]).astype(jnp.bfloat16)


def attend(query_rows, key_value_rows, halo, windows, spots, part, attended):
    before = [] if attended is None else [attended]
    rows, features = query_rows.shape
    query_rows = pltpu.with_memory_space_constraint(query_rows, pltpu.HBM)
    width = features // PARTS
    heads = width // HEAD_DIM
    steps = 2 if heads % 2 == 0 else 1
    block = width // steps
    halo_rows = halo.shape[1]
    first = part * steps
    keys = pl.cdiv(rows + halo_rows, LANES) * LANES
    return pl.pallas_call(
        functools.partial(attend_kernel, spots),
        grid=(steps,),
        out_shape=jax.ShapeDtypeStruct((rows, features), jnp.bfloat16),
        in_specs=[
            IN_SMEM,
            pl.BlockSpec((rows, block), lambda i: (0, first + i)),
            pl.BlockSpec((None, rows, block), lambda i: (0, 0, first + i)),
            pl.BlockSpec((None, rows, block), lambda i: (1, 0, first + i)),
            pl.BlockSpec((None, halo_rows, block), lambda i: (0, 0, i)),
            pl.BlockSpec((None, halo_rows, block), lambda i: (1, 0, i)),
        ]
        + [ANYWHERE] * len(before),
        out_specs=pl.BlockSpec((rows, block), lambda i: (0, first + i)),
        input_output_aliases={6: 0} if before else {},
        scratch_shapes=[pltpu.VMEM((rows, keys), jnp.float32)],
        compiler_params=pltpu.CompilerParams(vmem_limit_bytes=10 * MIB),
        cost_estimate=pl.CostEstimate(
            flops=32 * rows * keys * width, bytes_accessed=2 * width * (2 * rows + 2 * keys), transcendentals=heads * rows * keys
        ),
        name="attend",
    )(windows, query_rows, key_value_rows, key_value_rows, halo, halo, *before)


def arrange_kernel(near_ref, far_ref, out_ref):
    rows = near_ref.shape[0]
    depth = out_ref.shape[2]
    for owner in range(out_ref.shape[0]):
        at = slice(owner * depth, (owner + 1) * depth)
        out_ref[owner, :rows] = near_ref[:, at]
        out_ref[owner, rows:] = far_ref[:, at]


def arrange(near, far, count):
    rows, features = near.shape
    return pl.pallas_call(
        arrange_kernel,
        out_shape=jax.ShapeDtypeStruct((count, 2 * rows, features // count), near.dtype),
        in_specs=[IN_VMEM] * 2,
        out_specs=IN_VMEM,
        compiler_params=pltpu.CompilerParams(vmem_limit_bytes=8 * MIB),
        cost_estimate=pl.CostEstimate(flops=0, bytes_accessed=8 * near.size, transcendentals=0),
        name="arrange",
    )(near, far)


def project_kernel(strip, column, total, tables_ref, rows_ref, *refs):
    count = tables_ref.shape[2]
    w_refs, gate_refs, out_refs = refs[:count], refs[count : count + 2], refs[count + 2 :]
    owner, slab = lax.axis_index("owner"), lax.axis_index("slab")
    rows, width = out_refs[0].shape
    sources = [tables_ref[slab, owner, index] for index in range(count)]
    place = lax.axis_index("groups") * total + column + (1 - slab if strip else slab) * width
    for first in range(0, width, 2 * LANES):
        tile = min(2 * LANES, width - first)
        product = None
        for source, w_ref in zip(sources, w_refs):
            term = jnp.dot(rows_ref[source], w_ref[:, first : first + tile], preferred_element_type=jnp.float32)
            product = term if product is None else product + term
        here = pl.ds(pl.multiple_of(place + first, LANES), tile)
        for block in range(2):
            gate = gate_refs[block][:, here]
            result = product[block * rows : (block + 1) * rows] * gate
            out_refs[block][:, first : first + tile] = result.astype(jnp.bfloat16)


def project(table, arranged, chunks, gates, strip, column, total):
    count, rows, depth = arranged.shape
    width = chunks[0].shape[1]
    return pl.pallas_call(
        functools.partial(project_kernel, strip, column, total),
        out_shape=[jax.ShapeDtypeStruct((rows // 2, width), jnp.bfloat16)] * 2,
        in_specs=[IN_SMEM] + [IN_VMEM] * (1 + count + 2),
        out_specs=[IN_VMEM] * 2,
        compiler_params=pltpu.CompilerParams(vmem_limit_bytes=16 * MIB),
        cost_estimate=pl.CostEstimate(
            flops=3 * rows * width * depth * count,
            bytes_accessed=2 * (rows * (depth * count + width) + count * depth * width),
            transcendentals=0,
        ),
        name="project",
    )(table, arranged, *chunks, *gates)


def place_kernel(count, columns, total, *refs):
    in_refs, (out_ref, done) = refs[:count], refs[-2:]
    group, slab = lax.axis_index("groups"), lax.axis_index("slab")
    copies = []
    for index, in_ref in enumerate(in_refs):
        strip, away = divmod(index, 2)
        width = in_ref.shape[1]
        start = (1 - group if away else group) * total + columns[strip][0] + (1 - slab if columns[strip][1] else slab) * width
        at = pl.ds(pl.multiple_of(start, LANES), width)
        copies.append(pltpu.make_async_copy(in_ref, out_ref.at[:, at], done.at[index]))
    run_copies(copies)


def place(blocks, out, columns, total, model_width):
    rows = blocks[0].shape[0]
    held = [] if out is None else [out]
    return pl.pallas_call(
        functools.partial(place_kernel, len(blocks), columns, total),
        out_shape=jax.ShapeDtypeStruct((rows, model_width), jnp.bfloat16),
        in_specs=[IN_VMEM] * len(blocks) + [ANYWHERE] * len(held),
        out_specs=ANYWHERE,
        scratch_shapes=[pltpu.SemaphoreType.DMA((len(blocks),))],
        input_output_aliases={len(blocks): 0} if held else {},
        compiler_params=pltpu.CompilerParams(vmem_limit_bytes=4 * MIB),
        cost_estimate=pl.CostEstimate(flops=0, bytes_accessed=4 * sum(block.size for block in blocks), transcendentals=0),
        name="place",
    )(*blocks, *held)


def hop_order(pieces, turns):
    order = []
    for piece in range(pieces):
        hops = [(piece, strip, turn) for turn in range(1, turns[0] + 1) for strip in range(2) if turn <= turns[strip]]
        order = order[:-1] + hops[:1] + order[-1:] + hops[1:] if order else hops
    return order


def on_device(queries, key_value, keep, windows, gate, out_weight):
    frames_here, spots, features = queries.shape[1:]
    model_width = gate.shape[1]
    rows = frames_here * spots
    slabs = lax.axis_size("slab")
    total = model_width // lax.axis_size("groups")
    widths = piece_widths(total)

    count = lax.axis_size("owner")
    order = ring_order(count)
    spot_of = [order.index(owner) for owner in range(count)]
    ring = [
        (owner * slabs + slab, order[(spot_of[owner] + step) % count] * slabs + slab)
        for owner in range(count)
        for slab, step in enumerate((1, -1))
    ]
    turns = (count // 2, (count - 1) // 2)
    hops = hop_order(len(widths), turns)

    firsts = [2 * sum(widths[:piece]) for piece in range(len(widths))]
    held, arrived, crossed, edges = {}, [], {}, []
    for piece, width in enumerate(widths):
        own_strips, border = cut(out_weight, key_value, width, firsts[piece], total, piece == 0)
        edges = border or edges
        for strip, own in enumerate(own_strips):
            held[piece, strip, 0] = own

    def hop(slot, *others):
        if slot >= len(hops):
            return
        piece, strip, turn = hops[slot]
        waits = list(others)
        if slot >= FLIGHT:
            waits.append(arrived[slot - FLIGHT])
        if slot > 2 * FLIGHT:
            waits.append(crossed[hops[slot - 2 * FLIGHT - 1]])
        value = held[piece, strip, turn - 1]
        if waits:
            value = after(value, *waits)
        value = lax.ppermute(value, ("owner", "slab"), ring)
        held[hops[slot]] = value
        arrived.append(value)

    def cross(slot, *others):
        value = arrived[slot]
        crossed[hops[slot]] = swap(after(value, *others) if others else value, ("slab",))

    first_done = max(slot for slot, at in enumerate(hops) if at[0] == 0) if hops else 0
    halos = [swap(edge, ("slab",)) for edge in edges]
    for slot in range(FLIGHT):
        hop(slot)

    query_rows = queries.reshape(rows, features)
    key_value_rows = key_value.reshape(2, rows, features)
    waits, attended = {FLIGHT + 2: [held[piece, 0, 0] for piece in range(1, len(widths))]}, None
    for part in range(PARTS):
        attended = attend(query_rows, key_value_rows, halos[part], windows, spots, part, attended)
    a_blocks = (attended, swap(attended, ("groups",)))
    near_gate = scale_gate(after(keep, attended), gate)
    gates = (near_gate, swap(near_gate, ("groups",)))
    waits.setdefault(FLIGHT, []).append(attended)
    waits.setdefault(first_done - 1, []).append(a_blocks[1])

    arranged = arrange(*a_blocks, count)

    def project_strip(piece, strip, *others):
        chunks, sources = [], []
        for turn in range(turns[strip] + 1):
            chunks.append(held[piece, strip, turn])
            sources.append((-turn, turn))
        for turn in range(1, turns[1 - strip] + 1):
            chunks.append(crossed[piece, 1 - strip, turn])
            sources.append((turn, -turn))
        table = np.zeros((slabs, count, len(chunks)), np.int32)
        for slab in range(slabs):
            for owner in range(count):
                table[slab, owner] = [order[(spot_of[owner] + source[slab]) % count] for source in sources]
        if others:
            chunks[0] = after(chunks[0], *others)
        own, away = project(jnp.asarray(table), arranged, chunks, gates, strip, firsts[piece], total)
        return [own, swap(away, ("groups",))]

    results, needs = {}, {}
    if first_done >= 2 and first_done + 1 < len(hops):
        needs[first_done - 2] = [first_done - 1, gates[1], arranged]
    for slot in range(FLIGHT, len(hops)):
        strip = slot - first_done - 3
        if 0 <= strip < 2:
            results[0, strip] = project_strip(0, strip, *(arrived[first_done + 1 : first_done + 2] if strip else []))
            waits.setdefault(slot, []).append(results[0, strip][0])
            if strip:
                needs[len(hops) - 2] = [results[0, strip][1]]
            else:
                needs[first_done + 1] = [results[0, strip][0]]
                waits.setdefault(len(hops) - 1, []).append(results[0, strip][1])
        others = needs.get(slot - FLIGHT, [])
        cross(slot - FLIGHT, *(arrived[other] if isinstance(other, int) else other for other in others))
        hop(slot, *waits.get(slot, []))
    for slot in range(max(len(hops) - FLIGHT, 0), len(hops)):
        cross(slot, *needs.get(slot, []))
    for piece in range(len(widths)):
        for strip in range(2):
            if (piece, strip) not in results:
                results[piece, strip] = project_strip(piece, strip)
    out = None
    last = (len(widths) - 1, 1)
    for batch in ([key for key in results if key != last], [last]):
        blocks = [block for key in batch for block in results[key]]
        out = place(blocks, out, [(firsts[piece], strip) for piece, strip in batch], total, model_width)
    return out.reshape((1, frames_here, spots, model_width))


def solution(mesh):
    placed = (
        P(("groups", "owner"), "slab", None, None),
        P(None, ("groups", "owner"), "slab", None, None),
        P("groups"),
        P("groups", None),
        P("groups", None),
        P("owner", None),
    )
    return jax.shard_map(
        on_device,
        mesh=mesh,
        in_specs=placed,
        out_specs=P(("groups", "owner"), "slab", None, None),
        check_vma=False,
    )
```

profile of v0, /device:TPU:0, one launch (start us, length us, event | category | flops | bytes accessed | tf_op | source)
XLA Modules:
  0.0 104.6 jit_solution(10442609451794854778)
XLA Ops:
  0.0 1.8 %cut.2 = (bf16[320,896]{1,0:T(8,128)(2,1)S(1)}, bf16[320,896]{1,0:T(8,128)(2,1)S(1)}, bf16[2,1,112,1280]{3,2,1,0:T(8,128)(2,1)S(1)}, bf16[2,1,112,1280]{3,2,1,0:T(8,128)(2,1)S(1)}) custom-call(bf16[320,5120]{1,0:T(8,128)(2,1)} %weight_ref.3, bf16[2,1,2,112,2560]{4,3,2,1,0:T(8,128)(2,1)} %key_value_ref.3), custom_call_target="tpu_custom_call" | custom-call | bytes 2293760 | tf_op jit(solution)/shard_map/cut/pallas_call | solution.py:84
  2.4 2.9 %collective-permute-start.3 = (bf16[320,896]{1,0:T(8,128)(2,1)S(1)}, bf16[320,896]{1,0:T(8,128)(2,1)S(1)}, u32[]{:S(2)}, u32[]{:S(2)}) collective-permute-start(bf16[320,896]{1,0:T(8,128)(2,1)S(1)} %get-tuple-element.40.refs_0_), channel_id=1, source_target_pairs={{0,2},{1,5},{2,6},{3,1},{4,0},{5,9},{6,10},{7,3},{8,4},{9,13},{10,... | collective-permute-start | bytes 1720328 | tf_op jit(solution)/shard_map/ppermute | solution.py:331
  5.3 1.6 %collective-permute-start.6 = (bf16[320,896]{1,0:T(8,128)(2,1)S(1)}, bf16[320,896]{1,0:T(8,128)(2,1)S(1)}, u32[]{:S(2)}, u32[]{:S(2)}) collective-permute-start(bf16[320,896]{1,0:T(8,128)(2,1)S(1)} %get-tuple-element.55.refs_0_), channel_id=1, source_target_pairs={{0,2},{1,5},{2,6},{3,1},{4,0},{5,9},{6,10},{7,3},{8,4},{9,13},{10,... | collective-permute-start | bytes 1720328 | tf_op jit(solution)/shard_map/ppermute | solution.py:331
  6.9 3.4 %attend.2.refs_0_ = bf16[224,2560]{1,0:T(8,128)(2,1)S(1)} custom-call(s32[4,3]{1,0:T(4,128)S(1)} %copy-done.3, bf16[224,2560]{1,0:T(8,128)(2,1)} %bitcast.11, bf16[2,224,2560]{2,1,0:T(8,128)(2,1)S(1)} %bitcast.5, bf16[2,224,2560]{2,1,0:T(8,128)(2,1)S(1)} %bitcast.6, bf16[2,112,1280]{2,1,0:T(8,128)(2,1)S(1)} %collective-permute-done.1.k_halo_ref.v_halo_ref, ...), custom_call_target="tpu_custom_call" | custom-call | flops 3523215360 | bytes 3112960 | tf_op jit(solution)/shard_map/attend/pallas_call | solution.py:171
  10.3 3.4 %attend.3.near_ref = bf16[224,2560]{1,0:T(8,128)(2,1)S(1)} custom-call(s32[4,3]{1,0:T(4,128)S(1)} %copy-done.3, bf16[224,2560]{1,0:T(8,128)(2,1)} %bitcast.12, bf16[2,224,2560]{2,1,0:T(8,128)(2,1)S(1)} %bitcast.7, bf16[2,224,2560]{2,1,0:T(8,128)(2,1)S(1)} %bitcast.8, ...), custom_call_target="tpu_custom_call", output_to_operand_aliasing={{}: (6, {})} | custom-call | flops 3523215360 | bytes 3112960 | tf_op jit(solution)/shard_map/attend/pallas_call | solution.py:171
  13.7 1.6 %collective-permute-start.4 = (bf16[320,896]{1,0:T(8,128)(2,1)S(1)}, bf16[320,896]{1,0:T(8,128)(2,1)S(1)}, u32[]{:S(2)}, u32[]{:S(2)}) collective-permute-start(bf16[320,896]{1,0:T(8,128)(2,1)S(1)} %collective-permute-done.3.refs_1_), channel_id=1, source_target_pairs={{0,2},{1,5},{2,6},{3,1},{4,0},{5,9},{6,10},{7,3},{8,4},{9,13},{10,... | collective-permute-start | bytes 1720328 | tf_op jit(solution)/shard_map/ppermute | solution.py:331
  15.3 3.9 %collective-permute-done.6.refs_1_ = bf16[320,896]{1,0:T(8,128)(2,1)S(1)} collective-permute-done((bf16[320,896]{1,0:T(8,128)(2,1)S(1)}, bf16[320,896]{1,0:T(8,128)(2,1)S(1)}, u32[]{:S(2)}, u32[]{:S(2)}) %collective-permute-start.6) | collective-permute-done | bytes 573472 | tf_op jit(solution)/shard_map/ppermute | solution.py:331
  19.2 2.0 %collective-permute-start.9 = (bf16[320,896]{1,0:T(8,128)(2,1)S(1)}, bf16[320,896]{1,0:T(8,128)(2,1)S(1)}, u32[]{:S(2)}, u32[]{:S(2)}) collective-permute-start(bf16[320,896]{1,0:T(8,128)(2,1)S(1)} %collective-permute-done.6.refs_1_), channel_id=1, source_target_pairs={{0,2},{1,5},{2,6},{3,1},{4,0},{5,9},{6,10},{7,3},{8,4},{9,13},{10,... | collective-permute-start | bytes 1720328 | tf_op jit(solution)/shard_map/ppermute | solution.py:331
  23.8 1.6 %collective-permute-done.4.refs_2_ = bf16[320,896]{1,0:T(8,128)(2,1)S(1)} collective-permute-done((bf16[320,896]{1,0:T(8,128)(2,1)S(1)}, bf16[320,896]{1,0:T(8,128)(2,1)S(1)}, u32[]{:S(2)}, u32[]{:S(2)}) %collective-permute-start.4) | collective-permute-done | bytes 573472 | tf_op jit(solution)/shard_map/ppermute | solution.py:331
  25.4 2.0 %collective-permute-start.5 = (bf16[320,896]{1,0:T(8,128)(2,1)S(1)}, bf16[320,896]{1,0:T(8,128)(2,1)S(1)}, u32[]{:S(2)}, u32[]{:S(2)}) collective-permute-start(bf16[320,896]{1,0:T(8,128)(2,1)S(1)} %collective-permute-done.4.refs_2_), channel_id=1, source_target_pairs={{0,2},{1,5},{2,6},{3,1},{4,0},{5,9},{6,10},{7,3},{8,4},{9,13},{10,... | collective-permute-start | bytes 1720328 | tf_op jit(solution)/shard_map/ppermute | solution.py:331
  27.3 4.2 %collective-permute-done.9.refs_2_ = bf16[320,896]{1,0:T(8,128)(2,1)S(1)} collective-permute-done((bf16[320,896]{1,0:T(8,128)(2,1)S(1)}, bf16[320,896]{1,0:T(8,128)(2,1)S(1)}, u32[]{:S(2)}, u32[]{:S(2)}) %collective-permute-start.9) | collective-permute-done | bytes 573472 | tf_op jit(solution)/shard_map/ppermute | solution.py:331
  31.5 2.0 %collective-permute-start.13 = (bf16[320,896]{1,0:T(8,128)(2,1)S(1)}, bf16[320,896]{1,0:T(8,128)(2,1)S(1)}, u32[]{:S(2)}, u32[]{:S(2)}) collective-permute-start(bf16[320,896]{1,0:T(8,128)(2,1)S(1)} %collective-permute-done.9.refs_2_), channel_id=1, source_target_pairs={{0,2},{1,5},{2,6},{3,1},{4,0},{5,9},{6,10},{7,3},{8,4},{9,13},{10,... | collective-permute-start | bytes 1720328 | tf_op jit(solution)/shard_map/ppermute | solution.py:331
  34.0 3.7 %collective-permute-done.5.refs_3_ = bf16[320,896]{1,0:T(8,128)(2,1)S(1)} collective-permute-done((bf16[320,896]{1,0:T(8,128)(2,1)S(1)}, bf16[320,896]{1,0:T(8,128)(2,1)S(1)}, u32[]{:S(2)}, u32[]{:S(2)}) %collective-permute-start.5) | collective-permute-done | bytes 573472 | tf_op jit(solution)/shard_map/ppermute | solution.py:331
  37.6 6.1 %collective-permute-done.13.refs_3_ = bf16[320,896]{1,0:T(8,128)(2,1)S(1)} collective-permute-done((bf16[320,896]{1,0:T(8,128)(2,1)S(1)}, bf16[320,896]{1,0:T(8,128)(2,1)S(1)}, u32[]{:S(2)}, u32[]{:S(2)}) %collective-permute-start.13) | collective-permute-done | bytes 573472 | tf_op jit(solution)/shard_map/ppermute | solution.py:331
  43.8 2.0 %collective-permute-start.15 = (bf16[320,896]{1,0:T(8,128)(2,1)S(1)}, bf16[320,896]{1,0:T(8,128)(2,1)S(1)}, u32[]{:S(2)}, u32[]{:S(2)}) collective-permute-start(bf16[320,896]{1,0:T(8,128)(2,1)S(1)} %collective-permute-done.5.refs_3_), channel_id=1, source_target_pairs={{0,2},{1,5},{2,6},{3,1},{4,0},{5,9},{6,10},{7,3},{8,4},{9,13},{10,... | collective-permute-start | bytes 1720328 | tf_op jit(solution)/shard_map/ppermute | solution.py:331
  45.8 3.1 %collective-permute-done.2.far_ref = bf16[224,2560]{1,0:T(8,128)(2,1)S(1)} collective-permute-done((bf16[224,2560]{1,0:T(8,128)(2,1)S(1)}, bf16[224,2560]{1,0:T(8,128)(2,1)S(1)}, u32[]{:S(2)}, u32[]{:S(2)}) %collective-permute-start.2) | collective-permute-done | bytes 1146912 | tf_op jit(solution)/shard_map/ppermute | solution.py:46
  48.9 1.6 %collective-permute-start.8 = (bf16[320,384]{1,0:T(8,128)(2,1)S(1)}, bf16[320,384]{1,0:T(8,128)(2,1)S(1)}, u32[]{:S(2)}, u32[]{:S(2)}) collective-permute-start(bf16[320,384]{1,0:T(8,128)(2,1)S(1)} %get-tuple-element.44.refs_0_), channel_id=1, source_target_pairs={{0,2},{1,5},{2,6},{3,1},{4,0},{5,9},{6,10},{7,3},{8,4},{9,13},{10,... | collective-permute-start | bytes 737288 | tf_op jit(solution)/shard_map/ppermute | solution.py:331
  53.3 1.6 %collective-permute-done.16.refs_9_ = f32[1,5120]{1,0:T(1,128)S(1)} collective-permute-done((f32[1,5120]{1,0:T(1,128)S(1)}, f32[1,5120]{1,0:T(1,128)S(1)}, u32[]{:S(2)}, u32[]{:S(2)}) %collective-permute-start.16) | collective-permute-done | bytes 20512 | tf_op jit(solution)/shard_map/ppermute | solution.py:46
  56.7 2.0 %collective-permute-start.11 = (bf16[320,384]{1,0:T(8,128)(2,1)S(1)}, bf16[320,384]{1,0:T(8,128)(2,1)S(1)}, u32[]{:S(2)}, u32[]{:S(2)}) collective-permute-start(bf16[320,384]{1,0:T(8,128)(2,1)S(1)} %get-tuple-element.46.refs_0_), channel_id=1, source_target_pairs={{0,2},{1,5},{2,6},{3,1},{4,0},{5,9},{6,10},{7,3},{8,4},{9,13},{10,... | collective-permute-start | bytes 737288 | tf_op jit(solution)/shard_map/ppermute | solution.py:331
  58.6 4.2 %collective-permute-done.11.refs_1_ = bf16[320,384]{1,0:T(8,128)(2,1)S(1)} collective-permute-done((bf16[320,384]{1,0:T(8,128)(2,1)S(1)}, bf16[320,384]{1,0:T(8,128)(2,1)S(1)}, u32[]{:S(2)}, u32[]{:S(2)}) %collective-permute-start.11) | collective-permute-done | bytes 245792 | tf_op jit(solution)/shard_map/ppermute | solution.py:331
  62.9 2.0 %collective-permute-start.23 = (bf16[320,384]{1,0:T(8,128)(2,1)S(1)}, bf16[320,384]{1,0:T(8,128)(2,1)S(1)}, u32[]{:S(2)}, u32[]{:S(2)}) collective-permute-start(bf16[320,384]{1,0:T(8,128)(2,1)S(1)} %collective-permute-done.8.refs_1_), channel_id=1, source_target_pairs={{0,2},{1,5},{2,6},{3,1},{4,0},{5,9},{6,10},{7,3},{8,4},{9,13},{10,... | collective-permute-start | bytes 737288 | tf_op jit(solution)/shard_map/ppermute | solution.py:331
  64.8 4.4 %project.4 = (bf16[224,896]{1,0:T(8,128)(2,1)S(1)}, bf16[224,896]{1,0:T(8,128)(2,1)S(1)}) custom-call(s32[2,8,8]{2,1,0:T(8,128)S(1)} %copy-done.5, bf16[8,448,320]{2,1,0:T(8,128)(2,1)S(1)} %arrange.1.rows_ref, bf16[320,896]{1,0:T(8,128)(2,1)S(1)} %get-tuple-element.40.refs_0_, bf16[320,896]{1,0:T(8,128)(2,1)S(1)} %collective-permute-done.3.refs_1_, ...), custom_call_target="tpu_custom_call" | custom-call | flops 3082813440 | bytes 7684096 | tf_op jit(solution)/shard_map/project/pallas_call | solution.py:240
  69.2 1.6 %collective-permute-start.18 = (bf16[320,384]{1,0:T(8,128)(2,1)S(1)}, bf16[320,384]{1,0:T(8,128)(2,1)S(1)}, u32[]{:S(2)}, u32[]{:S(2)}) collective-permute-start(bf16[320,384]{1,0:T(8,128)(2,1)S(1)} %collective-permute-done.11.refs_1_), channel_id=1, source_target_pairs={{0,2},{1,5},{2,6},{3,1},{4,0},{5,9},{6,10},{7,3},{8,4},{9,13},{10,... | collective-permute-start | bytes 737288 | tf_op jit(solution)/shard_map/ppermute | solution.py:331
  72.4 4.4 %project.5 = (bf16[224,896]{1,0:T(8,128)(2,1)S(1)}, bf16[224,896]{1,0:T(8,128)(2,1)S(1)}) custom-call(s32[2,8,8]{2,1,0:T(8,128)S(1)} %copy-done.4, bf16[8,448,320]{2,1,0:T(8,128)(2,1)S(1)} %arrange.1.rows_ref, bf16[320,896]{1,0:T(8,128)(2,1)S(1)} %get-tuple-element.55.refs_0_, bf16[320,896]{1,0:T(8,128)(2,1)S(1)} %collective-permute-done.6.refs_1_, ...), custom_call_target="tpu_custom_call" | custom-call | flops 3082813440 | bytes 7684096 | tf_op jit(solution)/shard_map/project/pallas_call | solution.py:240
  77.4 1.6 %collective-permute-start.25 = (bf16[320,384]{1,0:T(8,128)(2,1)S(1)}, bf16[320,384]{1,0:T(8,128)(2,1)S(1)}, u32[]{:S(2)}, u32[]{:S(2)}) collective-permute-start(bf16[320,384]{1,0:T(8,128)(2,1)S(1)} %collective-permute-done.23.refs_2_), channel_id=1, source_target_pairs={{0,2},{1,5},{2,6},{3,1},{4,0},{5,9},{6,10},{7,3},{8,4},{9,13},{10,... | collective-permute-start | bytes 737288 | tf_op jit(solution)/shard_map/ppermute | solution.py:331
  80.6 2.5 %collective-permute-done.27.refs_1_ = bf16[224,896]{1,0:T(8,128)(2,1)S(1)} collective-permute-done((bf16[224,896]{1,0:T(8,128)(2,1)S(1)}, bf16[224,896]{1,0:T(8,128)(2,1)S(1)}, u32[]{:S(2)}, u32[]{:S(2)}) %collective-permute-start.27) | collective-permute-done | bytes 401440 | tf_op jit(solution)/shard_map/ppermute | solution.py:46
  83.6 1.6 %collective-permute-start.29 = (bf16[320,384]{1,0:T(8,128)(2,1)S(1)}, bf16[320,384]{1,0:T(8,128)(2,1)S(1)}, u32[]{:S(2)}, u32[]{:S(2)}) collective-permute-start(bf16[320,384]{1,0:T(8,128)(2,1)S(1)} %collective-permute-done.25.refs_3_), channel_id=1, source_target_pairs={{0,2},{1,5},{2,6},{3,1},{4,0},{5,9},{6,10},{7,3},{8,4},{9,13},{10,... | collective-permute-start | bytes 737288 | tf_op jit(solution)/shard_map/ppermute | solution.py:331
  86.3 3.1 %collective-permute-done.32.refs_3_ = bf16[224,896]{1,0:T(8,128)(2,1)S(1)} collective-permute-done((bf16[224,896]{1,0:T(8,128)(2,1)S(1)}, bf16[224,896]{1,0:T(8,128)(2,1)S(1)}, u32[]{:S(2)}, u32[]{:S(2)}) %collective-permute-start.32) | collective-permute-done | bytes 401440 | tf_op jit(solution)/shard_map/ppermute | solution.py:46
  90.9 2.5 %project.7 = (bf16[224,384]{1,0:T(8,128)(2,1)S(1)}, bf16[224,384]{1,0:T(8,128)(2,1)S(1)}) custom-call(s32[2,8,8]{2,1,0:T(8,128)S(1)} %copy-done.5, bf16[8,448,320]{2,1,0:T(8,128)(2,1)S(1)} %arrange.1.rows_ref, bf16[320,384]{1,0:T(8,128)(2,1)S(1)} %get-tuple-element.44.refs_0_, bf16[320,384]{1,0:T(8,128)(2,1)S(1)} %collective-permute-done.8.refs_1_, ...), custom_call_target="tpu_custom_call" | custom-call | flops 1321205760 | bytes 4603904 | tf_op jit(solution)/shard_map/project/pallas_call | solution.py:240
  95.0 2.5 %project.6 = (bf16[224,384]{1,0:T(8,128)(2,1)S(1)}, bf16[224,384]{1,0:T(8,128)(2,1)S(1)}) custom-call(s32[2,8,8]{2,1,0:T(8,128)S(1)} %copy-done.4, bf16[8,448,320]{2,1,0:T(8,128)(2,1)S(1)} %arrange.1.rows_ref, bf16[320,384]{1,0:T(8,128)(2,1)S(1)} %get-tuple-element.46.refs_0_, bf16[320,384]{1,0:T(8,128)(2,1)S(1)} %collective-permute-done.11.refs_1_, ...), custom_call_target="tpu_custom_call" | custom-call | flops 1321205760 | bytes 4603904 | tf_op jit(solution)/shard_map/project/pallas_call | solution.py:240
  98.1 1.8 %collective-permute-done.35.refs_5_ = bf16[224,384]{1,0:T(8,128)(2,1)S(1)} collective-permute-done((bf16[224,384]{1,0:T(8,128)(2,1)S(1)}, bf16[224,384]{1,0:T(8,128)(2,1)S(1)}, u32[]{:S(2)}, u32[]{:S(2)}) %collective-permute-start.35) | collective-permute-done | bytes 172064 | tf_op jit(solution)/shard_map/ppermute | solution.py:46
  101.2 2.5 %collective-permute-done.31.refs_1_ = bf16[224,384]{1,0:T(8,128)(2,1)S(1)} collective-permute-done((bf16[224,384]{1,0:T(8,128)(2,1)S(1)}, bf16[224,384]{1,0:T(8,128)(2,1)S(1)}, u32[]{:S(2)}, u32[]{:S(2)}) %collective-permute-start.31) | collective-permute-done | bytes 172064 | tf_op jit(solution)/shard_map/ppermute | solution.py:46
  (64 shorter events, 19.3 us)
Async XLA Ops:
  1.8 5.1 %collective-permute-start.1 = (bf16[2,112,1280]{2,1,0:T(8,128)(2,1)S(1)}, bf16[2,112,1280]{2,1,0:T(8,128)(2,1)S(1)}, u32[]{:S(2)}, u32[]{:S(2)}) collective-permute-start(bf16[2,112,1280]{2,1,0:T(8,128)(2,1)S(1)} %bitcast.10), channel_id=1, source_target_pairs={{0,1},{1,0},{2,3},{3,2},{4,5},{5,4},{6,7},{7,6},{8,9},{9,8},{10,11... | collective-permute-start | bytes 1720328 | tf_op jit(solution)/shard_map/ppermute | solution.py:46
  2.3 8.0 %collective-permute-start = (bf16[2,112,1280]{2,1,0:T(8,128)(2,1)S(1)}, bf16[2,112,1280]{2,1,0:T(8,128)(2,1)S(1)}, u32[]{:S(2)}, u32[]{:S(2)}) collective-permute-start(bf16[2,112,1280]{2,1,0:T(8,128)(2,1)S(1)} %bitcast.9), channel_id=1, source_target_pairs={{0,1},{1,0},{2,3},{3,2},{4,5},{5,4},{6,7},{7,6},{8,9},{9,8},{10,11... | collective-permute-start | bytes 1720328 | tf_op jit(solution)/shard_map/ppermute | solution.py:46
  2.4 11.3 %collective-permute-start.3 = (bf16[320,896]{1,0:T(8,128)(2,1)S(1)}, bf16[320,896]{1,0:T(8,128)(2,1)S(1)}, u32[]{:S(2)}, u32[]{:S(2)}) collective-permute-start(bf16[320,896]{1,0:T(8,128)(2,1)S(1)} %get-tuple-element.40.refs_0_), channel_id=1, source_target_pairs={{0,2},{1,5},{2,6},{3,1},{4,0},{5,9},{6,10},{7,3},{8,4},{9,13},{10,... | collective-permute-start | bytes 1720328 | tf_op jit(solution)/shard_map/ppermute | solution.py:331
  5.3 13.9 %collective-permute-start.6 = (bf16[320,896]{1,0:T(8,128)(2,1)S(1)}, bf16[320,896]{1,0:T(8,128)(2,1)S(1)}, u32[]{:S(2)}, u32[]{:S(2)}) collective-permute-start(bf16[320,896]{1,0:T(8,128)(2,1)S(1)} %get-tuple-element.55.refs_0_), channel_id=1, source_target_pairs={{0,2},{1,5},{2,6},{3,1},{4,0},{5,9},{6,10},{7,3},{8,4},{9,13},{10,... | collective-permute-start | bytes 1720328 | tf_op jit(solution)/shard_map/ppermute | solution.py:331
  13.7 11.7 %collective-permute-start.4 = (bf16[320,896]{1,0:T(8,128)(2,1)S(1)}, bf16[320,896]{1,0:T(8,128)(2,1)S(1)}, u32[]{:S(2)}, u32[]{:S(2)}) collective-permute-start(bf16[320,896]{1,0:T(8,128)(2,1)S(1)} %collective-permute-done.3.refs_1_), channel_id=1, source_target_pairs={{0,2},{1,5},{2,6},{3,1},{4,0},{5,9},{6,10},{7,3},{8,4},{9,13},{10,... | collective-permute-start | bytes 1720328 | tf_op jit(solution)/shard_map/ppermute | solution.py:331
  19.2 12.3 %collective-permute-start.9 = (bf16[320,896]{1,0:T(8,128)(2,1)S(1)}, bf16[320,896]{1,0:T(8,128)(2,1)S(1)}, u32[]{:S(2)}, u32[]{:S(2)}) collective-permute-start(bf16[320,896]{1,0:T(8,128)(2,1)S(1)} %collective-permute-done.6.refs_1_), channel_id=1, source_target_pairs={{0,2},{1,5},{2,6},{3,1},{4,0},{5,9},{6,10},{7,3},{8,4},{9,13},{10,... | collective-permute-start | bytes 1720328 | tf_op jit(solution)/shard_map/ppermute | solution.py:331
  21.2 10.3 %collective-permute-start.12 = (bf16[320,896]{1,0:T(8,128)(2,1)S(1)}, bf16[320,896]{1,0:T(8,128)(2,1)S(1)}, u32[]{:S(2)}, u32[]{:S(2)}) collective-permute-start(bf16[320,896]{1,0:T(8,128)(2,1)S(1)} %collective-permute-done.3.refs_1_), channel_id=1, source_target_pairs={{0,1},{1,0},{2,3},{3,2},{4,5},{5,4},{6,7},{7,6},{8,9},{9,8},{10,11... | collective-permute-start | bytes 1720328 | tf_op jit(solution)/shard_map/ppermute | solution.py:46
  21.2 27.7 %collective-permute-start.2 = (bf16[224,2560]{1,0:T(8,128)(2,1)S(1)}, bf16[224,2560]{1,0:T(8,128)(2,1)S(1)}, u32[]{:S(2)}, u32[]{:S(2)}) collective-permute-start(bf16[224,2560]{1,0:T(8,128)(2,1)S(1)} %attend.3.near_ref), channel_id=1, source_target_pairs={{0,16},{16,0},{1,17},{17,1},{2,18},{18,2},{3,19},{19,3},{4,20},{20... | collective-permute-start | bytes 3440648 | tf_op jit(solution)/shard_map/ppermute | solution.py:46
  25.4 12.3 %collective-permute-start.5 = (bf16[320,896]{1,0:T(8,128)(2,1)S(1)}, bf16[320,896]{1,0:T(8,128)(2,1)S(1)}, u32[]{:S(2)}, u32[]{:S(2)}) collective-permute-start(bf16[320,896]{1,0:T(8,128)(2,1)S(1)} %collective-permute-done.4.refs_2_), channel_id=1, source_target_pairs={{0,2},{1,5},{2,6},{3,1},{4,0},{5,9},{6,10},{7,3},{8,4},{9,13},{10,... | collective-permute-start | bytes 1720328 | tf_op jit(solution)/shard_map/ppermute | solution.py:331
  31.5 12.3 %collective-permute-start.13 = (bf16[320,896]{1,0:T(8,128)(2,1)S(1)}, bf16[320,896]{1,0:T(8,128)(2,1)S(1)}, u32[]{:S(2)}, u32[]{:S(2)}) collective-permute-start(bf16[320,896]{1,0:T(8,128)(2,1)S(1)} %collective-permute-done.9.refs_2_), channel_id=1, source_target_pairs={{0,2},{1,5},{2,6},{3,1},{4,0},{5,9},{6,10},{7,3},{8,4},{9,13},{10,... | collective-permute-start | bytes 1720328 | tf_op jit(solution)/shard_map/ppermute | solution.py:331
  33.5 10.3 %collective-permute-start.14 = (bf16[320,896]{1,0:T(8,128)(2,1)S(1)}, bf16[320,896]{1,0:T(8,128)(2,1)S(1)}, u32[]{:S(2)}, u32[]{:S(2)}) collective-permute-start(bf16[320,896]{1,0:T(8,128)(2,1)S(1)} %collective-permute-done.4.refs_2_), channel_id=1, source_target_pairs={{0,1},{1,0},{2,3},{3,2},{4,5},{5,4},{6,7},{7,6},{8,9},{9,8},{10,11... | collective-permute-start | bytes 1720328 | tf_op jit(solution)/shard_map/ppermute | solution.py:46
  33.5 12.3 %collective-permute-start.7 = (bf16[320,896]{1,0:T(8,128)(2,1)S(1)}, bf16[320,896]{1,0:T(8,128)(2,1)S(1)}, u32[]{:S(2)}, u32[]{:S(2)}) collective-permute-start(bf16[320,896]{1,0:T(8,128)(2,1)S(1)} %collective-permute-done.6.refs_1_), channel_id=1, source_target_pairs={{0,1},{1,0},{2,3},{3,2},{4,5},{5,4},{6,7},{7,6},{8,9},{9,8},{10,11... | collective-permute-start | bytes 1720328 | tf_op jit(solution)/shard_map/ppermute | solution.py:46
  43.8 12.3 %collective-permute-start.15 = (bf16[320,896]{1,0:T(8,128)(2,1)S(1)}, bf16[320,896]{1,0:T(8,128)(2,1)S(1)}, u32[]{:S(2)}, u32[]{:S(2)}) collective-permute-start(bf16[320,896]{1,0:T(8,128)(2,1)S(1)} %collective-permute-done.5.refs_3_), channel_id=1, source_target_pairs={{0,2},{1,5},{2,6},{3,1},{4,0},{5,9},{6,10},{7,3},{8,4},{9,13},{10,... | collective-permute-start | bytes 1720328 | tf_op jit(solution)/shard_map/ppermute | solution.py:331
  45.8 10.9 %collective-permute-start.10 = (bf16[320,896]{1,0:T(8,128)(2,1)S(1)}, bf16[320,896]{1,0:T(8,128)(2,1)S(1)}, u32[]{:S(2)}, u32[]{:S(2)}) collective-permute-start(bf16[320,896]{1,0:T(8,128)(2,1)S(1)} %collective-permute-done.9.refs_2_), channel_id=1, source_target_pairs={{0,1},{1,0},{2,3},{3,2},{4,5},{5,4},{6,7},{7,6},{8,9},{9,8},{10,11... | collective-permute-start | bytes 1720328 | tf_op jit(solution)/shard_map/ppermute | solution.py:46
  48.9 7.3 %collective-permute-start.8 = (bf16[320,384]{1,0:T(8,128)(2,1)S(1)}, bf16[320,384]{1,0:T(8,128)(2,1)S(1)}, u32[]{:S(2)}, u32[]{:S(2)}) collective-permute-start(bf16[320,384]{1,0:T(8,128)(2,1)S(1)} %get-tuple-element.44.refs_0_), channel_id=1, source_target_pairs={{0,2},{1,5},{2,6},{3,1},{4,0},{5,9},{6,10},{7,3},{8,4},{9,13},{10,... | collective-permute-start | bytes 737288 | tf_op jit(solution)/shard_map/ppermute | solution.py:331
  53.2 9.7 %collective-permute-start.22 = (bf16[320,896]{1,0:T(8,128)(2,1)S(1)}, bf16[320,896]{1,0:T(8,128)(2,1)S(1)}, u32[]{:S(2)}, u32[]{:S(2)}) collective-permute-start(bf16[320,896]{1,0:T(8,128)(2,1)S(1)} %collective-permute-done.5.refs_3_), channel_id=1, source_target_pairs={{0,1},{1,0},{2,3},{3,2},{4,5},{5,4},{6,7},{7,6},{8,9},{9,8},{10,11... | collective-permute-start | bytes 1720328 | tf_op jit(solution)/shard_map/ppermute | solution.py:46
  56.1 8.7 %collective-permute-start.17 = (bf16[320,896]{1,0:T(8,128)(2,1)S(1)}, bf16[320,896]{1,0:T(8,128)(2,1)S(1)}, u32[]{:S(2)}, u32[]{:S(2)}) collective-permute-start(bf16[320,896]{1,0:T(8,128)(2,1)S(1)} %collective-permute-done.13.refs_3_), channel_id=1, source_target_pairs={{0,1},{1,0},{2,3},{3,2},{4,5},{5,4},{6,7},{7,6},{8,9},{9,8},{10,11... | collective-permute-start | bytes 1720328 | tf_op jit(solution)/shard_map/ppermute | solution.py:46
  56.1 16.2 %collective-permute-start.19 = (bf16[320,896]{1,0:T(8,128)(2,1)S(1)}, bf16[320,896]{1,0:T(8,128)(2,1)S(1)}, u32[]{:S(2)}, u32[]{:S(2)}) collective-permute-start(bf16[320,896]{1,0:T(8,128)(2,1)S(1)} %collective-permute-done.15.refs_4_), channel_id=1, source_target_pairs={{0,1},{1,0},{2,3},{3,2},{4,5},{5,4},{6,7},{7,6},{8,9},{9,8},{10,11... | collective-permute-start | bytes 1720328 | tf_op jit(solution)/shard_map/ppermute | solution.py:46
  56.7 6.2 %collective-permute-start.11 = (bf16[320,384]{1,0:T(8,128)(2,1)S(1)}, bf16[320,384]{1,0:T(8,128)(2,1)S(1)}, u32[]{:S(2)}, u32[]{:S(2)}) collective-permute-start(bf16[320,384]{1,0:T(8,128)(2,1)S(1)} %get-tuple-element.46.refs_0_), channel_id=1, source_target_pairs={{0,2},{1,5},{2,6},{3,1},{4,0},{5,9},{6,10},{7,3},{8,4},{9,13},{10,... | collective-permute-start | bytes 737288 | tf_op jit(solution)/shard_map/ppermute | solution.py:331
  58.6 18.7 %collective-permute-start.21 = (bf16[320,384]{1,0:T(8,128)(2,1)S(1)}, bf16[320,384]{1,0:T(8,128)(2,1)S(1)}, u32[]{:S(2)}, u32[]{:S(2)}) collective-permute-start(bf16[320,384]{1,0:T(8,128)(2,1)S(1)} %collective-permute-done.8.refs_1_), channel_id=1, source_target_pairs={{0,1},{1,0},{2,3},{3,2},{4,5},{5,4},{6,7},{7,6},{8,9},{9,8},{10,11... | collective-permute-start | bytes 737288 | tf_op jit(solution)/shard_map/ppermute | solution.py:46
  62.9 14.5 %collective-permute-start.23 = (bf16[320,384]{1,0:T(8,128)(2,1)S(1)}, bf16[320,384]{1,0:T(8,128)(2,1)S(1)}, u32[]{:S(2)}, u32[]{:S(2)}) collective-permute-start(bf16[320,384]{1,0:T(8,128)(2,1)S(1)} %collective-permute-done.8.refs_1_), channel_id=1, source_target_pairs={{0,2},{1,5},{2,6},{3,1},{4,0},{5,9},{6,10},{7,3},{8,4},{9,13},{10,... | collective-permute-start | bytes 737288 | tf_op jit(solution)/shard_map/ppermute | solution.py:331
  69.2 9.8 %collective-permute-start.18 = (bf16[320,384]{1,0:T(8,128)(2,1)S(1)}, bf16[320,384]{1,0:T(8,128)(2,1)S(1)}, u32[]{:S(2)}, u32[]{:S(2)}) collective-permute-start(bf16[320,384]{1,0:T(8,128)(2,1)S(1)} %collective-permute-done.11.refs_1_), channel_id=1, source_target_pairs={{0,2},{1,5},{2,6},{3,1},{4,0},{5,9},{6,10},{7,3},{8,4},{9,13},{10,... | collective-permute-start | bytes 737288 | tf_op jit(solution)/shard_map/ppermute | solution.py:331
  70.9 12.2 %collective-permute-start.27 = (bf16[224,896]{1,0:T(8,128)(2,1)S(1)}, bf16[224,896]{1,0:T(8,128)(2,1)S(1)}, u32[]{:S(2)}, u32[]{:S(2)}) collective-permute-start(bf16[224,896]{1,0:T(8,128)(2,1)S(1)} %get-tuple-element.58), channel_id=1, source_target_pairs={{0,16},{16,0},{1,17},{17,1},{2,18},{18,2},{3,19},{19,3},{4,20},{20... | collective-permute-start | bytes 1204232 | tf_op jit(solution)/shard_map/ppermute | solution.py:46
  76.8 12.6 %collective-permute-start.32 = (bf16[224,896]{1,0:T(8,128)(2,1)S(1)}, bf16[224,896]{1,0:T(8,128)(2,1)S(1)}, u32[]{:S(2)}, u32[]{:S(2)}) collective-permute-start(bf16[224,896]{1,0:T(8,128)(2,1)S(1)} %get-tuple-element.63), channel_id=1, source_target_pairs={{0,16},{16,0},{1,17},{17,1},{2,18},{18,2},{3,19},{19,3},{4,20},{20... | collective-permute-start | bytes 1204232 | tf_op jit(solution)/shard_map/ppermute | solution.py:46
  77.4 6.2 %collective-permute-start.25 = (bf16[320,384]{1,0:T(8,128)(2,1)S(1)}, bf16[320,384]{1,0:T(8,128)(2,1)S(1)}, u32[]{:S(2)}, u32[]{:S(2)}) collective-permute-start(bf16[320,384]{1,0:T(8,128)(2,1)S(1)} %collective-permute-done.23.refs_2_), channel_id=1, source_target_pairs={{0,2},{1,5},{2,6},{3,1},{4,0},{5,9},{6,10},{7,3},{8,4},{9,13},{10,... | collective-permute-start | bytes 737288 | tf_op jit(solution)/shard_map/ppermute | solution.py:331
  79.0 7.2 %collective-permute-start.20 = (bf16[320,384]{1,0:T(8,128)(2,1)S(1)}, bf16[320,384]{1,0:T(8,128)(2,1)S(1)}, u32[]{:S(2)}, u32[]{:S(2)}) collective-permute-start(bf16[320,384]{1,0:T(8,128)(2,1)S(1)} %collective-permute-done.18.refs_2_), channel_id=1, source_target_pairs={{0,2},{1,5},{2,6},{3,1},{4,0},{5,9},{6,10},{7,3},{8,4},{9,13},{10,... | collective-permute-start | bytes 737288 | tf_op jit(solution)/shard_map/ppermute | solution.py:331
  83.6 6.3 %collective-permute-start.29 = (bf16[320,384]{1,0:T(8,128)(2,1)S(1)}, bf16[320,384]{1,0:T(8,128)(2,1)S(1)}, u32[]{:S(2)}, u32[]{:S(2)}) collective-permute-start(bf16[320,384]{1,0:T(8,128)(2,1)S(1)} %collective-permute-done.25.refs_3_), channel_id=1, source_target_pairs={{0,2},{1,5},{2,6},{3,1},{4,0},{5,9},{6,10},{7,3},{8,4},{9,13},{10,... | collective-permute-start | bytes 737288 | tf_op jit(solution)/shard_map/ppermute | solution.py:331
  85.2 5.2 %collective-permute-start.33 = (bf16[320,384]{1,0:T(8,128)(2,1)S(1)}, bf16[320,384]{1,0:T(8,128)(2,1)S(1)}, u32[]{:S(2)}, u32[]{:S(2)}) collective-permute-start(bf16[320,384]{1,0:T(8,128)(2,1)S(1)} %collective-permute-done.18.refs_2_), channel_id=1, source_target_pairs={{0,1},{1,0},{2,3},{3,2},{4,5},{5,4},{6,7},{7,6},{8,9},{9,8},{10,11... | collective-permute-start | bytes 737288 | tf_op jit(solution)/shard_map/ppermute | solution.py:46
  89.4 5.6 %collective-permute-start.24 = (bf16[320,384]{1,0:T(8,128)(2,1)S(1)}, bf16[320,384]{1,0:T(8,128)(2,1)S(1)}, u32[]{:S(2)}, u32[]{:S(2)}) collective-permute-start(bf16[320,384]{1,0:T(8,128)(2,1)S(1)} %collective-permute-done.23.refs_2_), channel_id=1, source_target_pairs={{0,1},{1,0},{2,3},{3,2},{4,5},{5,4},{6,7},{7,6},{8,9},{9,8},{10,11... | collective-permute-start | bytes 737288 | tf_op jit(solution)/shard_map/ppermute | solution.py:46
  89.9 5.1 %collective-permute-start.26 = (bf16[320,384]{1,0:T(8,128)(2,1)S(1)}, bf16[320,384]{1,0:T(8,128)(2,1)S(1)}, u32[]{:S(2)}, u32[]{:S(2)}) collective-permute-start(bf16[320,384]{1,0:T(8,128)(2,1)S(1)} %collective-permute-done.25.refs_3_), channel_id=1, source_target_pairs={{0,1},{1,0},{2,3},{3,2},{4,5},{5,4},{6,7},{7,6},{8,9},{9,8},{10,11... | collective-permute-start | bytes 737288 | tf_op jit(solution)/shard_map/ppermute | solution.py:46
  93.4 6.5 %collective-permute-start.35 = (bf16[224,384]{1,0:T(8,128)(2,1)S(1)}, bf16[224,384]{1,0:T(8,128)(2,1)S(1)}, u32[]{:S(2)}, u32[]{:S(2)}) collective-permute-start(bf16[224,384]{1,0:T(8,128)(2,1)S(1)} %get-tuple-element.66), channel_id=1, source_target_pairs={{0,16},{16,0},{1,17},{17,1},{2,18},{18,2},{3,19},{19,3},{4,20},{20... | collective-permute-start | bytes 516104 | tf_op jit(solution)/shard_map/ppermute | solution.py:46
  97.5 6.2 %collective-permute-start.31 = (bf16[224,384]{1,0:T(8,128)(2,1)S(1)}, bf16[224,384]{1,0:T(8,128)(2,1)S(1)}, u32[]{:S(2)}, u32[]{:S(2)}) collective-permute-start(bf16[224,384]{1,0:T(8,128)(2,1)S(1)} %get-tuple-element.62), channel_id=1, source_target_pairs={{0,16},{16,0},{1,17},{17,1},{2,18},{18,2},{3,19},{19,3},{4,20},{20... | collective-permute-start | bytes 516104 | tf_op jit(solution)/shard_map/ppermute | solution.py:46
  (10 other events, 130.5 us)
where the time goes:
time: 105 us
  waiting for transfers between devices  41.7 us (40%)
  starting transfers between devices  36 us (34%)
  Pallas kernels  26.6 us (25%)
    ppermute x14, waiting for transfers between devices, hop(): value = lax.ppermute(value, ('owner', 'slab'), ring)  26.5 us
    ppermute x14, starting transfers between devices, hop(): value = lax.ppermute(value, ('owner', 'slab'), ring)  25.9 us
    ppermute x22, waiting for transfers between devices, swap(): return lax.ppermute(value, axes, [(i, count - 1 - i) for i in range(count)])  15.1 us
    pallas_call x4, Pallas kernels, project(): pl.pallas_call(functools.partial(project_kernel, strip, column, total), o...  13.8 us
    ppermute x22, starting transfers between devices, swap(): return lax.ppermute(value, axes, [(i, count - 1 - i) for i in range(count)])  10 us
    pallas_call x2, Pallas kernels, attend(): pl.pallas_call(functools.partial(attend_kernel, spots), grid=(steps,), ou...  6.73 us
    pallas_call x2, Pallas kernels, cut(): pl.pallas_call(functools.partial(cut_kernel, first, total, with_border),...  2.85 us
  transfers between devices with their start and end apart: 36, of which 16 were waited for; matrix products, arithmetic and copies ran while one was open for 0% of the time, Pallas kernels for 23%

commit v1 on v0

--- a/solution.py
+++ b/solution.py
@@ -37,7 +37,7 @@
 
 def piece_widths(half_width):
     tiles = half_width // (2 * LANES)
-    late = 3 * tiles // 10
+    late = 2 * tiles // 5
     return [count * LANES for count in (tiles - late, late) if count]
 
 
@@ -350,7 +350,7 @@
     near_gate = scale_gate(after(keep, attended), gate)
     gates = (near_gate, swap(near_gate, ("groups",)))
     waits.setdefault(FLIGHT, []).append(attended)
-    waits.setdefault(first_done - 1, []).append(a_blocks[1])
+    waits.setdefault(first_done, []).append(a_blocks[1])
 
     arranged = arrange(*a_blocks, count)
 
@@ -375,12 +375,13 @@
     if first_done >= 2 and first_done + 1 < len(hops):
         needs[first_done - 2] = [first_done - 1, gates[1], arranged]
     for slot in range(FLIGHT, len(hops)):
-        strip = slot - first_done - 3
-        if 0 <= strip < 2:
+        strip = {first_done + 3: 0, first_done + 5: 1}.get(slot)
+        if strip is not None:
             results[0, strip] = project_strip(0, strip, *(arrived[first_done + 1 : first_done + 2] if strip else []))
             waits.setdefault(slot, []).append(results[0, strip][0])
             if strip:
                 needs[len(hops) - 2] = [results[0, strip][1]]
+                waits[slot].append(arrived[slot - 1])
             else:
                 needs[first_done + 1] = [results[0, strip][0]]
                 waits.setdefault(len(hops) - 1, []).append(results[0, strip][1])

time: 105 us -> 96.1 us (0.915)
  starting transfers between devices: 36 us -> 29.4 us
  Pallas kernels: 26.6 us -> 25.5 us
    ppermute x14, starting transfers between devices: 25.9 us -> 19.1 us  [hop(): value = lax.ppermute(value, ('owner', 'slab'), ring)]
    ppermute x14, waiting for transfers between devices: 26.5 us -> 21.5 us  [hop(): value = lax.ppermute(value, ('owner', 'slab'), ring)]
    ppermute x22, waiting for transfers between devices: 15.1 us -> 19.3 us  [swap(): return lax.ppermute(value, axes, [(i, count - 1 - i) for i in range(count)])]
  transfers between devices with their start and end apart: 36 -> 36, of which waited for: 16 -> 17; matrix products, arithmetic and copies ran while one was open for 0% -> 0% of each run, Pallas kernels for 23% -> 24%
where the time goes in v1:
time: 96.1 us; the launch traced here: 95.9 us
  waiting for transfers between devices  40.9 us (43%)
  starting transfers between devices  29.4 us (31%)
  Pallas kernels  25.5 us (27%)
    ppermute x14, waiting for transfers between devices, hop(): value = lax.ppermute(value, ('owner', 'slab'), ring)  21.5 us
    ppermute x22, waiting for transfers between devices, swap(): return lax.ppermute(value, axes, [(i, count - 1 - i) for i in range(count)])  19.3 us
    ppermute x14, starting transfers between devices, hop(): value = lax.ppermute(value, ('owner', 'slab'), ring)  19.1 us
    pallas_call x4, Pallas kernels, project(): pl.pallas_call(functools.partial(project_kernel, strip, column, total), o...  12.8 us
    ppermute x22, starting transfers between devices, swap(): return lax.ppermute(value, axes, [(i, count - 1 - i) for i in range(count)])  10.3 us
    pallas_call x2, Pallas kernels, attend(): pl.pallas_call(functools.partial(attend_kernel, spots), grid=(steps,), ou...  6.73 us
    pallas_call x2, Pallas kernels, cut(): pl.pallas_call(functools.partial(cut_kernel, first, total, with_border),...  2.81 us
    pallas_call x2, Pallas kernels, place(): pl.pallas_call(functools.partial(place_kernel, len(blocks), columns, tota...  2.05 us
  transfers between devices with their start and end apart: 36, of which 17 were waited for; matrix products, arithmetic and copies ran while one was open for 0% of the time, Pallas kernels for 24%

profile of v1, /device:TPU:0, one launch (start us, length us, event | category | flops | bytes accessed | tf_op | source)
XLA Modules:
  0.0 95.9 jit_solution(12497991300220393855)
XLA Ops:
  0.0 1.7 %cut.2 = (bf16[320,768]{1,0:T(8,128)(2,1)S(1)}, bf16[320,768]{1,0:T(8,128)(2,1)S(1)}, bf16[2,1,112,1280]{3,2,1,0:T(8,128)(2,1)S(1)}, bf16[2,1,112,1280]{3,2,1,0:T(8,128)(2,1)S(1)}) custom-call(bf16[320,5120]{1,0:T(8,128)(2,1)} %weight_ref.3, bf16[2,1,2,112,2560]{4,3,2,1,0:T(8,128)(2,1)} %key_value_ref.3), custom_call_target="tpu_custom_call" | custom-call | bytes 1966080 | tf_op jit(solution)/shard_map/cut/pallas_call | solution.py:84
  2.3 2.9 %collective-permute-start.3 = (bf16[320,768]{1,0:T(8,128)(2,1)S(1)}, bf16[320,768]{1,0:T(8,128)(2,1)S(1)}, u32[]{:S(2)}, u32[]{:S(2)}) collective-permute-start(bf16[320,768]{1,0:T(8,128)(2,1)S(1)} %get-tuple-element.40.refs_0_), channel_id=1, source_target_pairs={{0,2},{1,5},{2,6},{3,1},{4,0},{5,9},{6,10},{7,3},{8,4},{9,13},{10,... | collective-permute-start | bytes 1474568 | tf_op jit(solution)/shard_map/ppermute | solution.py:331
  5.3 1.6 %collective-permute-start.6 = (bf16[320,768]{1,0:T(8,128)(2,1)S(1)}, bf16[320,768]{1,0:T(8,128)(2,1)S(1)}, u32[]{:S(2)}, u32[]{:S(2)}) collective-permute-start(bf16[320,768]{1,0:T(8,128)(2,1)S(1)} %get-tuple-element.53.refs_0_), channel_id=1, source_target_pairs={{0,2},{1,5},{2,6},{3,1},{4,0},{5,9},{6,10},{7,3},{8,4},{9,13},{10,... | collective-permute-start | bytes 1474568 | tf_op jit(solution)/shard_map/ppermute | solution.py:331
  6.9 3.4 %attend.2.refs_0_ = bf16[224,2560]{1,0:T(8,128)(2,1)S(1)} custom-call(s32[4,3]{1,0:T(4,128)S(1)} %copy-done.3, bf16[224,2560]{1,0:T(8,128)(2,1)} %bitcast.11, bf16[2,224,2560]{2,1,0:T(8,128)(2,1)S(1)} %bitcast.5, bf16[2,224,2560]{2,1,0:T(8,128)(2,1)S(1)} %bitcast.6, bf16[2,112,1280]{2,1,0:T(8,128)(2,1)S(1)} %collective-permute-done.1.k_halo_ref.v_halo_ref, ...), custom_call_target="tpu_custom_call" | custom-call | flops 3523215360 | bytes 3112960 | tf_op jit(solution)/shard_map/attend/pallas_call | solution.py:171
  10.2 3.4 %attend.3.near_ref = bf16[224,2560]{1,0:T(8,128)(2,1)S(1)} custom-call(s32[4,3]{1,0:T(4,128)S(1)} %copy-done.3, bf16[224,2560]{1,0:T(8,128)(2,1)} %bitcast.12, bf16[2,224,2560]{2,1,0:T(8,128)(2,1)S(1)} %bitcast.7, bf16[2,224,2560]{2,1,0:T(8,128)(2,1)S(1)} %bitcast.8, ...), custom_call_target="tpu_custom_call", output_to_operand_aliasing={{}: (6, {})} | custom-call | flops 3523215360 | bytes 3112960 | tf_op jit(solution)/shard_map/attend/pallas_call | solution.py:171
  13.6 1.6 %collective-permute-start.2 = (bf16[224,2560]{1,0:T(8,128)(2,1)S(1)}, bf16[224,2560]{1,0:T(8,128)(2,1)S(1)}, u32[]{:S(2)}, u32[]{:S(2)}) collective-permute-start(bf16[224,2560]{1,0:T(8,128)(2,1)S(1)} %attend.3.near_ref), channel_id=1, source_target_pairs={{0,16},{16,0},{1,17},{17,1},{2,18},{18,2},{3,19},{19,3},{4,20},{20... | collective-permute-start | bytes 3440648 | tf_op jit(solution)/shard_map/ppermute | solution.py:46
  15.2 1.6 %collective-permute-start.4 = (bf16[320,768]{1,0:T(8,128)(2,1)S(1)}, bf16[320,768]{1,0:T(8,128)(2,1)S(1)}, u32[]{:S(2)}, u32[]{:S(2)}) collective-permute-start(bf16[320,768]{1,0:T(8,128)(2,1)S(1)} %collective-permute-done.3.refs_1_), channel_id=1, source_target_pairs={{0,2},{1,5},{2,6},{3,1},{4,0},{5,9},{6,10},{7,3},{8,4},{9,13},{10,... | collective-permute-start | bytes 1474568 | tf_op jit(solution)/shard_map/ppermute | solution.py:331
  17.4 2.0 %collective-permute-start.9 = (bf16[320,768]{1,0:T(8,128)(2,1)S(1)}, bf16[320,768]{1,0:T(8,128)(2,1)S(1)}, u32[]{:S(2)}, u32[]{:S(2)}) collective-permute-start(bf16[320,768]{1,0:T(8,128)(2,1)S(1)} %collective-permute-done.6.refs_1_), channel_id=1, source_target_pairs={{0,2},{1,5},{2,6},{3,1},{4,0},{5,9},{6,10},{7,3},{8,4},{9,13},{10,... | collective-permute-start | bytes 1474568 | tf_op jit(solution)/shard_map/ppermute | solution.py:331
  19.4 1.1 %cut.3 = (bf16[320,512]{1,0:T(8,128)(2,1)S(1)}, bf16[320,512]{1,0:T(8,128)(2,1)S(1)}) custom-call(bf16[320,5120]{1,0:T(8,128)(2,1)} %weight_ref.3, bf16[2,1,2,112,2560]{4,3,2,1,0:T(8,128)(2,1)} %key_value_ref.3), custom_call_target="tpu_custom_call" | custom-call | bytes 1310720 | tf_op jit(solution)/shard_map/cut/pallas_call | solution.py:84
  21.0 3.0 %collective-permute-done.4.refs_2_ = bf16[320,768]{1,0:T(8,128)(2,1)S(1)} collective-permute-done((bf16[320,768]{1,0:T(8,128)(2,1)S(1)}, bf16[320,768]{1,0:T(8,128)(2,1)S(1)}, u32[]{:S(2)}, u32[]{:S(2)}) %collective-permute-start.4) | collective-permute-done | bytes 491552 | tf_op jit(solution)/shard_map/ppermute | solution.py:331
  24.0 1.6 %collective-permute-start.5 = (bf16[320,768]{1,0:T(8,128)(2,1)S(1)}, bf16[320,768]{1,0:T(8,128)(2,1)S(1)}, u32[]{:S(2)}, u32[]{:S(2)}) collective-permute-start(bf16[320,768]{1,0:T(8,128)(2,1)S(1)} %collective-permute-done.4.refs_2_), channel_id=1, source_target_pairs={{0,2},{1,5},{2,6},{3,1},{4,0},{5,9},{6,10},{7,3},{8,4},{9,13},{10,... | collective-permute-start | bytes 1474568 | tf_op jit(solution)/shard_map/ppermute | solution.py:331
  25.6 3.7 %collective-permute-done.9.refs_2_ = bf16[320,768]{1,0:T(8,128)(2,1)S(1)} collective-permute-done((bf16[320,768]{1,0:T(8,128)(2,1)S(1)}, bf16[320,768]{1,0:T(8,128)(2,1)S(1)}, u32[]{:S(2)}, u32[]{:S(2)}) %collective-permute-start.9) | collective-permute-done | bytes 491552 | tf_op jit(solution)/shard_map/ppermute | solution.py:331
  29.3 1.6 %collective-permute-start.13 = (bf16[320,768]{1,0:T(8,128)(2,1)S(1)}, bf16[320,768]{1,0:T(8,128)(2,1)S(1)}, u32[]{:S(2)}, u32[]{:S(2)}) collective-permute-start(bf16[320,768]{1,0:T(8,128)(2,1)S(1)} %collective-permute-done.9.refs_2_), channel_id=1, source_target_pairs={{0,2},{1,5},{2,6},{3,1},{4,0},{5,9},{6,10},{7,3},{8,4},{9,13},{10,... | collective-permute-start | bytes 1474568 | tf_op jit(solution)/shard_map/ppermute | solution.py:331
  30.9 3.7 %collective-permute-done.5.refs_3_ = bf16[320,768]{1,0:T(8,128)(2,1)S(1)} collective-permute-done((bf16[320,768]{1,0:T(8,128)(2,1)S(1)}, bf16[320,768]{1,0:T(8,128)(2,1)S(1)}, u32[]{:S(2)}, u32[]{:S(2)}) %collective-permute-start.5) | collective-permute-done | bytes 491552 | tf_op jit(solution)/shard_map/ppermute | solution.py:331
  34.6 1.6 %collective-permute-start.8 = (bf16[320,512]{1,0:T(8,128)(2,1)S(1)}, bf16[320,512]{1,0:T(8,128)(2,1)S(1)}, u32[]{:S(2)}, u32[]{:S(2)}) collective-permute-start(bf16[320,512]{1,0:T(8,128)(2,1)S(1)} %get-tuple-element.44.refs_0_), channel_id=1, source_target_pairs={{0,2},{1,5},{2,6},{3,1},{4,0},{5,9},{6,10},{7,3},{8,4},{9,13},{10,... | collective-permute-start | bytes 983048 | tf_op jit(solution)/shard_map/ppermute | solution.py:331
  36.1 3.7 %collective-permute-done.13.refs_3_ = bf16[320,768]{1,0:T(8,128)(2,1)S(1)} collective-permute-done((bf16[320,768]{1,0:T(8,128)(2,1)S(1)}, bf16[320,768]{1,0:T(8,128)(2,1)S(1)}, u32[]{:S(2)}, u32[]{:S(2)}) %collective-permute-start.13) | collective-permute-done | bytes 491552 | tf_op jit(solution)/shard_map/ppermute | solution.py:331
  42.5 1.2 %collective-permute-start.16 = (f32[1,5120]{1,0:T(1,128)S(1)}, f32[1,5120]{1,0:T(1,128)S(1)}, u32[]{:S(2)}, u32[]{:S(2)}) collective-permute-start(f32[1,5120]{1,0:T(1,128)S(1)} %scale_gate.1.refs_8_), channel_id=1, source_target_pairs={{0,16},{16,0},{1,17},{17,1},{2,18},{18,2},{3,19},{19,3},{4,20},{20... | collective-permute-start | bytes 61448 | tf_op jit(solution)/shard_map/ppermute | solution.py:46
  44.4 2.0 %collective-permute-done.16.refs_9_ = f32[1,5120]{1,0:T(1,128)S(1)} collective-permute-done((f32[1,5120]{1,0:T(1,128)S(1)}, f32[1,5120]{1,0:T(1,128)S(1)}, u32[]{:S(2)}, u32[]{:S(2)}) %collective-permute-start.16) | collective-permute-done | bytes 20512 | tf_op jit(solution)/shard_map/ppermute | solution.py:46
  46.4 2.9 %collective-permute-done.15.refs_4_ = bf16[320,768]{1,0:T(8,128)(2,1)S(1)} collective-permute-done((bf16[320,768]{1,0:T(8,128)(2,1)S(1)}, bf16[320,768]{1,0:T(8,128)(2,1)S(1)}, u32[]{:S(2)}, u32[]{:S(2)}) %collective-permute-start.15) | collective-permute-done | bytes 491552 | tf_op jit(solution)/shard_map/ppermute | solution.py:331
  49.3 1.0 %collective-permute-start.11 = (bf16[320,512]{1,0:T(8,128)(2,1)S(1)}, bf16[320,512]{1,0:T(8,128)(2,1)S(1)}, u32[]{:S(2)}, u32[]{:S(2)}) collective-permute-start(bf16[320,512]{1,0:T(8,128)(2,1)S(1)} %get-tuple-element.46.refs_0_), channel_id=1, source_target_pairs={{0,2},{1,5},{2,6},{3,1},{4,0},{5,9},{6,10},{7,3},{8,4},{9,13},{10,... | collective-permute-start | bytes 983048 | tf_op jit(solution)/shard_map/ppermute | solution.py:331
  51.9 3.7 %project.4 = (bf16[224,768]{1,0:T(8,128)(2,1)S(1)}, bf16[224,768]{1,0:T(8,128)(2,1)S(1)}) custom-call(s32[2,8,8]{2,1,0:T(8,128)S(1)} %copy-done.5, bf16[8,448,320]{2,1,0:T(8,128)(2,1)S(1)} %arrange.1.rows_ref, bf16[320,768]{1,0:T(8,128)(2,1)S(1)} %get-tuple-element.40.refs_0_, bf16[320,768]{1,0:T(8,128)(2,1)S(1)} %collective-permute-done.3.refs_1_, ...), custom_call_target="tpu_custom_call" | custom-call | flops 2642411520 | bytes 6914048 | tf_op jit(solution)/shard_map/project/pallas_call | solution.py:240
  57.4 2.5 %collective-permute-done.21.refs_2_ = bf16[320,512]{1,0:T(8,128)(2,1)S(1)} collective-permute-done((bf16[320,512]{1,0:T(8,128)(2,1)S(1)}, bf16[320,512]{1,0:T(8,128)(2,1)S(1)}, u32[]{:S(2)}, u32[]{:S(2)}) %collective-permute-start.21) | collective-permute-done | bytes 327712 | tf_op jit(solution)/shard_map/ppermute | solution.py:331
  62.0 3.7 %project.5 = (bf16[224,768]{1,0:T(8,128)(2,1)S(1)}, bf16[224,768]{1,0:T(8,128)(2,1)S(1)}) custom-call(s32[2,8,8]{2,1,0:T(8,128)S(1)} %copy-done.4, bf16[8,448,320]{2,1,0:T(8,128)(2,1)S(1)} %arrange.1.rows_ref, bf16[320,768]{1,0:T(8,128)(2,1)S(1)} %get-tuple-element.53.refs_0_, bf16[320,768]{1,0:T(8,128)(2,1)S(1)} %collective-permute-done.6.refs_1_, ...), custom_call_target="tpu_custom_call" | custom-call | flops 2642411520 | bytes 6914048 | tf_op jit(solution)/shard_map/project/pallas_call | solution.py:240
  67.0 1.2 %collective-permute-start.24 = (bf16[320,512]{1,0:T(8,128)(2,1)S(1)}, bf16[320,512]{1,0:T(8,128)(2,1)S(1)}, u32[]{:S(2)}, u32[]{:S(2)}) collective-permute-start(bf16[320,512]{1,0:T(8,128)(2,1)S(1)} %collective-permute-done.18.refs_2_), channel_id=1, source_target_pairs={{0,2},{1,5},{2,6},{3,1},{4,0},{5,9},{6,10},{7,3},{8,4},{9,13},{10,... | collective-permute-start | bytes 983048 | tf_op jit(solution)/shard_map/ppermute | solution.py:331
  68.3 3.6 %collective-permute-done.27.refs_1_ = bf16[224,768]{1,0:T(8,128)(2,1)S(1)} collective-permute-done((bf16[224,768]{1,0:T(8,128)(2,1)S(1)}, bf16[224,768]{1,0:T(8,128)(2,1)S(1)}, u32[]{:S(2)}, u32[]{:S(2)}) %collective-permute-start.27) | collective-permute-done | bytes 344096 | tf_op jit(solution)/shard_map/ppermute | solution.py:46
  72.2 6.0 %collective-permute-done.32.refs_3_ = bf16[224,768]{1,0:T(8,128)(2,1)S(1)} collective-permute-done((bf16[224,768]{1,0:T(8,128)(2,1)S(1)}, bf16[224,768]{1,0:T(8,128)(2,1)S(1)}, u32[]{:S(2)}, u32[]{:S(2)}) %collective-permute-start.32) | collective-permute-done | bytes 344096 | tf_op jit(solution)/shard_map/ppermute | solution.py:46
  79.8 2.7 %project.7 = (bf16[224,512]{1,0:T(8,128)(2,1)S(1)}, bf16[224,512]{1,0:T(8,128)(2,1)S(1)}) custom-call(s32[2,8,8]{2,1,0:T(8,128)S(1)} %copy-done.5, bf16[8,448,320]{2,1,0:T(8,128)(2,1)S(1)} %arrange.1.rows_ref, bf16[320,512]{1,0:T(8,128)(2,1)S(1)} %get-tuple-element.44.refs_0_, bf16[320,512]{1,0:T(8,128)(2,1)S(1)} %collective-permute-done.8.refs_1_, ...), custom_call_target="tpu_custom_call" | custom-call | flops 1761607680 | bytes 5373952 | tf_op jit(solution)/shard_map/project/pallas_call | solution.py:240
  82.5 1.6 %collective-permute-start.35 = (bf16[224,512]{1,0:T(8,128)(2,1)S(1)}, bf16[224,512]{1,0:T(8,128)(2,1)S(1)}, u32[]{:S(2)}, u32[]{:S(2)}) collective-permute-start(bf16[224,512]{1,0:T(8,128)(2,1)S(1)} %get-tuple-element.66), channel_id=1, source_target_pairs={{0,16},{16,0},{1,17},{17,1},{2,18},{18,2},{3,19},{19,3},{4,20},{20... | collective-permute-start | bytes 688136 | tf_op jit(solution)/shard_map/ppermute | solution.py:46
  84.1 2.7 %project.6 = (bf16[224,512]{1,0:T(8,128)(2,1)S(1)}, bf16[224,512]{1,0:T(8,128)(2,1)S(1)}) custom-call(s32[2,8,8]{2,1,0:T(8,128)S(1)} %copy-done.4, bf16[8,448,320]{2,1,0:T(8,128)(2,1)S(1)} %arrange.1.rows_ref, bf16[320,512]{1,0:T(8,128)(2,1)S(1)} %get-tuple-element.46.refs_0_, bf16[320,512]{1,0:T(8,128)(2,1)S(1)} %collective-permute-done.11.refs_1_, ...), custom_call_target="tpu_custom_call" | custom-call | flops 1761607680 | bytes 5373952 | tf_op jit(solution)/shard_map/project/pallas_call | solution.py:240
  87.4 3.6 %collective-permute-done.35.refs_5_ = bf16[224,512]{1,0:T(8,128)(2,1)S(1)} collective-permute-done((bf16[224,512]{1,0:T(8,128)(2,1)S(1)}, bf16[224,512]{1,0:T(8,128)(2,1)S(1)}, u32[]{:S(2)}, u32[]{:S(2)}) %collective-permute-start.35) | collective-permute-done | bytes 229408 | tf_op jit(solution)/shard_map/ppermute | solution.py:46
  91.0 1.3 %place.2.refs_2_ = bf16[224,5120]{1,0:T(8,128)(2,1)} custom-call(bf16[224,768]{1,0:T(8,128)(2,1)S(1)} %get-tuple-element.51.refs_0_, bf16[224,768]{1,0:T(8,128)(2,1)S(1)} %collective-permute-done.27.refs_1_, bf16[224,768]{1,0:T(8,128)(2,1)S(1)} %get-tuple-element.54.refs_2_, bf16[224,768]{1,0:T(8,128)(2,1)S(1)} %collective-permute-done.32.refs_3_, ...), custom_call_target="tpu_custom_call" | custom-call | bytes 3670016 | tf_op jit(solution)/shard_map/place/pallas_call | solution.py:271
  92.3 2.8 %collective-permute-done.31.refs_1_ = bf16[224,512]{1,0:T(8,128)(2,1)S(1)} collective-permute-done((bf16[224,512]{1,0:T(8,128)(2,1)S(1)}, bf16[224,512]{1,0:T(8,128)(2,1)S(1)}, u32[]{:S(2)}, u32[]{:S(2)}) %collective-permute-start.31) | collective-permute-done | bytes 229408 | tf_op jit(solution)/shard_map/ppermute | solution.py:46
  (64 shorter events, 15.2 us)
Async XLA Ops:
  2.3 8.0 %collective-permute-start = (bf16[2,112,1280]{2,1,0:T(8,128)(2,1)S(1)}, bf16[2,112,1280]{2,1,0:T(8,128)(2,1)S(1)}, u32[]{:S(2)}, u32[]{:S(2)}) collective-permute-start(bf16[2,112,1280]{2,1,0:T(8,128)(2,1)S(1)} %bitcast.9), channel_id=1, source_target_pairs={{0,1},{1,0},{2,3},{3,2},{4,5},{5,4},{6,7},{7,6},{8,9},{9,8},{10,11... | collective-permute-start | bytes 1720328 | tf_op jit(solution)/shard_map/ppermute | solution.py:46
  2.3 12.9 %collective-permute-start.3 = (bf16[320,768]{1,0:T(8,128)(2,1)S(1)}, bf16[320,768]{1,0:T(8,128)(2,1)S(1)}, u32[]{:S(2)}, u32[]{:S(2)}) collective-permute-start(bf16[320,768]{1,0:T(8,128)(2,1)S(1)} %get-tuple-element.40.refs_0_), channel_id=1, source_target_pairs={{0,2},{1,5},{2,6},{3,1},{4,0},{5,9},{6,10},{7,3},{8,4},{9,13},{10,... | collective-permute-start | bytes 1474568 | tf_op jit(solution)/shard_map/ppermute | solution.py:331
  5.3 12.1 %collective-permute-start.6 = (bf16[320,768]{1,0:T(8,128)(2,1)S(1)}, bf16[320,768]{1,0:T(8,128)(2,1)S(1)}, u32[]{:S(2)}, u32[]{:S(2)}) collective-permute-start(bf16[320,768]{1,0:T(8,128)(2,1)S(1)} %get-tuple-element.53.refs_0_), channel_id=1, source_target_pairs={{0,2},{1,5},{2,6},{3,1},{4,0},{5,9},{6,10},{7,3},{8,4},{9,13},{10,... | collective-permute-start | bytes 1474568 | tf_op jit(solution)/shard_map/ppermute | solution.py:331
  13.6 26.8 %collective-permute-start.2 = (bf16[224,2560]{1,0:T(8,128)(2,1)S(1)}, bf16[224,2560]{1,0:T(8,128)(2,1)S(1)}, u32[]{:S(2)}, u32[]{:S(2)}) collective-permute-start(bf16[224,2560]{1,0:T(8,128)(2,1)S(1)} %attend.3.near_ref), channel_id=1, source_target_pairs={{0,16},{16,0},{1,17},{17,1},{2,18},{18,2},{3,19},{19,3},{4,20},{20... | collective-permute-start | bytes 3440648 | tf_op jit(solution)/shard_map/ppermute | solution.py:46
  15.2 8.8 %collective-permute-start.4 = (bf16[320,768]{1,0:T(8,128)(2,1)S(1)}, bf16[320,768]{1,0:T(8,128)(2,1)S(1)}, u32[]{:S(2)}, u32[]{:S(2)}) collective-permute-start(bf16[320,768]{1,0:T(8,128)(2,1)S(1)} %collective-permute-done.3.refs_1_), channel_id=1, source_target_pairs={{0,2},{1,5},{2,6},{3,1},{4,0},{5,9},{6,10},{7,3},{8,4},{9,13},{10,... | collective-permute-start | bytes 1474568 | tf_op jit(solution)/shard_map/ppermute | solution.py:331
  17.4 11.9 %collective-permute-start.9 = (bf16[320,768]{1,0:T(8,128)(2,1)S(1)}, bf16[320,768]{1,0:T(8,128)(2,1)S(1)}, u32[]{:S(2)}, u32[]{:S(2)}) collective-permute-start(bf16[320,768]{1,0:T(8,128)(2,1)S(1)} %collective-permute-done.6.refs_1_), channel_id=1, source_target_pairs={{0,2},{1,5},{2,6},{3,1},{4,0},{5,9},{6,10},{7,3},{8,4},{9,13},{10,... | collective-permute-start | bytes 1474568 | tf_op jit(solution)/shard_map/ppermute | solution.py:331
  19.4 9.9 %collective-permute-start.12 = (bf16[320,768]{1,0:T(8,128)(2,1)S(1)}, bf16[320,768]{1,0:T(8,128)(2,1)S(1)}, u32[]{:S(2)}, u32[]{:S(2)}) collective-permute-start(bf16[320,768]{1,0:T(8,128)(2,1)S(1)} %collective-permute-done.3.refs_1_), channel_id=1, source_target_pairs={{0,1},{1,0},{2,3},{3,2},{4,5},{5,4},{6,7},{7,6},{8,9},{9,8},{10,11... | collective-permute-start | bytes 1474568 | tf_op jit(solution)/shard_map/ppermute | solution.py:46
  20.5 10.4 %collective-permute-start.7 = (bf16[320,768]{1,0:T(8,128)(2,1)S(1)}, bf16[320,768]{1,0:T(8,128)(2,1)S(1)}, u32[]{:S(2)}, u32[]{:S(2)}) collective-permute-start(bf16[320,768]{1,0:T(8,128)(2,1)S(1)} %collective-permute-done.6.refs_1_), channel_id=1, source_target_pairs={{0,1},{1,0},{2,3},{3,2},{4,5},{5,4},{6,7},{7,6},{8,9},{9,8},{10,11... | collective-permute-start | bytes 1474568 | tf_op jit(solution)/shard_map/ppermute | solution.py:46
  24.0 10.5 %collective-permute-start.5 = (bf16[320,768]{1,0:T(8,128)(2,1)S(1)}, bf16[320,768]{1,0:T(8,128)(2,1)S(1)}, u32[]{:S(2)}, u32[]{:S(2)}) collective-permute-start(bf16[320,768]{1,0:T(8,128)(2,1)S(1)} %collective-permute-done.4.refs_2_), channel_id=1, source_target_pairs={{0,2},{1,5},{2,6},{3,1},{4,0},{5,9},{6,10},{7,3},{8,4},{9,13},{10,... | collective-permute-start | bytes 1474568 | tf_op jit(solution)/shard_map/ppermute | solution.py:331
  29.3 10.5 %collective-permute-start.13 = (bf16[320,768]{1,0:T(8,128)(2,1)S(1)}, bf16[320,768]{1,0:T(8,128)(2,1)S(1)}, u32[]{:S(2)}, u32[]{:S(2)}) collective-permute-start(bf16[320,768]{1,0:T(8,128)(2,1)S(1)} %collective-permute-done.9.refs_2_), channel_id=1, source_target_pairs={{0,2},{1,5},{2,6},{3,1},{4,0},{5,9},{6,10},{7,3},{8,4},{9,13},{10,... | collective-permute-start | bytes 1474568 | tf_op jit(solution)/shard_map/ppermute | solution.py:331
  30.9 9.0 %collective-permute-start.14 = (bf16[320,768]{1,0:T(8,128)(2,1)S(1)}, bf16[320,768]{1,0:T(8,128)(2,1)S(1)}, u32[]{:S(2)}, u32[]{:S(2)}) collective-permute-start(bf16[320,768]{1,0:T(8,128)(2,1)S(1)} %collective-permute-done.4.refs_2_), channel_id=1, source_target_pairs={{0,1},{1,0},{2,3},{3,2},{4,5},{5,4},{6,7},{7,6},{8,9},{9,8},{10,11... | collective-permute-start | bytes 1474568 | tf_op jit(solution)/shard_map/ppermute | solution.py:46
  34.6 11.8 %collective-permute-start.8 = (bf16[320,512]{1,0:T(8,128)(2,1)S(1)}, bf16[320,512]{1,0:T(8,128)(2,1)S(1)}, u32[]{:S(2)}, u32[]{:S(2)}) collective-permute-start(bf16[320,512]{1,0:T(8,128)(2,1)S(1)} %get-tuple-element.44.refs_0_), channel_id=1, source_target_pairs={{0,2},{1,5},{2,6},{3,1},{4,0},{5,9},{6,10},{7,3},{8,4},{9,13},{10,... | collective-permute-start | bytes 983048 | tf_op jit(solution)/shard_map/ppermute | solution.py:331
  40.5 8.8 %collective-permute-start.15 = (bf16[320,768]{1,0:T(8,128)(2,1)S(1)}, bf16[320,768]{1,0:T(8,128)(2,1)S(1)}, u32[]{:S(2)}, u32[]{:S(2)}) collective-permute-start(bf16[320,768]{1,0:T(8,128)(2,1)S(1)} %collective-permute-done.5.refs_3_), channel_id=1, source_target_pairs={{0,2},{1,5},{2,6},{3,1},{4,0},{5,9},{6,10},{7,3},{8,4},{9,13},{10,... | collective-permute-start | bytes 1474568 | tf_op jit(solution)/shard_map/ppermute | solution.py:331
  41.4 7.9 %collective-permute-start.10 = (bf16[320,768]{1,0:T(8,128)(2,1)S(1)}, bf16[320,768]{1,0:T(8,128)(2,1)S(1)}, u32[]{:S(2)}, u32[]{:S(2)}) collective-permute-start(bf16[320,768]{1,0:T(8,128)(2,1)S(1)} %collective-permute-done.9.refs_2_), channel_id=1, source_target_pairs={{0,1},{1,0},{2,3},{3,2},{4,5},{5,4},{6,7},{7,6},{8,9},{9,8},{10,11... | collective-permute-start | bytes 1474568 | tf_op jit(solution)/shard_map/ppermute | solution.py:46
  41.6 9.5 %collective-permute-start.19 = (bf16[320,768]{1,0:T(8,128)(2,1)S(1)}, bf16[320,768]{1,0:T(8,128)(2,1)S(1)}, u32[]{:S(2)}, u32[]{:S(2)}) collective-permute-start(bf16[320,768]{1,0:T(8,128)(2,1)S(1)} %collective-permute-done.5.refs_3_), channel_id=1, source_target_pairs={{0,1},{1,0},{2,3},{3,2},{4,5},{5,4},{6,7},{7,6},{8,9},{9,8},{10,11... | collective-permute-start | bytes 1474568 | tf_op jit(solution)/shard_map/ppermute | solution.py:46
  46.4 5.5 %collective-permute-start.17 = (bf16[320,768]{1,0:T(8,128)(2,1)S(1)}, bf16[320,768]{1,0:T(8,128)(2,1)S(1)}, u32[]{:S(2)}, u32[]{:S(2)}) collective-permute-start(bf16[320,768]{1,0:T(8,128)(2,1)S(1)} %collective-permute-done.13.refs_3_), channel_id=1, source_target_pairs={{0,1},{1,0},{2,3},{3,2},{4,5},{5,4},{6,7},{7,6},{8,9},{9,8},{10,11... | collective-permute-start | bytes 1474568 | tf_op jit(solution)/shard_map/ppermute | solution.py:46
  49.3 12.8 %collective-permute-start.20 = (bf16[320,768]{1,0:T(8,128)(2,1)S(1)}, bf16[320,768]{1,0:T(8,128)(2,1)S(1)}, u32[]{:S(2)}, u32[]{:S(2)}) collective-permute-start(bf16[320,768]{1,0:T(8,128)(2,1)S(1)} %collective-permute-done.15.refs_4_), channel_id=1, source_target_pairs={{0,1},{1,0},{2,3},{3,2},{4,5},{5,4},{6,7},{7,6},{8,9},{9,8},{10,11... | collective-permute-start | bytes 1474568 | tf_op jit(solution)/shard_map/ppermute | solution.py:46
  49.3 7.1 %collective-permute-start.11 = (bf16[320,512]{1,0:T(8,128)(2,1)S(1)}, bf16[320,512]{1,0:T(8,128)(2,1)S(1)}, u32[]{:S(2)}, u32[]{:S(2)}) collective-permute-start(bf16[320,512]{1,0:T(8,128)(2,1)S(1)} %get-tuple-element.46.refs_0_), channel_id=1, source_target_pairs={{0,2},{1,5},{2,6},{3,1},{4,0},{5,9},{6,10},{7,3},{8,4},{9,13},{10,... | collective-permute-start | bytes 983048 | tf_op jit(solution)/shard_map/ppermute | solution.py:331
  50.3 7.1 %collective-permute-start.22 = (bf16[320,512]{1,0:T(8,128)(2,1)S(1)}, bf16[320,512]{1,0:T(8,128)(2,1)S(1)}, u32[]{:S(2)}, u32[]{:S(2)}) collective-permute-start(bf16[320,512]{1,0:T(8,128)(2,1)S(1)} %collective-permute-done.8.refs_1_), channel_id=1, source_target_pairs={{0,1},{1,0},{2,3},{3,2},{4,5},{5,4},{6,7},{7,6},{8,9},{9,8},{10,11... | collective-permute-start | bytes 983048 | tf_op jit(solution)/shard_map/ppermute | solution.py:46
  51.1 8.8 %collective-permute-start.21 = (bf16[320,512]{1,0:T(8,128)(2,1)S(1)}, bf16[320,512]{1,0:T(8,128)(2,1)S(1)}, u32[]{:S(2)}, u32[]{:S(2)}) collective-permute-start(bf16[320,512]{1,0:T(8,128)(2,1)S(1)} %collective-permute-done.8.refs_1_), channel_id=1, source_target_pairs={{0,2},{1,5},{2,6},{3,1},{4,0},{5,9},{6,10},{7,3},{8,4},{9,13},{10,... | collective-permute-start | bytes 983048 | tf_op jit(solution)/shard_map/ppermute | solution.py:331
  56.4 10.3 %collective-permute-start.18 = (bf16[320,512]{1,0:T(8,128)(2,1)S(1)}, bf16[320,512]{1,0:T(8,128)(2,1)S(1)}, u32[]{:S(2)}, u32[]{:S(2)}) collective-permute-start(bf16[320,512]{1,0:T(8,128)(2,1)S(1)} %collective-permute-done.11.refs_1_), channel_id=1, source_target_pairs={{0,2},{1,5},{2,6},{3,1},{4,0},{5,9},{6,10},{7,3},{8,4},{9,13},{10,... | collective-permute-start | bytes 983048 | tf_op jit(solution)/shard_map/ppermute | solution.py:331
  59.9 7.1 %collective-permute-start.23 = (bf16[320,512]{1,0:T(8,128)(2,1)S(1)}, bf16[320,512]{1,0:T(8,128)(2,1)S(1)}, u32[]{:S(2)}, u32[]{:S(2)}) collective-permute-start(bf16[320,512]{1,0:T(8,128)(2,1)S(1)} %collective-permute-done.21.refs_2_), channel_id=1, source_target_pairs={{0,2},{1,5},{2,6},{3,1},{4,0},{5,9},{6,10},{7,3},{8,4},{9,13},{10,... | collective-permute-start | bytes 983048 | tf_op jit(solution)/shard_map/ppermute | solution.py:331
  60.9 10.9 %collective-permute-start.27 = (bf16[224,768]{1,0:T(8,128)(2,1)S(1)}, bf16[224,768]{1,0:T(8,128)(2,1)S(1)}, u32[]{:S(2)}, u32[]{:S(2)}) collective-permute-start(bf16[224,768]{1,0:T(8,128)(2,1)S(1)} %get-tuple-element.58), channel_id=1, source_target_pairs={{0,16},{16,0},{1,17},{17,1},{2,18},{18,2},{3,19},{19,3},{4,20},{20... | collective-permute-start | bytes 1032200 | tf_op jit(solution)/shard_map/ppermute | solution.py:46
  61.9 6.4 %collective-permute-start.28 = (bf16[320,512]{1,0:T(8,128)(2,1)S(1)}, bf16[320,512]{1,0:T(8,128)(2,1)S(1)}, u32[]{:S(2)}, u32[]{:S(2)}) collective-permute-start(bf16[320,512]{1,0:T(8,128)(2,1)S(1)} %collective-permute-done.11.refs_1_), channel_id=1, source_target_pairs={{0,1},{1,0},{2,3},{3,2},{4,5},{5,4},{6,7},{7,6},{8,9},{9,8},{10,11... | collective-permute-start | bytes 983048 | tf_op jit(solution)/shard_map/ppermute | solution.py:46
  65.7 12.4 %collective-permute-start.32 = (bf16[224,768]{1,0:T(8,128)(2,1)S(1)}, bf16[224,768]{1,0:T(8,128)(2,1)S(1)}, u32[]{:S(2)}, u32[]{:S(2)}) collective-permute-start(bf16[224,768]{1,0:T(8,128)(2,1)S(1)} %get-tuple-element.63), channel_id=1, source_target_pairs={{0,16},{16,0},{1,17},{17,1},{2,18},{18,2},{3,19},{19,3},{4,20},{20... | collective-permute-start | bytes 1032200 | tf_op jit(solution)/shard_map/ppermute | solution.py:46
  67.0 11.2 %collective-permute-start.24 = (bf16[320,512]{1,0:T(8,128)(2,1)S(1)}, bf16[320,512]{1,0:T(8,128)(2,1)S(1)}, u32[]{:S(2)}, u32[]{:S(2)}) collective-permute-start(bf16[320,512]{1,0:T(8,128)(2,1)S(1)} %collective-permute-done.18.refs_2_), channel_id=1, source_target_pairs={{0,2},{1,5},{2,6},{3,1},{4,0},{5,9},{6,10},{7,3},{8,4},{9,13},{10,... | collective-permute-start | bytes 983048 | tf_op jit(solution)/shard_map/ppermute | solution.py:331
  71.8 7.1 %collective-permute-start.29 = (bf16[320,512]{1,0:T(8,128)(2,1)S(1)}, bf16[320,512]{1,0:T(8,128)(2,1)S(1)}, u32[]{:S(2)}, u32[]{:S(2)}) collective-permute-start(bf16[320,512]{1,0:T(8,128)(2,1)S(1)} %collective-permute-done.23.refs_3_), channel_id=1, source_target_pairs={{0,2},{1,5},{2,6},{3,1},{4,0},{5,9},{6,10},{7,3},{8,4},{9,13},{10,... | collective-permute-start | bytes 983048 | tf_op jit(solution)/shard_map/ppermute | solution.py:331
  72.2 7.0 %collective-permute-start.33 = (bf16[320,512]{1,0:T(8,128)(2,1)S(1)}, bf16[320,512]{1,0:T(8,128)(2,1)S(1)}, u32[]{:S(2)}, u32[]{:S(2)}) collective-permute-start(bf16[320,512]{1,0:T(8,128)(2,1)S(1)} %collective-permute-done.18.refs_2_), channel_id=1, source_target_pairs={{0,1},{1,0},{2,3},{3,2},{4,5},{5,4},{6,7},{7,6},{8,9},{9,8},{10,11... | collective-permute-start | bytes 983048 | tf_op jit(solution)/shard_map/ppermute | solution.py:46
  78.2 5.9 %collective-permute-start.25 = (bf16[320,512]{1,0:T(8,128)(2,1)S(1)}, bf16[320,512]{1,0:T(8,128)(2,1)S(1)}, u32[]{:S(2)}, u32[]{:S(2)}) collective-permute-start(bf16[320,512]{1,0:T(8,128)(2,1)S(1)} %collective-permute-done.21.refs_2_), channel_id=1, source_target_pairs={{0,1},{1,0},{2,3},{3,2},{4,5},{5,4},{6,7},{7,6},{8,9},{9,8},{10,11... | collective-permute-start | bytes 983048 | tf_op jit(solution)/shard_map/ppermute | solution.py:46
  78.7 5.4 %collective-permute-start.26 = (bf16[320,512]{1,0:T(8,128)(2,1)S(1)}, bf16[320,512]{1,0:T(8,128)(2,1)S(1)}, u32[]{:S(2)}, u32[]{:S(2)}) collective-permute-start(bf16[320,512]{1,0:T(8,128)(2,1)S(1)} %collective-permute-done.23.refs_3_), channel_id=1, source_target_pairs={{0,1},{1,0},{2,3},{3,2},{4,5},{5,4},{6,7},{7,6},{8,9},{9,8},{10,11... | collective-permute-start | bytes 983048 | tf_op jit(solution)/shard_map/ppermute | solution.py:46
  82.5 8.5 %collective-permute-start.35 = (bf16[224,512]{1,0:T(8,128)(2,1)S(1)}, bf16[224,512]{1,0:T(8,128)(2,1)S(1)}, u32[]{:S(2)}, u32[]{:S(2)}) collective-permute-start(bf16[224,512]{1,0:T(8,128)(2,1)S(1)} %get-tuple-element.66), channel_id=1, source_target_pairs={{0,16},{16,0},{1,17},{17,1},{2,18},{18,2},{3,19},{19,3},{4,20},{20... | collective-permute-start | bytes 688136 | tf_op jit(solution)/shard_map/ppermute | solution.py:46
  86.8 8.3 %collective-permute-start.31 = (bf16[224,512]{1,0:T(8,128)(2,1)S(1)}, bf16[224,512]{1,0:T(8,128)(2,1)S(1)}, u32[]{:S(2)}, u32[]{:S(2)}) collective-permute-start(bf16[224,512]{1,0:T(8,128)(2,1)S(1)} %get-tuple-element.62), channel_id=1, source_target_pairs={{0,16},{16,0},{1,17},{17,1},{2,18},{18,2},{3,19},{19,3},{4,20},{20... | collective-permute-start | bytes 688136 | tf_op jit(solution)/shard_map/ppermute | solution.py:46
  (10 other events, 108.3 us)

commit v2 on v1

--- a/solution.py
+++ b/solution.py
@@ -384,7 +384,7 @@
                 waits[slot].append(arrived[slot - 1])
             else:
                 needs[first_done + 1] = [results[0, strip][0]]
-                waits.setdefault(len(hops) - 1, []).append(results[0, strip][1])
+                waits.setdefault(len(hops) - 2, []).append(results[0, strip][1])
         others = needs.get(slot - FLIGHT, [])
         cross(slot - FLIGHT, *(arrived[other] if isinstance(other, int) else other for other in others))
         hop(slot, *waits.get(slot, []))

time: 96.1 us -> 95.9 us (level)
  waiting for transfers between devices: 40.9 us -> 39.7 us
  starting transfers between devices: 29.4 us -> 30.4 us
    ppermute x22, waiting for transfers between devices: 19.3 us -> 17.2 us  [swap(): return lax.ppermute(value, axes, [(i, count - 1 - i) for i in range(count)])]
    ppermute x22, starting transfers between devices: 10.3 us -> 12.2 us  [swap(): return lax.ppermute(value, axes, [(i, count - 1 - i) for i in range(count)])]
  transfers between devices with their start and end apart: 36 -> 36, of which waited for: 17 -> 14; matrix products, arithmetic and copies ran while one was open for 0% -> 0% of each run, Pallas kernels for 24% -> 24%
where the time goes in v2:
time: 95.9 us; the launch traced here: 95.7 us
  waiting for transfers between devices  39.7 us (41%)
  starting transfers between devices  30.4 us (32%)
  Pallas kernels  25.5 us (27%)
    ppermute x14, waiting for transfers between devices, hop(): value = lax.ppermute(value, ('owner', 'slab'), ring)  22.5 us
    ppermute x14, starting transfers between devices, hop(): value = lax.ppermute(value, ('owner', 'slab'), ring)  18.2 us
    ppermute x22, waiting for transfers between devices, swap(): return lax.ppermute(value, axes, [(i, count - 1 - i) for i in range(count)])  17.2 us
    pallas_call x4, Pallas kernels, project(): pl.pallas_call(functools.partial(project_kernel, strip, column, total), o...  12.7 us
    ppermute x22, starting transfers between devices, swap(): return lax.ppermute(value, axes, [(i, count - 1 - i) for i in range(count)])  12.2 us
    pallas_call x2, Pallas kernels, attend(): pl.pallas_call(functools.partial(attend_kernel, spots), grid=(steps,), ou...  6.73 us
    pallas_call x2, Pallas kernels, cut(): pl.pallas_call(functools.partial(cut_kernel, first, total, with_border),...  2.81 us
    pallas_call x2, Pallas kernels, place(): pl.pallas_call(functools.partial(place_kernel, len(blocks), columns, tota...  2.05 us
  transfers between devices with their start and end apart: 36, of which 14 were waited for; matrix products, arithmetic and copies ran while one was open for 0% of the time, Pallas kernels for 24%

profile of v2, /device:TPU:0, one launch (start us, length us, event | category | flops | bytes accessed | tf_op | source)
XLA Modules:
  0.0 95.7 jit_solution(8189660081215399151)
XLA Ops:
  0.0 1.7 %cut.2 = (bf16[320,768]{1,0:T(8,128)(2,1)S(1)}, bf16[320,768]{1,0:T(8,128)(2,1)S(1)}, bf16[2,1,112,1280]{3,2,1,0:T(8,128)(2,1)S(1)}, bf16[2,1,112,1280]{3,2,1,0:T(8,128)(2,1)S(1)}) custom-call(bf16[320,5120]{1,0:T(8,128)(2,1)} %weight_ref.3, bf16[2,1,2,112,2560]{4,3,2,1,0:T(8,128)(2,1)} %key_value_ref.3), custom_call_target="tpu_custom_call" | custom-call | bytes 1966080 | tf_op jit(solution)/shard_map/cut/pallas_call | solution.py:84
  2.3 2.9 %collective-permute-start.3 = (bf16[320,768]{1,0:T(8,128)(2,1)S(1)}, bf16[320,768]{1,0:T(8,128)(2,1)S(1)}, u32[]{:S(2)}, u32[]{:S(2)}) collective-permute-start(bf16[320,768]{1,0:T(8,128)(2,1)S(1)} %get-tuple-element.40.refs_0_), channel_id=1, source_target_pairs={{0,2},{1,5},{2,6},{3,1},{4,0},{5,9},{6,10},{7,3},{8,4},{9,13},{10,... | collective-permute-start | bytes 1474568 | tf_op jit(solution)/shard_map/ppermute | solution.py:331
  5.3 1.6 %collective-permute-start.6 = (bf16[320,768]{1,0:T(8,128)(2,1)S(1)}, bf16[320,768]{1,0:T(8,128)(2,1)S(1)}, u32[]{:S(2)}, u32[]{:S(2)}) collective-permute-start(bf16[320,768]{1,0:T(8,128)(2,1)S(1)} %get-tuple-element.54.refs_0_), channel_id=1, source_target_pairs={{0,2},{1,5},{2,6},{3,1},{4,0},{5,9},{6,10},{7,3},{8,4},{9,13},{10,... | collective-permute-start | bytes 1474568 | tf_op jit(solution)/shard_map/ppermute | solution.py:331
  6.9 3.4 %attend.2.refs_0_ = bf16[224,2560]{1,0:T(8,128)(2,1)S(1)} custom-call(s32[4,3]{1,0:T(4,128)S(1)} %copy-done.3, bf16[224,2560]{1,0:T(8,128)(2,1)} %bitcast.11, bf16[2,224,2560]{2,1,0:T(8,128)(2,1)S(1)} %bitcast.5, bf16[2,224,2560]{2,1,0:T(8,128)(2,1)S(1)} %bitcast.6, bf16[2,112,1280]{2,1,0:T(8,128)(2,1)S(1)} %collective-permute-done.1.k_halo_ref.v_halo_ref, ...), custom_call_target="tpu_custom_call" | custom-call | flops 3523215360 | bytes 3112960 | tf_op jit(solution)/shard_map/attend/pallas_call | solution.py:171
  10.2 3.4 %attend.3.near_ref = bf16[224,2560]{1,0:T(8,128)(2,1)S(1)} custom-call(s32[4,3]{1,0:T(4,128)S(1)} %copy-done.3, bf16[224,2560]{1,0:T(8,128)(2,1)} %bitcast.12, bf16[2,224,2560]{2,1,0:T(8,128)(2,1)S(1)} %bitcast.7, bf16[2,224,2560]{2,1,0:T(8,128)(2,1)S(1)} %bitcast.8, ...), custom_call_target="tpu_custom_call", output_to_operand_aliasing={{}: (6, {})} | custom-call | flops 3523215360 | bytes 3112960 | tf_op jit(solution)/shard_map/attend/pallas_call | solution.py:171
  13.7 1.6 %collective-permute-start.4 = (bf16[320,768]{1,0:T(8,128)(2,1)S(1)}, bf16[320,768]{1,0:T(8,128)(2,1)S(1)}, u32[]{:S(2)}, u32[]{:S(2)}) collective-permute-start(bf16[320,768]{1,0:T(8,128)(2,1)S(1)} %collective-permute-done.3.refs_1_), channel_id=1, source_target_pairs={{0,2},{1,5},{2,6},{3,1},{4,0},{5,9},{6,10},{7,3},{8,4},{9,13},{10,... | collective-permute-start | bytes 1474568 | tf_op jit(solution)/shard_map/ppermute | solution.py:331
  15.3 1.5 %collective-permute-start.2 = (bf16[224,2560]{1,0:T(8,128)(2,1)S(1)}, bf16[224,2560]{1,0:T(8,128)(2,1)S(1)}, u32[]{:S(2)}, u32[]{:S(2)}) collective-permute-start(bf16[224,2560]{1,0:T(8,128)(2,1)S(1)} %attend.3.near_ref), channel_id=1, source_target_pairs={{0,16},{16,0},{1,17},{17,1},{2,18},{18,2},{3,19},{19,3},{4,20},{20... | collective-permute-start | bytes 3440648 | tf_op jit(solution)/shard_map/ppermute | solution.py:46
  17.4 2.0 %collective-permute-start.9 = (bf16[320,768]{1,0:T(8,128)(2,1)S(1)}, bf16[320,768]{1,0:T(8,128)(2,1)S(1)}, u32[]{:S(2)}, u32[]{:S(2)}) collective-permute-start(bf16[320,768]{1,0:T(8,128)(2,1)S(1)} %collective-permute-done.6.refs_1_), channel_id=1, source_target_pairs={{0,2},{1,5},{2,6},{3,1},{4,0},{5,9},{6,10},{7,3},{8,4},{9,13},{10,... | collective-permute-start | bytes 1474568 | tf_op jit(solution)/shard_map/ppermute | solution.py:331
  21.0 1.6 %collective-permute-done.4.refs_2_ = bf16[320,768]{1,0:T(8,128)(2,1)S(1)} collective-permute-done((bf16[320,768]{1,0:T(8,128)(2,1)S(1)}, bf16[320,768]{1,0:T(8,128)(2,1)S(1)}, u32[]{:S(2)}, u32[]{:S(2)}) %collective-permute-start.4) | collective-permute-done | bytes 491552 | tf_op jit(solution)/shard_map/ppermute | solution.py:331
  22.7 2.0 %collective-permute-start.5 = (bf16[320,768]{1,0:T(8,128)(2,1)S(1)}, bf16[320,768]{1,0:T(8,128)(2,1)S(1)}, u32[]{:S(2)}, u32[]{:S(2)}) collective-permute-start(bf16[320,768]{1,0:T(8,128)(2,1)S(1)} %collective-permute-done.4.refs_2_), channel_id=1, source_target_pairs={{0,2},{1,5},{2,6},{3,1},{4,0},{5,9},{6,10},{7,3},{8,4},{9,13},{10,... | collective-permute-start | bytes 1474568 | tf_op jit(solution)/shard_map/ppermute | solution.py:331
  24.6 3.3 %collective-permute-done.9.refs_2_ = bf16[320,768]{1,0:T(8,128)(2,1)S(1)} collective-permute-done((bf16[320,768]{1,0:T(8,128)(2,1)S(1)}, bf16[320,768]{1,0:T(8,128)(2,1)S(1)}, u32[]{:S(2)}, u32[]{:S(2)}) %collective-permute-start.9) | collective-permute-done | bytes 491552 | tf_op jit(solution)/shard_map/ppermute | solution.py:331
  27.9 2.0 %collective-permute-start.13 = (bf16[320,768]{1,0:T(8,128)(2,1)S(1)}, bf16[320,768]{1,0:T(8,128)(2,1)S(1)}, u32[]{:S(2)}, u32[]{:S(2)}) collective-permute-start(bf16[320,768]{1,0:T(8,128)(2,1)S(1)} %collective-permute-done.9.refs_2_), channel_id=1, source_target_pairs={{0,2},{1,5},{2,6},{3,1},{4,0},{5,9},{6,10},{7,3},{8,4},{9,13},{10,... | collective-permute-start | bytes 1474568 | tf_op jit(solution)/shard_map/ppermute | solution.py:331
  29.9 3.3 %collective-permute-done.5.refs_3_ = bf16[320,768]{1,0:T(8,128)(2,1)S(1)} collective-permute-done((bf16[320,768]{1,0:T(8,128)(2,1)S(1)}, bf16[320,768]{1,0:T(8,128)(2,1)S(1)}, u32[]{:S(2)}, u32[]{:S(2)}) %collective-permute-start.5) | collective-permute-done | bytes 491552 | tf_op jit(solution)/shard_map/ppermute | solution.py:331
  33.2 2.0 %collective-permute-start.8 = (bf16[320,512]{1,0:T(8,128)(2,1)S(1)}, bf16[320,512]{1,0:T(8,128)(2,1)S(1)}, u32[]{:S(2)}, u32[]{:S(2)}) collective-permute-start(bf16[320,512]{1,0:T(8,128)(2,1)S(1)} %get-tuple-element.44.refs_0_), channel_id=1, source_target_pairs={{0,2},{1,5},{2,6},{3,1},{4,0},{5,9},{6,10},{7,3},{8,4},{9,13},{10,... | collective-permute-start | bytes 983048 | tf_op jit(solution)/shard_map/ppermute | solution.py:331
  35.2 3.3 %collective-permute-done.13.refs_3_ = bf16[320,768]{1,0:T(8,128)(2,1)S(1)} collective-permute-done((bf16[320,768]{1,0:T(8,128)(2,1)S(1)}, bf16[320,768]{1,0:T(8,128)(2,1)S(1)}, u32[]{:S(2)}, u32[]{:S(2)}) %collective-permute-start.13) | collective-permute-done | bytes 491552 | tf_op jit(solution)/shard_map/ppermute | solution.py:331
  38.5 3.3 %collective-permute-done.2.far_ref = bf16[224,2560]{1,0:T(8,128)(2,1)S(1)} collective-permute-done((bf16[224,2560]{1,0:T(8,128)(2,1)S(1)}, bf16[224,2560]{1,0:T(8,128)(2,1)S(1)}, u32[]{:S(2)}, u32[]{:S(2)}) %collective-permute-start.2) | collective-permute-done | bytes 1146912 | tf_op jit(solution)/shard_map/ppermute | solution.py:46
  43.3 1.6 %collective-permute-start.16 = (f32[1,5120]{1,0:T(1,128)S(1)}, f32[1,5120]{1,0:T(1,128)S(1)}, u32[]{:S(2)}, u32[]{:S(2)}) collective-permute-start(f32[1,5120]{1,0:T(1,128)S(1)} %scale_gate.1.refs_8_), channel_id=1, source_target_pairs={{0,16},{16,0},{1,17},{17,1},{2,18},{18,2},{3,19},{19,3},{4,20},{20... | collective-permute-start | bytes 61448 | tf_op jit(solution)/shard_map/ppermute | solution.py:46
  45.5 1.7 %collective-permute-done.16.refs_9_ = f32[1,5120]{1,0:T(1,128)S(1)} collective-permute-done((f32[1,5120]{1,0:T(1,128)S(1)}, f32[1,5120]{1,0:T(1,128)S(1)}, u32[]{:S(2)}, u32[]{:S(2)}) %collective-permute-start.16) | collective-permute-done | bytes 20512 | tf_op jit(solution)/shard_map/ppermute | solution.py:46
  47.2 3.4 %collective-permute-done.15.refs_4_ = bf16[320,768]{1,0:T(8,128)(2,1)S(1)} collective-permute-done((bf16[320,768]{1,0:T(8,128)(2,1)S(1)}, bf16[320,768]{1,0:T(8,128)(2,1)S(1)}, u32[]{:S(2)}, u32[]{:S(2)}) %collective-permute-start.15) | collective-permute-done | bytes 491552 | tf_op jit(solution)/shard_map/ppermute | solution.py:331
  52.8 3.7 %project.4 = (bf16[224,768]{1,0:T(8,128)(2,1)S(1)}, bf16[224,768]{1,0:T(8,128)(2,1)S(1)}) custom-call(s32[2,8,8]{2,1,0:T(8,128)S(1)} %copy-done.5, bf16[8,448,320]{2,1,0:T(8,128)(2,1)S(1)} %arrange.1.rows_ref, bf16[320,768]{1,0:T(8,128)(2,1)S(1)} %get-tuple-element.40.refs_0_, bf16[320,768]{1,0:T(8,128)(2,1)S(1)} %collective-permute-done.3.refs_1_, ...), custom_call_target="tpu_custom_call" | custom-call | flops 2642411520 | bytes 6914048 | tf_op jit(solution)/shard_map/project/pallas_call | solution.py:240
  56.5 1.6 %collective-permute-start.19 = (bf16[224,768]{1,0:T(8,128)(2,1)S(1)}, bf16[224,768]{1,0:T(8,128)(2,1)S(1)}, u32[]{:S(2)}, u32[]{:S(2)}) collective-permute-start(bf16[224,768]{1,0:T(8,128)(2,1)S(1)} %get-tuple-element.53), channel_id=1, source_target_pairs={{0,16},{16,0},{1,17},{17,1},{2,18},{18,2},{3,19},{19,3},{4,20},{20... | collective-permute-start | bytes 1032200 | tf_op jit(solution)/shard_map/ppermute | solution.py:46
  58.5 2.7 %collective-permute-done.22.refs_2_ = bf16[320,512]{1,0:T(8,128)(2,1)S(1)} collective-permute-done((bf16[320,512]{1,0:T(8,128)(2,1)S(1)}, bf16[320,512]{1,0:T(8,128)(2,1)S(1)}, u32[]{:S(2)}, u32[]{:S(2)}) %collective-permute-start.22) | collective-permute-done | bytes 327712 | tf_op jit(solution)/shard_map/ppermute | solution.py:331
  62.1 3.7 %project.5 = (bf16[224,768]{1,0:T(8,128)(2,1)S(1)}, bf16[224,768]{1,0:T(8,128)(2,1)S(1)}) custom-call(s32[2,8,8]{2,1,0:T(8,128)S(1)} %copy-done.4, bf16[8,448,320]{2,1,0:T(8,128)(2,1)S(1)} %arrange.1.rows_ref, bf16[320,768]{1,0:T(8,128)(2,1)S(1)} %get-tuple-element.54.refs_0_, bf16[320,768]{1,0:T(8,128)(2,1)S(1)} %collective-permute-done.6.refs_1_, ...), custom_call_target="tpu_custom_call" | custom-call | flops 2642411520 | bytes 6914048 | tf_op jit(solution)/shard_map/project/pallas_call | solution.py:240
  65.7 1.6 %collective-permute-start.32 = (bf16[224,768]{1,0:T(8,128)(2,1)S(1)}, bf16[224,768]{1,0:T(8,128)(2,1)S(1)}, u32[]{:S(2)}, u32[]{:S(2)}) collective-permute-start(bf16[224,768]{1,0:T(8,128)(2,1)S(1)} %get-tuple-element.63), channel_id=1, source_target_pairs={{0,16},{16,0},{1,17},{17,1},{2,18},{18,2},{3,19},{19,3},{4,20},{20... | collective-permute-start | bytes 1032200 | tf_op jit(solution)/shard_map/ppermute | solution.py:46
  67.3 1.4 %collective-permute-done.24.refs_3_ = bf16[320,512]{1,0:T(8,128)(2,1)S(1)} collective-permute-done((bf16[320,512]{1,0:T(8,128)(2,1)S(1)}, bf16[320,512]{1,0:T(8,128)(2,1)S(1)}, u32[]{:S(2)}, u32[]{:S(2)}) %collective-permute-start.24) | collective-permute-done | bytes 327712 | tf_op jit(solution)/shard_map/ppermute | solution.py:331
  69.1 1.4 %collective-permute-start.29 = (bf16[320,512]{1,0:T(8,128)(2,1)S(1)}, bf16[320,512]{1,0:T(8,128)(2,1)S(1)}, u32[]{:S(2)}, u32[]{:S(2)}) collective-permute-start(bf16[320,512]{1,0:T(8,128)(2,1)S(1)} %collective-permute-done.24.refs_3_), channel_id=1, source_target_pairs={{0,2},{1,5},{2,6},{3,1},{4,0},{5,9},{6,10},{7,3},{8,4},{9,13},{10,... | collective-permute-start | bytes 983048 | tf_op jit(solution)/shard_map/ppermute | solution.py:331
  70.5 5.4 %collective-permute-done.32.refs_3_ = bf16[224,768]{1,0:T(8,128)(2,1)S(1)} collective-permute-done((bf16[224,768]{1,0:T(8,128)(2,1)S(1)}, bf16[224,768]{1,0:T(8,128)(2,1)S(1)}, u32[]{:S(2)}, u32[]{:S(2)}) %collective-permute-start.32) | collective-permute-done | bytes 344096 | tf_op jit(solution)/shard_map/ppermute | solution.py:46
  76.4 2.8 %collective-permute-done.29.refs_4_ = bf16[320,512]{1,0:T(8,128)(2,1)S(1)} collective-permute-done((bf16[320,512]{1,0:T(8,128)(2,1)S(1)}, bf16[320,512]{1,0:T(8,128)(2,1)S(1)}, u32[]{:S(2)}, u32[]{:S(2)}) %collective-permute-start.29) | collective-permute-done | bytes 327712 | tf_op jit(solution)/shard_map/ppermute | solution.py:331
  79.3 2.7 %project.7 = (bf16[224,512]{1,0:T(8,128)(2,1)S(1)}, bf16[224,512]{1,0:T(8,128)(2,1)S(1)}) custom-call(s32[2,8,8]{2,1,0:T(8,128)S(1)} %copy-done.5, bf16[8,448,320]{2,1,0:T(8,128)(2,1)S(1)} %arrange.1.rows_ref, bf16[320,512]{1,0:T(8,128)(2,1)S(1)} %get-tuple-element.44.refs_0_, bf16[320,512]{1,0:T(8,128)(2,1)S(1)} %collective-permute-done.8.refs_1_, ...), custom_call_target="tpu_custom_call" | custom-call | flops 1761607680 | bytes 5373952 | tf_op jit(solution)/shard_map/project/pallas_call | solution.py:240
  83.2 2.7 %project.6 = (bf16[224,512]{1,0:T(8,128)(2,1)S(1)}, bf16[224,512]{1,0:T(8,128)(2,1)S(1)}) custom-call(s32[2,8,8]{2,1,0:T(8,128)S(1)} %copy-done.4, bf16[8,448,320]{2,1,0:T(8,128)(2,1)S(1)} %arrange.1.rows_ref, bf16[320,512]{1,0:T(8,128)(2,1)S(1)} %get-tuple-element.46.refs_0_, bf16[320,512]{1,0:T(8,128)(2,1)S(1)} %collective-permute-done.11.refs_1_, ...), custom_call_target="tpu_custom_call" | custom-call | flops 1761607680 | bytes 5373952 | tf_op jit(solution)/shard_map/project/pallas_call | solution.py:240
  86.9 3.6 %collective-permute-done.35.refs_5_ = bf16[224,512]{1,0:T(8,128)(2,1)S(1)} collective-permute-done((bf16[224,512]{1,0:T(8,128)(2,1)S(1)}, bf16[224,512]{1,0:T(8,128)(2,1)S(1)}, u32[]{:S(2)}, u32[]{:S(2)}) %collective-permute-start.35) | collective-permute-done | bytes 229408 | tf_op jit(solution)/shard_map/ppermute | solution.py:46
  91.7 3.2 %collective-permute-done.31.refs_1_ = bf16[224,512]{1,0:T(8,128)(2,1)S(1)} collective-permute-done((bf16[224,512]{1,0:T(8,128)(2,1)S(1)}, bf16[224,512]{1,0:T(8,128)(2,1)S(1)}, u32[]{:S(2)}, u32[]{:S(2)}) %collective-permute-start.31) | collective-permute-done | bytes 229408 | tf_op jit(solution)/shard_map/ppermute | solution.py:46
  (64 shorter events, 13.8 us)
Async XLA Ops:
  2.3 8.0 %collective-permute-start = (bf16[2,112,1280]{2,1,0:T(8,128)(2,1)S(1)}, bf16[2,112,1280]{2,1,0:T(8,128)(2,1)S(1)}, u32[]{:S(2)}, u32[]{:S(2)}) collective-permute-start(bf16[2,112,1280]{2,1,0:T(8,128)(2,1)S(1)} %bitcast.9), channel_id=1, source_target_pairs={{0,1},{1,0},{2,3},{3,2},{4,5},{5,4},{6,7},{7,6},{8,9},{9,8},{10,11... | collective-permute-start | bytes 1720328 | tf_op jit(solution)/shard_map/ppermute | solution.py:46
  2.3 11.3 %collective-permute-start.3 = (bf16[320,768]{1,0:T(8,128)(2,1)S(1)}, bf16[320,768]{1,0:T(8,128)(2,1)S(1)}, u32[]{:S(2)}, u32[]{:S(2)}) collective-permute-start(bf16[320,768]{1,0:T(8,128)(2,1)S(1)} %get-tuple-element.40.refs_0_), channel_id=1, source_target_pairs={{0,2},{1,5},{2,6},{3,1},{4,0},{5,9},{6,10},{7,3},{8,4},{9,13},{10,... | collective-permute-start | bytes 1474568 | tf_op jit(solution)/shard_map/ppermute | solution.py:331
  5.3 12.1 %collective-permute-start.6 = (bf16[320,768]{1,0:T(8,128)(2,1)S(1)}, bf16[320,768]{1,0:T(8,128)(2,1)S(1)}, u32[]{:S(2)}, u32[]{:S(2)}) collective-permute-start(bf16[320,768]{1,0:T(8,128)(2,1)S(1)} %get-tuple-element.54.refs_0_), channel_id=1, source_target_pairs={{0,2},{1,5},{2,6},{3,1},{4,0},{5,9},{6,10},{7,3},{8,4},{9,13},{10,... | collective-permute-start | bytes 1474568 | tf_op jit(solution)/shard_map/ppermute | solution.py:331
  13.7 9.0 %collective-permute-start.4 = (bf16[320,768]{1,0:T(8,128)(2,1)S(1)}, bf16[320,768]{1,0:T(8,128)(2,1)S(1)}, u32[]{:S(2)}, u32[]{:S(2)}) collective-permute-start(bf16[320,768]{1,0:T(8,128)(2,1)S(1)} %collective-permute-done.3.refs_1_), channel_id=1, source_target_pairs={{0,2},{1,5},{2,6},{3,1},{4,0},{5,9},{6,10},{7,3},{8,4},{9,13},{10,... | collective-permute-start | bytes 1474568 | tf_op jit(solution)/shard_map/ppermute | solution.py:331
  15.3 26.5 %collective-permute-start.2 = (bf16[224,2560]{1,0:T(8,128)(2,1)S(1)}, bf16[224,2560]{1,0:T(8,128)(2,1)S(1)}, u32[]{:S(2)}, u32[]{:S(2)}) collective-permute-start(bf16[224,2560]{1,0:T(8,128)(2,1)S(1)} %attend.3.near_ref), channel_id=1, source_target_pairs={{0,16},{16,0},{1,17},{17,1},{2,18},{18,2},{3,19},{19,3},{4,20},{20... | collective-permute-start | bytes 3440648 | tf_op jit(solution)/shard_map/ppermute | solution.py:46
  17.4 10.5 %collective-permute-start.9 = (bf16[320,768]{1,0:T(8,128)(2,1)S(1)}, bf16[320,768]{1,0:T(8,128)(2,1)S(1)}, u32[]{:S(2)}, u32[]{:S(2)}) collective-permute-start(bf16[320,768]{1,0:T(8,128)(2,1)S(1)} %collective-permute-done.6.refs_1_), channel_id=1, source_target_pairs={{0,2},{1,5},{2,6},{3,1},{4,0},{5,9},{6,10},{7,3},{8,4},{9,13},{10,... | collective-permute-start | bytes 1474568 | tf_op jit(solution)/shard_map/ppermute | solution.py:331
  19.4 8.6 %collective-permute-start.12 = (bf16[320,768]{1,0:T(8,128)(2,1)S(1)}, bf16[320,768]{1,0:T(8,128)(2,1)S(1)}, u32[]{:S(2)}, u32[]{:S(2)}) collective-permute-start(bf16[320,768]{1,0:T(8,128)(2,1)S(1)} %collective-permute-done.3.refs_1_), channel_id=1, source_target_pairs={{0,1},{1,0},{2,3},{3,2},{4,5},{5,4},{6,7},{7,6},{8,9},{9,8},{10,11... | collective-permute-start | bytes 1474568 | tf_op jit(solution)/shard_map/ppermute | solution.py:46
  20.5 9.4 %collective-permute-start.7 = (bf16[320,768]{1,0:T(8,128)(2,1)S(1)}, bf16[320,768]{1,0:T(8,128)(2,1)S(1)}, u32[]{:S(2)}, u32[]{:S(2)}) collective-permute-start(bf16[320,768]{1,0:T(8,128)(2,1)S(1)} %collective-permute-done.6.refs_1_), channel_id=1, source_target_pairs={{0,1},{1,0},{2,3},{3,2},{4,5},{5,4},{6,7},{7,6},{8,9},{9,8},{10,11... | collective-permute-start | bytes 1474568 | tf_op jit(solution)/shard_map/ppermute | solution.py:46
  22.7 10.5 %collective-permute-start.5 = (bf16[320,768]{1,0:T(8,128)(2,1)S(1)}, bf16[320,768]{1,0:T(8,128)(2,1)S(1)}, u32[]{:S(2)}, u32[]{:S(2)}) collective-permute-start(bf16[320,768]{1,0:T(8,128)(2,1)S(1)} %collective-permute-done.4.refs_2_), channel_id=1, source_target_pairs={{0,2},{1,5},{2,6},{3,1},{4,0},{5,9},{6,10},{7,3},{8,4},{9,13},{10,... | collective-permute-start | bytes 1474568 | tf_op jit(solution)/shard_map/ppermute | solution.py:331
  27.9 10.5 %collective-permute-start.13 = (bf16[320,768]{1,0:T(8,128)(2,1)S(1)}, bf16[320,768]{1,0:T(8,128)(2,1)S(1)}, u32[]{:S(2)}, u32[]{:S(2)}) collective-permute-start(bf16[320,768]{1,0:T(8,128)(2,1)S(1)} %collective-permute-done.9.refs_2_), channel_id=1, source_target_pairs={{0,2},{1,5},{2,6},{3,1},{4,0},{5,9},{6,10},{7,3},{8,4},{9,13},{10,... | collective-permute-start | bytes 1474568 | tf_op jit(solution)/shard_map/ppermute | solution.py:331
  29.9 8.6 %collective-permute-start.14 = (bf16[320,768]{1,0:T(8,128)(2,1)S(1)}, bf16[320,768]{1,0:T(8,128)(2,1)S(1)}, u32[]{:S(2)}, u32[]{:S(2)}) collective-permute-start(bf16[320,768]{1,0:T(8,128)(2,1)S(1)} %collective-permute-done.4.refs_2_), channel_id=1, source_target_pairs={{0,1},{1,0},{2,3},{3,2},{4,5},{5,4},{6,7},{7,6},{8,9},{9,8},{10,11... | collective-permute-start | bytes 1474568 | tf_op jit(solution)/shard_map/ppermute | solution.py:46
  33.2 13.9 %collective-permute-start.8 = (bf16[320,512]{1,0:T(8,128)(2,1)S(1)}, bf16[320,512]{1,0:T(8,128)(2,1)S(1)}, u32[]{:S(2)}, u32[]{:S(2)}) collective-permute-start(bf16[320,512]{1,0:T(8,128)(2,1)S(1)} %get-tuple-element.44.refs_0_), channel_id=1, source_target_pairs={{0,2},{1,5},{2,6},{3,1},{4,0},{5,9},{6,10},{7,3},{8,4},{9,13},{10,... | collective-permute-start | bytes 983048 | tf_op jit(solution)/shard_map/ppermute | solution.py:331
  41.7 8.8 %collective-permute-start.15 = (bf16[320,768]{1,0:T(8,128)(2,1)S(1)}, bf16[320,768]{1,0:T(8,128)(2,1)S(1)}, u32[]{:S(2)}, u32[]{:S(2)}) collective-permute-start(bf16[320,768]{1,0:T(8,128)(2,1)S(1)} %collective-permute-done.5.refs_3_), channel_id=1, source_target_pairs={{0,2},{1,5},{2,6},{3,1},{4,0},{5,9},{6,10},{7,3},{8,4},{9,13},{10,... | collective-permute-start | bytes 1474568 | tf_op jit(solution)/shard_map/ppermute | solution.py:331
  42.2 8.4 %collective-permute-start.10 = (bf16[320,768]{1,0:T(8,128)(2,1)S(1)}, bf16[320,768]{1,0:T(8,128)(2,1)S(1)}, u32[]{:S(2)}, u32[]{:S(2)}) collective-permute-start(bf16[320,768]{1,0:T(8,128)(2,1)S(1)} %collective-permute-done.9.refs_2_), channel_id=1, source_target_pairs={{0,1},{1,0},{2,3},{3,2},{4,5},{5,4},{6,7},{7,6},{8,9},{9,8},{10,11... | collective-permute-start | bytes 1474568 | tf_op jit(solution)/shard_map/ppermute | solution.py:46
  42.5 9.8 %collective-permute-start.20 = (bf16[320,768]{1,0:T(8,128)(2,1)S(1)}, bf16[320,768]{1,0:T(8,128)(2,1)S(1)}, u32[]{:S(2)}, u32[]{:S(2)}) collective-permute-start(bf16[320,768]{1,0:T(8,128)(2,1)S(1)} %collective-permute-done.5.refs_3_), channel_id=1, source_target_pairs={{0,1},{1,0},{2,3},{3,2},{4,5},{5,4},{6,7},{7,6},{8,9},{9,8},{10,11... | collective-permute-start | bytes 1474568 | tf_op jit(solution)/shard_map/ppermute | solution.py:46
  47.2 5.7 %collective-permute-start.17 = (bf16[320,768]{1,0:T(8,128)(2,1)S(1)}, bf16[320,768]{1,0:T(8,128)(2,1)S(1)}, u32[]{:S(2)}, u32[]{:S(2)}) collective-permute-start(bf16[320,768]{1,0:T(8,128)(2,1)S(1)} %collective-permute-done.13.refs_3_), channel_id=1, source_target_pairs={{0,1},{1,0},{2,3},{3,2},{4,5},{5,4},{6,7},{7,6},{8,9},{9,8},{10,11... | collective-permute-start | bytes 1474568 | tf_op jit(solution)/shard_map/ppermute | solution.py:46
  50.6 11.5 %collective-permute-start.21 = (bf16[320,768]{1,0:T(8,128)(2,1)S(1)}, bf16[320,768]{1,0:T(8,128)(2,1)S(1)}, u32[]{:S(2)}, u32[]{:S(2)}) collective-permute-start(bf16[320,768]{1,0:T(8,128)(2,1)S(1)} %collective-permute-done.15.refs_4_), channel_id=1, source_target_pairs={{0,1},{1,0},{2,3},{3,2},{4,5},{5,4},{6,7},{7,6},{8,9},{9,8},{10,11... | collective-permute-start | bytes 1474568 | tf_op jit(solution)/shard_map/ppermute | solution.py:46
  50.6 7.5 %collective-permute-start.11 = (bf16[320,512]{1,0:T(8,128)(2,1)S(1)}, bf16[320,512]{1,0:T(8,128)(2,1)S(1)}, u32[]{:S(2)}, u32[]{:S(2)}) collective-permute-start(bf16[320,512]{1,0:T(8,128)(2,1)S(1)} %get-tuple-element.46.refs_0_), channel_id=1, source_target_pairs={{0,2},{1,5},{2,6},{3,1},{4,0},{5,9},{6,10},{7,3},{8,4},{9,13},{10,... | collective-permute-start | bytes 983048 | tf_op jit(solution)/shard_map/ppermute | solution.py:331
  51.1 7.4 %collective-permute-start.23 = (bf16[320,512]{1,0:T(8,128)(2,1)S(1)}, bf16[320,512]{1,0:T(8,128)(2,1)S(1)}, u32[]{:S(2)}, u32[]{:S(2)}) collective-permute-start(bf16[320,512]{1,0:T(8,128)(2,1)S(1)} %collective-permute-done.8.refs_1_), channel_id=1, source_target_pairs={{0,1},{1,0},{2,3},{3,2},{4,5},{5,4},{6,7},{7,6},{8,9},{9,8},{10,11... | collective-permute-start | bytes 983048 | tf_op jit(solution)/shard_map/ppermute | solution.py:46
  52.3 8.9 %collective-permute-start.22 = (bf16[320,512]{1,0:T(8,128)(2,1)S(1)}, bf16[320,512]{1,0:T(8,128)(2,1)S(1)}, u32[]{:S(2)}, u32[]{:S(2)}) collective-permute-start(bf16[320,512]{1,0:T(8,128)(2,1)S(1)} %collective-permute-done.8.refs_1_), channel_id=1, source_target_pairs={{0,2},{1,5},{2,6},{3,1},{4,0},{5,9},{6,10},{7,3},{8,4},{9,13},{10,... | collective-permute-start | bytes 983048 | tf_op jit(solution)/shard_map/ppermute | solution.py:331
  56.5 10.8 %collective-permute-start.19 = (bf16[224,768]{1,0:T(8,128)(2,1)S(1)}, bf16[224,768]{1,0:T(8,128)(2,1)S(1)}, u32[]{:S(2)}, u32[]{:S(2)}) collective-permute-start(bf16[224,768]{1,0:T(8,128)(2,1)S(1)} %get-tuple-element.53), channel_id=1, source_target_pairs={{0,16},{16,0},{1,17},{17,1},{2,18},{18,2},{3,19},{19,3},{4,20},{20... | collective-permute-start | bytes 1032200 | tf_op jit(solution)/shard_map/ppermute | solution.py:46
  58.1 9.2 %collective-permute-start.18 = (bf16[320,512]{1,0:T(8,128)(2,1)S(1)}, bf16[320,512]{1,0:T(8,128)(2,1)S(1)}, u32[]{:S(2)}, u32[]{:S(2)}) collective-permute-start(bf16[320,512]{1,0:T(8,128)(2,1)S(1)} %collective-permute-done.11.refs_1_), channel_id=1, source_target_pairs={{0,2},{1,5},{2,6},{3,1},{4,0},{5,9},{6,10},{7,3},{8,4},{9,13},{10,... | collective-permute-start | bytes 983048 | tf_op jit(solution)/shard_map/ppermute | solution.py:331
  61.2 7.4 %collective-permute-start.24 = (bf16[320,512]{1,0:T(8,128)(2,1)S(1)}, bf16[320,512]{1,0:T(8,128)(2,1)S(1)}, u32[]{:S(2)}, u32[]{:S(2)}) collective-permute-start(bf16[320,512]{1,0:T(8,128)(2,1)S(1)} %collective-permute-done.22.refs_2_), channel_id=1, source_target_pairs={{0,2},{1,5},{2,6},{3,1},{4,0},{5,9},{6,10},{7,3},{8,4},{9,13},{10,... | collective-permute-start | bytes 983048 | tf_op jit(solution)/shard_map/ppermute | solution.py:331
  61.7 7.4 %collective-permute-start.28 = (bf16[320,512]{1,0:T(8,128)(2,1)S(1)}, bf16[320,512]{1,0:T(8,128)(2,1)S(1)}, u32[]{:S(2)}, u32[]{:S(2)}) collective-permute-start(bf16[320,512]{1,0:T(8,128)(2,1)S(1)} %collective-permute-done.11.refs_1_), channel_id=1, source_target_pairs={{0,1},{1,0},{2,3},{3,2},{4,5},{5,4},{6,7},{7,6},{8,9},{9,8},{10,11... | collective-permute-start | bytes 983048 | tf_op jit(solution)/shard_map/ppermute | solution.py:46
  65.7 10.2 %collective-permute-start.32 = (bf16[224,768]{1,0:T(8,128)(2,1)S(1)}, bf16[224,768]{1,0:T(8,128)(2,1)S(1)}, u32[]{:S(2)}, u32[]{:S(2)}) collective-permute-start(bf16[224,768]{1,0:T(8,128)(2,1)S(1)} %get-tuple-element.63), channel_id=1, source_target_pairs={{0,16},{16,0},{1,17},{17,1},{2,18},{18,2},{3,19},{19,3},{4,20},{20... | collective-permute-start | bytes 1032200 | tf_op jit(solution)/shard_map/ppermute | solution.py:46
  68.7 7.2 %collective-permute-start.25 = (bf16[320,512]{1,0:T(8,128)(2,1)S(1)}, bf16[320,512]{1,0:T(8,128)(2,1)S(1)}, u32[]{:S(2)}, u32[]{:S(2)}) collective-permute-start(bf16[320,512]{1,0:T(8,128)(2,1)S(1)} %collective-permute-done.18.refs_2_), channel_id=1, source_target_pairs={{0,2},{1,5},{2,6},{3,1},{4,0},{5,9},{6,10},{7,3},{8,4},{9,13},{10,... | collective-permute-start | bytes 983048 | tf_op jit(solution)/shard_map/ppermute | solution.py:331
  69.1 10.1 %collective-permute-start.29 = (bf16[320,512]{1,0:T(8,128)(2,1)S(1)}, bf16[320,512]{1,0:T(8,128)(2,1)S(1)}, u32[]{:S(2)}, u32[]{:S(2)}) collective-permute-start(bf16[320,512]{1,0:T(8,128)(2,1)S(1)} %collective-permute-done.24.refs_3_), channel_id=1, source_target_pairs={{0,2},{1,5},{2,6},{3,1},{4,0},{5,9},{6,10},{7,3},{8,4},{9,13},{10,... | collective-permute-start | bytes 983048 | tf_op jit(solution)/shard_map/ppermute | solution.py:331
  70.5 8.7 %collective-permute-start.33 = (bf16[320,512]{1,0:T(8,128)(2,1)S(1)}, bf16[320,512]{1,0:T(8,128)(2,1)S(1)}, u32[]{:S(2)}, u32[]{:S(2)}) collective-permute-start(bf16[320,512]{1,0:T(8,128)(2,1)S(1)} %collective-permute-done.18.refs_2_), channel_id=1, source_target_pairs={{0,1},{1,0},{2,3},{3,2},{4,5},{5,4},{6,7},{7,6},{8,9},{9,8},{10,11... | collective-permute-start | bytes 983048 | tf_op jit(solution)/shard_map/ppermute | solution.py:46
  75.9 7.3 %collective-permute-start.26 = (bf16[320,512]{1,0:T(8,128)(2,1)S(1)}, bf16[320,512]{1,0:T(8,128)(2,1)S(1)}, u32[]{:S(2)}, u32[]{:S(2)}) collective-permute-start(bf16[320,512]{1,0:T(8,128)(2,1)S(1)} %collective-permute-done.22.refs_2_), channel_id=1, source_target_pairs={{0,1},{1,0},{2,3},{3,2},{4,5},{5,4},{6,7},{7,6},{8,9},{9,8},{10,11... | collective-permute-start | bytes 983048 | tf_op jit(solution)/shard_map/ppermute | solution.py:46
  76.4 6.8 %collective-permute-start.27 = (bf16[320,512]{1,0:T(8,128)(2,1)S(1)}, bf16[320,512]{1,0:T(8,128)(2,1)S(1)}, u32[]{:S(2)}, u32[]{:S(2)}) collective-permute-start(bf16[320,512]{1,0:T(8,128)(2,1)S(1)} %collective-permute-done.24.refs_3_), channel_id=1, source_target_pairs={{0,1},{1,0},{2,3},{3,2},{4,5},{5,4},{6,7},{7,6},{8,9},{9,8},{10,11... | collective-permute-start | bytes 983048 | tf_op jit(solution)/shard_map/ppermute | solution.py:46
  82.0 8.5 %collective-permute-start.35 = (bf16[224,512]{1,0:T(8,128)(2,1)S(1)}, bf16[224,512]{1,0:T(8,128)(2,1)S(1)}, u32[]{:S(2)}, u32[]{:S(2)}) collective-permute-start(bf16[224,512]{1,0:T(8,128)(2,1)S(1)} %get-tuple-element.66), channel_id=1, source_target_pairs={{0,16},{16,0},{1,17},{17,1},{2,18},{18,2},{3,19},{19,3},{4,20},{20... | collective-permute-start | bytes 688136 | tf_op jit(solution)/shard_map/ppermute | solution.py:46
  85.9 9.1 %collective-permute-start.31 = (bf16[224,512]{1,0:T(8,128)(2,1)S(1)}, bf16[224,512]{1,0:T(8,128)(2,1)S(1)}, u32[]{:S(2)}, u32[]{:S(2)}) collective-permute-start(bf16[224,512]{1,0:T(8,128)(2,1)S(1)} %get-tuple-element.62), channel_id=1, source_target_pairs={{0,16},{16,0},{1,17},{17,1},{2,18},{18,2},{3,19},{19,3},{4,20},{20... | collective-permute-start | bytes 688136 | tf_op jit(solution)/shard_map/ppermute | solution.py:46
  (10 other events, 109.2 us)

commit v3 on v2

--- a/solution.py
+++ b/solution.py
@@ -214,34 +214,44 @@
     )(near, far)
 
 
-def project_kernel(strip, column, total, tables_ref, rows_ref, *refs):
+def project_kernel(strip, column, total, begun, tables_ref, rows_ref, *refs):
     count = tables_ref.shape[2]
-    w_refs, gate_refs, out_refs = refs[:count], refs[count : count + 2], refs[count + 2 :]
+    w_refs, refs = refs[:count], refs[count:]
+    sum_ref, refs = (refs[0], refs[1:]) if begun else (None, refs)
     owner, slab = lax.axis_index("owner"), lax.axis_index("slab")
-    rows, width = out_refs[0].shape
+    width = w_refs[0].shape[1]
     sources = [tables_ref[slab, owner, index] for index in range(count)]
     place = lax.axis_index("groups") * total + column + (1 - slab if strip else slab) * width
     for first in range(0, width, 2 * LANES):
         tile = min(2 * LANES, width - first)
-        product = None
+        at = slice(first, first + tile)
+        product = sum_ref[:, at] if begun else None
         for source, w_ref in zip(sources, w_refs):
-            term = jnp.dot(rows_ref[source], w_ref[:, first : first + tile], preferred_element_type=jnp.float32)
+            term = jnp.dot(rows_ref[source], w_ref[:, at], preferred_element_type=jnp.float32)
             product = term if product is None else product + term
+        if len(refs) == 1:
+            refs[0][:, at] = product
+            continue
         here = pl.ds(pl.multiple_of(place + first, LANES), tile)
+        rows = refs[2].shape[0]
         for block in range(2):
-            gate = gate_refs[block][:, here]
+            gate = refs[block][:, here]
             result = product[block * rows : (block + 1) * rows] * gate
-            out_refs[block][:, first : first + tile] = result.astype(jnp.bfloat16)
-
-
-def project(table, arranged, chunks, gates, strip, column, total):
-    count, rows, depth = arranged.shape
-    width = chunks[0].shape[1]
+            refs[2 + block][:, at] = result.astype(jnp.bfloat16)
+
+
+def project(table, arranged, chunks, begun, gates, strip, column, total):
+    rows, depth = arranged.shape[1:]
+    count, width = len(chunks), chunks[0].shape[1]
+    begun = [] if begun is None else [begun]
+    out_shape = jax.ShapeDtypeStruct((rows, width), jnp.float32)
+    if gates:
+        out_shape = [jax.ShapeDtypeStruct((rows // 2, width), jnp.bfloat16)] * 2
     return pl.pallas_call(
-        functools.partial(project_kernel, strip, column, total),
-        out_shape=[jax.ShapeDtypeStruct((rows // 2, width), jnp.bfloat16)] * 2,
-        in_specs=[IN_SMEM] + [IN_VMEM] * (1 + count + 2),
-        out_specs=[IN_VMEM] * 2,
+        functools.partial(project_kernel, strip, column, total, bool(begun)),
+        out_shape=out_shape,
+        in_specs=[IN_SMEM] + [IN_VMEM] * (1 + count + len(begun) + len(gates)),
+        out_specs=[IN_VMEM] * 2 if gates else IN_VMEM,
         compiler_params=pltpu.CompilerParams(vmem_limit_bytes=16 * MIB),
         cost_estimate=pl.CostEstimate(
             flops=3 * rows * width * depth * count,
@@ -249,7 +259,7 @@
             transcendentals=0,
         ),
         name="project",
-    )(table, arranged, *chunks, *gates)
+    )(table, arranged, *chunks, *begun, *gates)
 
 
 def place_kernel(count, columns, total, *refs):
@@ -354,22 +364,34 @@
 
     arranged = arrange(*a_blocks, count)
 
-    def project_strip(piece, strip, *others):
-        chunks, sources = [], []
-        for turn in range(turns[strip] + 1):
-            chunks.append(held[piece, strip, turn])
-            sources.append((-turn, turn))
-        for turn in range(1, turns[1 - strip] + 1):
-            chunks.append(crossed[piece, 1 - strip, turn])
-            sources.append((turn, -turn))
-        table = np.zeros((slabs, count, len(chunks)), np.int32)
+    begun = {}
+
+    def project_strip(piece, strip, *others, final=True):
+        sources = [(-turn, turn) for turn in range(turns[strip] + 1)]
+        sources += [(turn, -turn) for turn in range(1, turns[1 - strip] + 1)]
+        late = {len(sources) - 1, turns[strip]} if strip == 0 else {len(sources) - 1}
+        batch = sorted(late if final else set(range(len(sources))) - late)
+        if final and (piece, strip) not in begun:
+            project_strip(piece, strip, final=False)
+        if not batch:
+            begun[piece, strip] = None
+            return None
+        chunks = [
+            held[piece, strip, index] if index <= turns[strip] else crossed[piece, 1 - strip, index - turns[strip]]
+            for index in batch
+        ]
+        table = np.zeros((slabs, count, len(batch)), np.int32)
         for slab in range(slabs):
             for owner in range(count):
-                table[slab, owner] = [order[(spot_of[owner] + source[slab]) % count] for source in sources]
+                table[slab, owner] = [order[(spot_of[owner] + sources[index][slab]) % count] for index in batch]
         if others:
             chunks[0] = after(chunks[0], *others)
-        own, away = project(jnp.asarray(table), arranged, chunks, gates, strip, firsts[piece], total)
-        return [own, swap(away, ("groups",))]
+        before, gates_here = (begun[piece, strip], gates) if final else (None, ())
+        result = project(jnp.asarray(table), arranged, chunks, before, gates_here, strip, firsts[piece], total)
+        if not final:
+            begun[piece, strip] = result
+            return result
+        return [result[0], swap(result[1], ("groups",))]
 
     results, needs = {}, {}
     if first_done >= 2 and first_done + 1 < len(hops):
@@ -388,6 +410,8 @@
         others = needs.get(slot - FLIGHT, [])
         cross(slot - FLIGHT, *(arrived[other] if isinstance(other, int) else other for other in others))
         hop(slot, *waits.get(slot, []))
+    if len(hops) > 2 * FLIGHT and len(widths) > 1:
+        needs[len(hops) - 1] = [project_strip(len(widths) - 1, strip, final=False) for strip in range(2)]
     for slot in range(max(len(hops) - FLIGHT, 0), len(hops)):
         cross(slot, *needs.get(slot, []))
     for piece in range(len(widths)):

time: 95.9 us -> 94.9 us (0.990)
  waiting for transfers between devices: 39.7 us -> 34 us
  Pallas kernels: 25.5 us -> 28.8 us
  starting transfers between devices: 30.4 us -> 31.6 us
    ppermute x14, starting transfers between devices: 18.2 us -> 22.8 us  [hop(): value = lax.ppermute(value, ('owner', 'slab'), ring)]
    pallas_call x4 -> x8, Pallas kernels: 12.7 us -> 16.1 us  [project(): pl.pallas_call(functools.partial(project_kernel, strip, column, total, bo...]
    ppermute x22, starting transfers between devices: 12.2 us -> 8.82 us  [swap(): return lax.ppermute(value, axes, [(i, count - 1 - i) for i in range(count)])]
    ppermute x14, waiting for transfers between devices: 22.5 us -> 19.4 us  [hop(): value = lax.ppermute(value, ('owner', 'slab'), ring)]
    ppermute x22, waiting for transfers between devices: 17.2 us -> 14.6 us  [swap(): return lax.ppermute(value, axes, [(i, count - 1 - i) for i in range(count)])]
  transfers between devices with their start and end apart: 36 -> 36, of which waited for: 14 -> 12; matrix products, arithmetic and copies ran while one was open for 0% -> 0% of each run, Pallas kernels for 24% -> 28%
where the time goes in v3:
time: 94.9 us; the launch traced here: 94.7 us
  waiting for transfers between devices  34 us (36%)
  starting transfers between devices  31.6 us (33%)
  Pallas kernels  28.8 us (30%)
    ppermute x14, starting transfers between devices, hop(): value = lax.ppermute(value, ('owner', 'slab'), ring)  22.8 us
    ppermute x14, waiting for transfers between devices, hop(): value = lax.ppermute(value, ('owner', 'slab'), ring)  19.4 us
    pallas_call x8, Pallas kernels, project(): pl.pallas_call(functools.partial(project_kernel, strip, column, total, bo...  16.1 us
    ppermute x22, waiting for transfers between devices, swap(): return lax.ppermute(value, axes, [(i, count - 1 - i) for i in range(count)])  14.6 us
    ppermute x22, starting transfers between devices, swap(): return lax.ppermute(value, axes, [(i, count - 1 - i) for i in range(count)])  8.82 us
    pallas_call x2, Pallas kernels, attend(): pl.pallas_call(functools.partial(attend_kernel, spots), grid=(steps,), ou...  6.73 us
    pallas_call x2, Pallas kernels, cut(): pl.pallas_call(functools.partial(cut_kernel, first, total, with_border),...  2.81 us
    pallas_call x2, Pallas kernels, place(): pl.pallas_call(functools.partial(place_kernel, len(blocks), columns, tota...  2.05 us
  transfers between devices with their start and end apart: 36, of which 12 were waited for; matrix products, arithmetic and copies ran while one was open for 0% of the time, Pallas kernels for 28%

profile of v3, /device:TPU:0, one launch (start us, length us, event | category | flops | bytes accessed | tf_op | source)
XLA Modules:
  0.0 94.7 jit_solution(14437444657905890540)
XLA Ops:
  0.0 1.7 %cut.2 = (bf16[320,768]{1,0:T(8,128)(2,1)S(1)}, bf16[320,768]{1,0:T(8,128)(2,1)S(1)}, bf16[2,1,112,1280]{3,2,1,0:T(8,128)(2,1)S(1)}, bf16[2,1,112,1280]{3,2,1,0:T(8,128)(2,1)S(1)}) custom-call(bf16[320,5120]{1,0:T(8,128)(2,1)} %weight_ref.3, bf16[2,1,2,112,2560]{4,3,2,1,0:T(8,128)(2,1)} %key_value_ref.3), custom_call_target="tpu_custom_call" | custom-call | bytes 1966080 | tf_op jit(solution)/shard_map/cut/pallas_call | solution.py:84
  2.3 2.9 %collective-permute-start.3 = (bf16[320,768]{1,0:T(8,128)(2,1)S(1)}, bf16[320,768]{1,0:T(8,128)(2,1)S(1)}, u32[]{:S(2)}, u32[]{:S(2)}) collective-permute-start(bf16[320,768]{1,0:T(8,128)(2,1)S(1)} %get-tuple-element.40.refs_0_), channel_id=1, source_target_pairs={{0,2},{1,5},{2,6},{3,1},{4,0},{5,9},{6,10},{7,3},{8,4},{9,13},{10,... | collective-permute-start | bytes 1474568 | tf_op jit(solution)/shard_map/ppermute | solution.py:341
  5.3 1.6 %collective-permute-start.6 = (bf16[320,768]{1,0:T(8,128)(2,1)S(1)}, bf16[320,768]{1,0:T(8,128)(2,1)S(1)}, u32[]{:S(2)}, u32[]{:S(2)}) collective-permute-start(bf16[320,768]{1,0:T(8,128)(2,1)S(1)} %get-tuple-element.43.refs_0_), channel_id=1, source_target_pairs={{0,2},{1,5},{2,6},{3,1},{4,0},{5,9},{6,10},{7,3},{8,4},{9,13},{10,... | collective-permute-start | bytes 1474568 | tf_op jit(solution)/shard_map/ppermute | solution.py:341
  6.9 3.4 %attend.2.refs_0_ = bf16[224,2560]{1,0:T(8,128)(2,1)S(1)} custom-call(s32[4,3]{1,0:T(4,128)S(1)} %copy-done.7, bf16[224,2560]{1,0:T(8,128)(2,1)} %bitcast.11, bf16[2,224,2560]{2,1,0:T(8,128)(2,1)S(1)} %bitcast.5, bf16[2,224,2560]{2,1,0:T(8,128)(2,1)S(1)} %bitcast.6, bf16[2,112,1280]{2,1,0:T(8,128)(2,1)S(1)} %collective-permute-done.1.k_halo_ref.v_halo_ref, ...), custom_call_target="tpu_custom_call" | custom-call | flops 3523215360 | bytes 3112960 | tf_op jit(solution)/shard_map/attend/pallas_call | solution.py:171
  10.2 3.4 %attend.3.near_ref = bf16[224,2560]{1,0:T(8,128)(2,1)S(1)} custom-call(s32[4,3]{1,0:T(4,128)S(1)} %copy-done.7, bf16[224,2560]{1,0:T(8,128)(2,1)} %bitcast.12, bf16[2,224,2560]{2,1,0:T(8,128)(2,1)S(1)} %bitcast.7, bf16[2,224,2560]{2,1,0:T(8,128)(2,1)S(1)} %bitcast.8, ...), custom_call_target="tpu_custom_call", output_to_operand_aliasing={{}: (6, {})} | custom-call | flops 3523215360 | bytes 3112960 | tf_op jit(solution)/shard_map/attend/pallas_call | solution.py:171
  13.6 1.6 %collective-permute-start.2 = (bf16[224,2560]{1,0:T(8,128)(2,1)S(1)}, bf16[224,2560]{1,0:T(8,128)(2,1)S(1)}, u32[]{:S(2)}, u32[]{:S(2)}) collective-permute-start(bf16[224,2560]{1,0:T(8,128)(2,1)S(1)} %attend.3.near_ref), channel_id=1, source_target_pairs={{0,16},{16,0},{1,17},{17,1},{2,18},{18,2},{3,19},{19,3},{4,20},{20... | collective-permute-start | bytes 3440648 | tf_op jit(solution)/shard_map/ppermute | solution.py:46
  15.2 1.6 %collective-permute-start.4 = (bf16[320,768]{1,0:T(8,128)(2,1)S(1)}, bf16[320,768]{1,0:T(8,128)(2,1)S(1)}, u32[]{:S(2)}, u32[]{:S(2)}) collective-permute-start(bf16[320,768]{1,0:T(8,128)(2,1)S(1)} %collective-permute-done.3.refs_1_), channel_id=1, source_target_pairs={{0,2},{1,5},{2,6},{3,1},{4,0},{5,9},{6,10},{7,3},{8,4},{9,13},{10,... | collective-permute-start | bytes 1474568 | tf_op jit(solution)/shard_map/ppermute | solution.py:341
  17.4 2.0 %collective-permute-start.9 = (bf16[320,768]{1,0:T(8,128)(2,1)S(1)}, bf16[320,768]{1,0:T(8,128)(2,1)S(1)}, u32[]{:S(2)}, u32[]{:S(2)}) collective-permute-start(bf16[320,768]{1,0:T(8,128)(2,1)S(1)} %collective-permute-done.6.refs_1_), channel_id=1, source_target_pairs={{0,2},{1,5},{2,6},{3,1},{4,0},{5,9},{6,10},{7,3},{8,4},{9,13},{10,... | collective-permute-start | bytes 1474568 | tf_op jit(solution)/shard_map/ppermute | solution.py:341
  21.0 3.0 %collective-permute-done.4.refs_2_ = bf16[320,768]{1,0:T(8,128)(2,1)S(1)} collective-permute-done((bf16[320,768]{1,0:T(8,128)(2,1)S(1)}, bf16[320,768]{1,0:T(8,128)(2,1)S(1)}, u32[]{:S(2)}, u32[]{:S(2)}) %collective-permute-start.4) | collective-permute-done | bytes 491552 | tf_op jit(solution)/shard_map/ppermute | solution.py:341
  24.0 1.6 %collective-permute-start.5 = (bf16[320,768]{1,0:T(8,128)(2,1)S(1)}, bf16[320,768]{1,0:T(8,128)(2,1)S(1)}, u32[]{:S(2)}, u32[]{:S(2)}) collective-permute-start(bf16[320,768]{1,0:T(8,128)(2,1)S(1)} %collective-permute-done.4.refs_2_), channel_id=1, source_target_pairs={{0,2},{1,5},{2,6},{3,1},{4,0},{5,9},{6,10},{7,3},{8,4},{9,13},{10,... | collective-permute-start | bytes 1474568 | tf_op jit(solution)/shard_map/ppermute | solution.py:341
  25.6 3.7 %collective-permute-done.9.refs_2_ = bf16[320,768]{1,0:T(8,128)(2,1)S(1)} collective-permute-done((bf16[320,768]{1,0:T(8,128)(2,1)S(1)}, bf16[320,768]{1,0:T(8,128)(2,1)S(1)}, u32[]{:S(2)}, u32[]{:S(2)}) %collective-permute-start.9) | collective-permute-done | bytes 491552 | tf_op jit(solution)/shard_map/ppermute | solution.py:341
  29.3 1.6 %collective-permute-start.11 = (bf16[320,768]{1,0:T(8,128)(2,1)S(1)}, bf16[320,768]{1,0:T(8,128)(2,1)S(1)}, u32[]{:S(2)}, u32[]{:S(2)}) collective-permute-start(bf16[320,768]{1,0:T(8,128)(2,1)S(1)} %collective-permute-done.9.refs_2_), channel_id=1, source_target_pairs={{0,2},{1,5},{2,6},{3,1},{4,0},{5,9},{6,10},{7,3},{8,4},{9,13},{10,... | collective-permute-start | bytes 1474568 | tf_op jit(solution)/shard_map/ppermute | solution.py:341
  30.9 3.7 %collective-permute-done.5.refs_3_ = bf16[320,768]{1,0:T(8,128)(2,1)S(1)} collective-permute-done((bf16[320,768]{1,0:T(8,128)(2,1)S(1)}, bf16[320,768]{1,0:T(8,128)(2,1)S(1)}, u32[]{:S(2)}, u32[]{:S(2)}) %collective-permute-start.5) | collective-permute-done | bytes 491552 | tf_op jit(solution)/shard_map/ppermute | solution.py:341
  34.6 1.6 %collective-permute-start.8 = (bf16[320,512]{1,0:T(8,128)(2,1)S(1)}, bf16[320,512]{1,0:T(8,128)(2,1)S(1)}, u32[]{:S(2)}, u32[]{:S(2)}) collective-permute-start(bf16[320,512]{1,0:T(8,128)(2,1)S(1)} %get-tuple-element.44.refs_0_), channel_id=1, source_target_pairs={{0,2},{1,5},{2,6},{3,1},{4,0},{5,9},{6,10},{7,3},{8,4},{9,13},{10,... | collective-permute-start | bytes 983048 | tf_op jit(solution)/shard_map/ppermute | solution.py:341
  36.1 3.7 %collective-permute-done.11.refs_3_ = bf16[320,768]{1,0:T(8,128)(2,1)S(1)} collective-permute-done((bf16[320,768]{1,0:T(8,128)(2,1)S(1)}, bf16[320,768]{1,0:T(8,128)(2,1)S(1)}, u32[]{:S(2)}, u32[]{:S(2)}) %collective-permute-start.11) | collective-permute-done | bytes 491552 | tf_op jit(solution)/shard_map/ppermute | solution.py:341
  43.7 2.3 %collective-permute-done.20.refs_4_.refs_3_ = f32[1,5120]{1,0:T(1,128)S(1)} collective-permute-done((f32[1,5120]{1,0:T(1,128)S(1)}, f32[1,5120]{1,0:T(1,128)S(1)}, u32[]{:S(2)}, u32[]{:S(2)}) %collective-permute-start.20) | collective-permute-done | bytes 20512 | tf_op jit(solution)/shard_map/ppermute | solution.py:46
  45.9 1.6 %collective-permute-start.19 = (bf16[320,512]{1,0:T(8,128)(2,1)S(1)}, bf16[320,512]{1,0:T(8,128)(2,1)S(1)}, u32[]{:S(2)}, u32[]{:S(2)}) collective-permute-start(bf16[320,512]{1,0:T(8,128)(2,1)S(1)} %get-tuple-element.51.refs_0_), channel_id=1, source_target_pairs={{0,2},{1,5},{2,6},{3,1},{4,0},{5,9},{6,10},{7,3},{8,4},{9,13},{10,... | collective-permute-start | bytes 983048 | tf_op jit(solution)/shard_map/ppermute | solution.py:341
  47.6 1.7 %collective-permute-done.13.refs_0_ = bf16[320,768]{1,0:T(8,128)(2,1)S(1)} collective-permute-done((bf16[320,768]{1,0:T(8,128)(2,1)S(1)}, bf16[320,768]{1,0:T(8,128)(2,1)S(1)}, u32[]{:S(2)}, u32[]{:S(2)}) %collective-permute-start.13) | collective-permute-done | bytes 491552 | tf_op jit(solution)/shard_map/ppermute | solution.py:341
  50.3 3.0 %project.8.refs_2_ = f32[448,768]{1,0:T(8,128)S(1)} custom-call(s32[2,8,6]{2,1,0:T(8,128)S(1)} %copy-done.5, bf16[8,448,320]{2,1,0:T(8,128)(2,1)S(1)} %arrange.1.rows_ref, bf16[320,768]{1,0:T(8,128)(2,1)S(1)} %get-tuple-element.40.refs_0_, bf16[320,768]{1,0:T(8,128)(2,1)S(1)} %collective-permute-done.3.refs_1_, ...), custom_call_target="tpu_custom_call" | custom-call | flops 1981808640 | bytes 5357568 | tf_op jit(solution)/shard_map/project/pallas_call | solution.py:250
  53.3 1.6 %project.9 = (bf16[224,768]{1,0:T(8,128)(2,1)S(1)}, bf16[224,768]{1,0:T(8,128)(2,1)S(1)}) custom-call(s32[2,8,2]{2,1,0:T(8,128)S(1)} %copy-done.3, bf16[8,448,320]{2,1,0:T(8,128)(2,1)S(1)} %arrange.1.rows_ref, bf16[320,768]{1,0:T(8,128)(2,1)S(1)} %collective-permute-done.13.refs_0_, bf16[320,768]{1,0:T(8,128)(2,1)S(1)} %collective-permute-done.21.refs_1_, ...), custom_call_target="tpu_custom_call" | custom-call | flops 660602880 | bytes 2244608 | tf_op jit(solution)/shard_map/project/pallas_call | solution.py:250
  54.9 1.6 %collective-permute-start.24 = (bf16[320,512]{1,0:T(8,128)(2,1)S(1)}, bf16[320,512]{1,0:T(8,128)(2,1)S(1)}, u32[]{:S(2)}, u32[]{:S(2)}) collective-permute-start(bf16[320,512]{1,0:T(8,128)(2,1)S(1)} %collective-permute-done.19.refs_1_), channel_id=1, source_target_pairs={{0,2},{1,5},{2,6},{3,1},{4,0},{5,9},{6,10},{7,3},{8,4},{9,13},{10,... | collective-permute-start | bytes 983048 | tf_op jit(solution)/shard_map/ppermute | solution.py:341
  57.4 1.6 %collective-permute-start.17 = (bf16[320,512]{1,0:T(8,128)(2,1)S(1)}, bf16[320,512]{1,0:T(8,128)(2,1)S(1)}, u32[]{:S(2)}, u32[]{:S(2)}) collective-permute-start(bf16[320,512]{1,0:T(8,128)(2,1)S(1)} %collective-permute-done.15.refs_2_), channel_id=1, source_target_pairs={{0,2},{1,5},{2,6},{3,1},{4,0},{5,9},{6,10},{7,3},{8,4},{9,13},{10,... | collective-permute-start | bytes 983048 | tf_op jit(solution)/shard_map/ppermute | solution.py:341
  59.0 3.0 %collective-permute-done.24.refs_2_ = bf16[320,512]{1,0:T(8,128)(2,1)S(1)} collective-permute-done((bf16[320,512]{1,0:T(8,128)(2,1)S(1)}, bf16[320,512]{1,0:T(8,128)(2,1)S(1)}, u32[]{:S(2)}, u32[]{:S(2)}) %collective-permute-start.24) | collective-permute-done | bytes 327712 | tf_op jit(solution)/shard_map/ppermute | solution.py:341
  62.0 3.3 %project.11.refs_1_ = f32[448,768]{1,0:T(8,128)S(1)} custom-call(s32[2,8,7]{2,1,0:T(8,128)S(1)} %copy-done.4, bf16[8,448,320]{2,1,0:T(8,128)(2,1)S(1)} %arrange.1.rows_ref, bf16[320,768]{1,0:T(8,128)(2,1)S(1)} %get-tuple-element.43.refs_0_, bf16[320,768]{1,0:T(8,128)(2,1)S(1)} %collective-permute-done.6.refs_1_, ...), custom_call_target="tpu_custom_call" | custom-call | flops 2312110080 | bytes 6135808 | tf_op jit(solution)/shard_map/project/pallas_call | solution.py:250
  67.5 1.6 %collective-permute-start.28 = (bf16[320,512]{1,0:T(8,128)(2,1)S(1)}, bf16[320,512]{1,0:T(8,128)(2,1)S(1)}, u32[]{:S(2)}, u32[]{:S(2)}) collective-permute-start(bf16[320,512]{1,0:T(8,128)(2,1)S(1)} %collective-permute-done.24.refs_2_), channel_id=1, source_target_pairs={{0,2},{1,5},{2,6},{3,1},{4,0},{5,9},{6,10},{7,3},{8,4},{9,13},{10,... | collective-permute-start | bytes 983048 | tf_op jit(solution)/shard_map/ppermute | solution.py:341
  69.6 1.6 %collective-permute-start.23 = (bf16[320,512]{1,0:T(8,128)(2,1)S(1)}, bf16[320,512]{1,0:T(8,128)(2,1)S(1)}, u32[]{:S(2)}, u32[]{:S(2)}) collective-permute-start(bf16[320,512]{1,0:T(8,128)(2,1)S(1)} %collective-permute-done.17.refs_3_), channel_id=1, source_target_pairs={{0,2},{1,5},{2,6},{3,1},{4,0},{5,9},{6,10},{7,3},{8,4},{9,13},{10,... | collective-permute-start | bytes 983048 | tf_op jit(solution)/shard_map/ppermute | solution.py:341
  71.2 2.2 %project.10.refs_2_ = f32[448,512]{1,0:T(8,128)S(1)} custom-call(s32[2,8,6]{2,1,0:T(8,128)S(1)} %copy-done.5, bf16[8,448,320]{2,1,0:T(8,128)(2,1)S(1)} %arrange.1.rows_ref, bf16[320,512]{1,0:T(8,128)(2,1)S(1)} %get-tuple-element.44.refs_0_, bf16[320,512]{1,0:T(8,128)(2,1)S(1)} %collective-permute-done.8.refs_1_, ...), custom_call_target="tpu_custom_call" | custom-call | flops 1321205760 | bytes 4145152 | tf_op jit(solution)/shard_map/project/pallas_call | solution.py:250
  73.4 3.7 %collective-permute-done.33.refs_3_ = bf16[224,768]{1,0:T(8,128)(2,1)S(1)} collective-permute-done((bf16[224,768]{1,0:T(8,128)(2,1)S(1)}, bf16[224,768]{1,0:T(8,128)(2,1)S(1)}, u32[]{:S(2)}, u32[]{:S(2)}) %collective-permute-start.33) | collective-permute-done | bytes 344096 | tf_op jit(solution)/shard_map/ppermute | solution.py:46
  77.1 2.5 %project.13.refs_1_ = f32[448,512]{1,0:T(8,128)S(1)} custom-call(s32[2,8,7]{2,1,0:T(8,128)S(1)} %copy-done.4, bf16[8,448,320]{2,1,0:T(8,128)(2,1)S(1)} %arrange.1.rows_ref, bf16[320,512]{1,0:T(8,128)(2,1)S(1)} %get-tuple-element.51.refs_0_, bf16[320,512]{1,0:T(8,128)(2,1)S(1)} %collective-permute-done.19.refs_1_, ...), custom_call_target="tpu_custom_call" | custom-call | flops 1541406720 | bytes 4759552 | tf_op jit(solution)/shard_map/project/pallas_call | solution.py:250
  80.1 1.3 %project.15 = (bf16[224,512]{1,0:T(8,128)(2,1)S(1)}, bf16[224,512]{1,0:T(8,128)(2,1)S(1)}) custom-call(s32[2,8,2]{2,1,0:T(8,128)S(1)} %copy-done.3, bf16[8,448,320]{2,1,0:T(8,128)(2,1)S(1)} %arrange.1.rows_ref, bf16[320,512]{1,0:T(8,128)(2,1)S(1)} %collective-permute-done.23.refs_0_, bf16[320,512]{1,0:T(8,128)(2,1)S(1)} %collective-permute-done.34.refs_1_, ...), custom_call_target="tpu_custom_call" | custom-call | flops 440401920 | bytes 1687552 | tf_op jit(solution)/shard_map/project/pallas_call | solution.py:250
  84.7 5.3 %collective-permute-done.35.refs_5_ = bf16[224,512]{1,0:T(8,128)(2,1)S(1)} collective-permute-done((bf16[224,512]{1,0:T(8,128)(2,1)S(1)}, bf16[224,512]{1,0:T(8,128)(2,1)S(1)}, u32[]{:S(2)}, u32[]{:S(2)}) %collective-permute-start.35) | collective-permute-done | bytes 229408 | tf_op jit(solution)/shard_map/ppermute | solution.py:46
  91.3 2.7 %collective-permute-done.32.refs_1_ = bf16[224,512]{1,0:T(8,128)(2,1)S(1)} collective-permute-done((bf16[224,512]{1,0:T(8,128)(2,1)S(1)}, bf16[224,512]{1,0:T(8,128)(2,1)S(1)}, u32[]{:S(2)}, u32[]{:S(2)}) %collective-permute-start.32) | collective-permute-done | bytes 229408 | tf_op jit(solution)/shard_map/ppermute | solution.py:46
  (72 shorter events, 17.2 us)
Async XLA Ops:
  2.3 8.0 %collective-permute-start = (bf16[2,112,1280]{2,1,0:T(8,128)(2,1)S(1)}, bf16[2,112,1280]{2,1,0:T(8,128)(2,1)S(1)}, u32[]{:S(2)}, u32[]{:S(2)}) collective-permute-start(bf16[2,112,1280]{2,1,0:T(8,128)(2,1)S(1)} %bitcast.9), channel_id=1, source_target_pairs={{0,1},{1,0},{2,3},{3,2},{4,5},{5,4},{6,7},{7,6},{8,9},{9,8},{10,11... | collective-permute-start | bytes 1720328 | tf_op jit(solution)/shard_map/ppermute | solution.py:46
  2.3 12.9 %collective-permute-start.3 = (bf16[320,768]{1,0:T(8,128)(2,1)S(1)}, bf16[320,768]{1,0:T(8,128)(2,1)S(1)}, u32[]{:S(2)}, u32[]{:S(2)}) collective-permute-start(bf16[320,768]{1,0:T(8,128)(2,1)S(1)} %get-tuple-element.40.refs_0_), channel_id=1, source_target_pairs={{0,2},{1,5},{2,6},{3,1},{4,0},{5,9},{6,10},{7,3},{8,4},{9,13},{10,... | collective-permute-start | bytes 1474568 | tf_op jit(solution)/shard_map/ppermute | solution.py:341
  5.3 12.1 %collective-permute-start.6 = (bf16[320,768]{1,0:T(8,128)(2,1)S(1)}, bf16[320,768]{1,0:T(8,128)(2,1)S(1)}, u32[]{:S(2)}, u32[]{:S(2)}) collective-permute-start(bf16[320,768]{1,0:T(8,128)(2,1)S(1)} %get-tuple-element.43.refs_0_), channel_id=1, source_target_pairs={{0,2},{1,5},{2,6},{3,1},{4,0},{5,9},{6,10},{7,3},{8,4},{9,13},{10,... | collective-permute-start | bytes 1474568 | tf_op jit(solution)/shard_map/ppermute | solution.py:341
  13.6 26.8 %collective-permute-start.2 = (bf16[224,2560]{1,0:T(8,128)(2,1)S(1)}, bf16[224,2560]{1,0:T(8,128)(2,1)S(1)}, u32[]{:S(2)}, u32[]{:S(2)}) collective-permute-start(bf16[224,2560]{1,0:T(8,128)(2,1)S(1)} %attend.3.near_ref), channel_id=1, source_target_pairs={{0,16},{16,0},{1,17},{17,1},{2,18},{18,2},{3,19},{19,3},{4,20},{20... | collective-permute-start | bytes 3440648 | tf_op jit(solution)/shard_map/ppermute | solution.py:46
  15.2 8.8 %collective-permute-start.4 = (bf16[320,768]{1,0:T(8,128)(2,1)S(1)}, bf16[320,768]{1,0:T(8,128)(2,1)S(1)}, u32[]{:S(2)}, u32[]{:S(2)}) collective-permute-start(bf16[320,768]{1,0:T(8,128)(2,1)S(1)} %collective-permute-done.3.refs_1_), channel_id=1, source_target_pairs={{0,2},{1,5},{2,6},{3,1},{4,0},{5,9},{6,10},{7,3},{8,4},{9,13},{10,... | collective-permute-start | bytes 1474568 | tf_op jit(solution)/shard_map/ppermute | solution.py:341
  17.4 11.9 %collective-permute-start.9 = (bf16[320,768]{1,0:T(8,128)(2,1)S(1)}, bf16[320,768]{1,0:T(8,128)(2,1)S(1)}, u32[]{:S(2)}, u32[]{:S(2)}) collective-permute-start(bf16[320,768]{1,0:T(8,128)(2,1)S(1)} %collective-permute-done.6.refs_1_), channel_id=1, source_target_pairs={{0,2},{1,5},{2,6},{3,1},{4,0},{5,9},{6,10},{7,3},{8,4},{9,13},{10,... | collective-permute-start | bytes 1474568 | tf_op jit(solution)/shard_map/ppermute | solution.py:341
  19.4 9.9 %collective-permute-start.10 = (bf16[320,768]{1,0:T(8,128)(2,1)S(1)}, bf16[320,768]{1,0:T(8,128)(2,1)S(1)}, u32[]{:S(2)}, u32[]{:S(2)}) collective-permute-start(bf16[320,768]{1,0:T(8,128)(2,1)S(1)} %collective-permute-done.3.refs_1_), channel_id=1, source_target_pairs={{0,1},{1,0},{2,3},{3,2},{4,5},{5,4},{6,7},{7,6},{8,9},{9,8},{10,11... | collective-permute-start | bytes 1474568 | tf_op jit(solution)/shard_map/ppermute | solution.py:46
  20.5 10.4 %collective-permute-start.7 = (bf16[320,768]{1,0:T(8,128)(2,1)S(1)}, bf16[320,768]{1,0:T(8,128)(2,1)S(1)}, u32[]{:S(2)}, u32[]{:S(2)}) collective-permute-start(bf16[320,768]{1,0:T(8,128)(2,1)S(1)} %collective-permute-done.6.refs_1_), channel_id=1, source_target_pairs={{0,1},{1,0},{2,3},{3,2},{4,5},{5,4},{6,7},{7,6},{8,9},{9,8},{10,11... | collective-permute-start | bytes 1474568 | tf_op jit(solution)/shard_map/ppermute | solution.py:46
  24.0 10.5 %collective-permute-start.5 = (bf16[320,768]{1,0:T(8,128)(2,1)S(1)}, bf16[320,768]{1,0:T(8,128)(2,1)S(1)}, u32[]{:S(2)}, u32[]{:S(2)}) collective-permute-start(bf16[320,768]{1,0:T(8,128)(2,1)S(1)} %collective-permute-done.4.refs_2_), channel_id=1, source_target_pairs={{0,2},{1,5},{2,6},{3,1},{4,0},{5,9},{6,10},{7,3},{8,4},{9,13},{10,... | collective-permute-start | bytes 1474568 | tf_op jit(solution)/shard_map/ppermute | solution.py:341
  29.3 10.5 %collective-permute-start.11 = (bf16[320,768]{1,0:T(8,128)(2,1)S(1)}, bf16[320,768]{1,0:T(8,128)(2,1)S(1)}, u32[]{:S(2)}, u32[]{:S(2)}) collective-permute-start(bf16[320,768]{1,0:T(8,128)(2,1)S(1)} %collective-permute-done.9.refs_2_), channel_id=1, source_target_pairs={{0,2},{1,5},{2,6},{3,1},{4,0},{5,9},{6,10},{7,3},{8,4},{9,13},{10,... | collective-permute-start | bytes 1474568 | tf_op jit(solution)/shard_map/ppermute | solution.py:341
  30.9 9.0 %collective-permute-start.12 = (bf16[320,768]{1,0:T(8,128)(2,1)S(1)}, bf16[320,768]{1,0:T(8,128)(2,1)S(1)}, u32[]{:S(2)}, u32[]{:S(2)}) collective-permute-start(bf16[320,768]{1,0:T(8,128)(2,1)S(1)} %collective-permute-done.4.refs_2_), channel_id=1, source_target_pairs={{0,1},{1,0},{2,3},{3,2},{4,5},{5,4},{6,7},{7,6},{8,9},{9,8},{10,11... | collective-permute-start | bytes 1474568 | tf_op jit(solution)/shard_map/ppermute | solution.py:46
  34.6 11.4 %collective-permute-start.8 = (bf16[320,512]{1,0:T(8,128)(2,1)S(1)}, bf16[320,512]{1,0:T(8,128)(2,1)S(1)}, u32[]{:S(2)}, u32[]{:S(2)}) collective-permute-start(bf16[320,512]{1,0:T(8,128)(2,1)S(1)} %get-tuple-element.44.refs_0_), channel_id=1, source_target_pairs={{0,2},{1,5},{2,6},{3,1},{4,0},{5,9},{6,10},{7,3},{8,4},{9,13},{10,... | collective-permute-start | bytes 983048 | tf_op jit(solution)/shard_map/ppermute | solution.py:341
  36.1 9.8 %collective-permute-start.18 = (bf16[320,768]{1,0:T(8,128)(2,1)S(1)}, bf16[320,768]{1,0:T(8,128)(2,1)S(1)}, u32[]{:S(2)}, u32[]{:S(2)}) collective-permute-start(bf16[320,768]{1,0:T(8,128)(2,1)S(1)} %collective-permute-done.9.refs_2_), channel_id=1, source_target_pairs={{0,1},{1,0},{2,3},{3,2},{4,5},{5,4},{6,7},{7,6},{8,9},{9,8},{10,11... | collective-permute-start | bytes 1474568 | tf_op jit(solution)/shard_map/ppermute | solution.py:46
  39.8 7.7 %collective-permute-start.14 = (bf16[320,768]{1,0:T(8,128)(2,1)S(1)}, bf16[320,768]{1,0:T(8,128)(2,1)S(1)}, u32[]{:S(2)}, u32[]{:S(2)}) collective-permute-start(bf16[320,768]{1,0:T(8,128)(2,1)S(1)} %collective-permute-done.5.refs_3_), channel_id=1, source_target_pairs={{0,1},{1,0},{2,3},{3,2},{4,5},{5,4},{6,7},{7,6},{8,9},{9,8},{10,11... | collective-permute-start | bytes 1474568 | tf_op jit(solution)/shard_map/ppermute | solution.py:46
  40.5 8.8 %collective-permute-start.13 = (bf16[320,768]{1,0:T(8,128)(2,1)S(1)}, bf16[320,768]{1,0:T(8,128)(2,1)S(1)}, u32[]{:S(2)}, u32[]{:S(2)}) collective-permute-start(bf16[320,768]{1,0:T(8,128)(2,1)S(1)} %collective-permute-done.5.refs_3_), channel_id=1, source_target_pairs={{0,2},{1,5},{2,6},{3,1},{4,0},{5,9},{6,10},{7,3},{8,4},{9,13},{10,... | collective-permute-start | bytes 1474568 | tf_op jit(solution)/shard_map/ppermute | solution.py:341
  45.9 7.4 %collective-permute-start.21 = (bf16[320,768]{1,0:T(8,128)(2,1)S(1)}, bf16[320,768]{1,0:T(8,128)(2,1)S(1)}, u32[]{:S(2)}, u32[]{:S(2)}) collective-permute-start(bf16[320,768]{1,0:T(8,128)(2,1)S(1)} %collective-permute-done.11.refs_3_), channel_id=1, source_target_pairs={{0,1},{1,0},{2,3},{3,2},{4,5},{5,4},{6,7},{7,6},{8,9},{9,8},{10,11... | collective-permute-start | bytes 1474568 | tf_op jit(solution)/shard_map/ppermute | solution.py:46
  45.9 8.9 %collective-permute-start.19 = (bf16[320,512]{1,0:T(8,128)(2,1)S(1)}, bf16[320,512]{1,0:T(8,128)(2,1)S(1)}, u32[]{:S(2)}, u32[]{:S(2)}) collective-permute-start(bf16[320,512]{1,0:T(8,128)(2,1)S(1)} %get-tuple-element.51.refs_0_), channel_id=1, source_target_pairs={{0,2},{1,5},{2,6},{3,1},{4,0},{5,9},{6,10},{7,3},{8,4},{9,13},{10,... | collective-permute-start | bytes 983048 | tf_op jit(solution)/shard_map/ppermute | solution.py:341
  47.6 9.8 %collective-permute-start.16 = (bf16[320,512]{1,0:T(8,128)(2,1)S(1)}, bf16[320,512]{1,0:T(8,128)(2,1)S(1)}, u32[]{:S(2)}, u32[]{:S(2)}) collective-permute-start(bf16[320,512]{1,0:T(8,128)(2,1)S(1)} %collective-permute-done.8.refs_1_), channel_id=1, source_target_pairs={{0,1},{1,0},{2,3},{3,2},{4,5},{5,4},{6,7},{7,6},{8,9},{9,8},{10,11... | collective-permute-start | bytes 983048 | tf_op jit(solution)/shard_map/ppermute | solution.py:46
  49.3 8.1 %collective-permute-start.15 = (bf16[320,512]{1,0:T(8,128)(2,1)S(1)}, bf16[320,512]{1,0:T(8,128)(2,1)S(1)}, u32[]{:S(2)}, u32[]{:S(2)}) collective-permute-start(bf16[320,512]{1,0:T(8,128)(2,1)S(1)} %collective-permute-done.8.refs_1_), channel_id=1, source_target_pairs={{0,2},{1,5},{2,6},{3,1},{4,0},{5,9},{6,10},{7,3},{8,4},{9,13},{10,... | collective-permute-start | bytes 983048 | tf_op jit(solution)/shard_map/ppermute | solution.py:341
  54.9 7.1 %collective-permute-start.24 = (bf16[320,512]{1,0:T(8,128)(2,1)S(1)}, bf16[320,512]{1,0:T(8,128)(2,1)S(1)}, u32[]{:S(2)}, u32[]{:S(2)}) collective-permute-start(bf16[320,512]{1,0:T(8,128)(2,1)S(1)} %collective-permute-done.19.refs_1_), channel_id=1, source_target_pairs={{0,2},{1,5},{2,6},{3,1},{4,0},{5,9},{6,10},{7,3},{8,4},{9,13},{10,... | collective-permute-start | bytes 983048 | tf_op jit(solution)/shard_map/ppermute | solution.py:341
  56.5 8.8 %collective-permute-start.27 = (bf16[320,768]{1,0:T(8,128)(2,1)S(1)}, bf16[320,768]{1,0:T(8,128)(2,1)S(1)}, u32[]{:S(2)}, u32[]{:S(2)}) collective-permute-start(bf16[320,768]{1,0:T(8,128)(2,1)S(1)} %collective-permute-done.13.refs_0_), channel_id=1, source_target_pairs={{0,1},{1,0},{2,3},{3,2},{4,5},{5,4},{6,7},{7,6},{8,9},{9,8},{10,11... | collective-permute-start | bytes 1474568 | tf_op jit(solution)/shard_map/ppermute | solution.py:46
  56.5 11.0 %collective-permute-start.26 = (bf16[224,768]{1,0:T(8,128)(2,1)S(1)}, bf16[224,768]{1,0:T(8,128)(2,1)S(1)}, u32[]{:S(2)}, u32[]{:S(2)}) collective-permute-start(bf16[224,768]{1,0:T(8,128)(2,1)S(1)} %get-tuple-element.58), channel_id=1, source_target_pairs={{0,16},{16,0},{1,17},{17,1},{2,18},{18,2},{3,19},{19,3},{4,20},{20... | collective-permute-start | bytes 1032200 | tf_op jit(solution)/shard_map/ppermute | solution.py:46
  57.4 10.1 %collective-permute-start.17 = (bf16[320,512]{1,0:T(8,128)(2,1)S(1)}, bf16[320,512]{1,0:T(8,128)(2,1)S(1)}, u32[]{:S(2)}, u32[]{:S(2)}) collective-permute-start(bf16[320,512]{1,0:T(8,128)(2,1)S(1)} %collective-permute-done.15.refs_2_), channel_id=1, source_target_pairs={{0,2},{1,5},{2,6},{3,1},{4,0},{5,9},{6,10},{7,3},{8,4},{9,13},{10,... | collective-permute-start | bytes 983048 | tf_op jit(solution)/shard_map/ppermute | solution.py:341
  59.0 10.1 %collective-permute-start.22 = (bf16[320,512]{1,0:T(8,128)(2,1)S(1)}, bf16[320,512]{1,0:T(8,128)(2,1)S(1)}, u32[]{:S(2)}, u32[]{:S(2)}) collective-permute-start(bf16[320,512]{1,0:T(8,128)(2,1)S(1)} %collective-permute-done.19.refs_1_), channel_id=1, source_target_pairs={{0,1},{1,0},{2,3},{3,2},{4,5},{5,4},{6,7},{7,6},{8,9},{9,8},{10,11... | collective-permute-start | bytes 983048 | tf_op jit(solution)/shard_map/ppermute | solution.py:46
  62.0 7.6 %collective-permute-start.25 = (bf16[320,512]{1,0:T(8,128)(2,1)S(1)}, bf16[320,512]{1,0:T(8,128)(2,1)S(1)}, u32[]{:S(2)}, u32[]{:S(2)}) collective-permute-start(bf16[320,512]{1,0:T(8,128)(2,1)S(1)} %collective-permute-done.24.refs_2_), channel_id=1, source_target_pairs={{0,1},{1,0},{2,3},{3,2},{4,5},{5,4},{6,7},{7,6},{8,9},{9,8},{10,11... | collective-permute-start | bytes 983048 | tf_op jit(solution)/shard_map/ppermute | solution.py:46
  66.5 10.5 %collective-permute-start.33 = (bf16[224,768]{1,0:T(8,128)(2,1)S(1)}, bf16[224,768]{1,0:T(8,128)(2,1)S(1)}, u32[]{:S(2)}, u32[]{:S(2)}) collective-permute-start(bf16[224,768]{1,0:T(8,128)(2,1)S(1)} %get-tuple-element.65), channel_id=1, source_target_pairs={{0,16},{16,0},{1,17},{17,1},{2,18},{18,2},{3,19},{19,3},{4,20},{20... | collective-permute-start | bytes 1032200 | tf_op jit(solution)/shard_map/ppermute | solution.py:46
  67.5 9.6 %collective-permute-start.28 = (bf16[320,512]{1,0:T(8,128)(2,1)S(1)}, bf16[320,512]{1,0:T(8,128)(2,1)S(1)}, u32[]{:S(2)}, u32[]{:S(2)}) collective-permute-start(bf16[320,512]{1,0:T(8,128)(2,1)S(1)} %collective-permute-done.24.refs_2_), channel_id=1, source_target_pairs={{0,2},{1,5},{2,6},{3,1},{4,0},{5,9},{6,10},{7,3},{8,4},{9,13},{10,... | collective-permute-start | bytes 983048 | tf_op jit(solution)/shard_map/ppermute | solution.py:341
  69.1 8.0 %collective-permute-start.29 = (bf16[320,512]{1,0:T(8,128)(2,1)S(1)}, bf16[320,512]{1,0:T(8,128)(2,1)S(1)}, u32[]{:S(2)}, u32[]{:S(2)}) collective-permute-start(bf16[320,512]{1,0:T(8,128)(2,1)S(1)} %collective-permute-done.15.refs_2_), channel_id=1, source_target_pairs={{0,1},{1,0},{2,3},{3,2},{4,5},{5,4},{6,7},{7,6},{8,9},{9,8},{10,11... | collective-permute-start | bytes 983048 | tf_op jit(solution)/shard_map/ppermute | solution.py:46
  69.1 8.0 %collective-permute-start.30 = (bf16[320,512]{1,0:T(8,128)(2,1)S(1)}, bf16[320,512]{1,0:T(8,128)(2,1)S(1)}, u32[]{:S(2)}, u32[]{:S(2)}) collective-permute-start(bf16[320,512]{1,0:T(8,128)(2,1)S(1)} %collective-permute-done.17.refs_3_), channel_id=1, source_target_pairs={{0,1},{1,0},{2,3},{3,2},{4,5},{5,4},{6,7},{7,6},{8,9},{9,8},{10,11... | collective-permute-start | bytes 983048 | tf_op jit(solution)/shard_map/ppermute | solution.py:46
  69.6 10.0 %collective-permute-start.23 = (bf16[320,512]{1,0:T(8,128)(2,1)S(1)}, bf16[320,512]{1,0:T(8,128)(2,1)S(1)}, u32[]{:S(2)}, u32[]{:S(2)}) collective-permute-start(bf16[320,512]{1,0:T(8,128)(2,1)S(1)} %collective-permute-done.17.refs_3_), channel_id=1, source_target_pairs={{0,2},{1,5},{2,6},{3,1},{4,0},{5,9},{6,10},{7,3},{8,4},{9,13},{10,... | collective-permute-start | bytes 983048 | tf_op jit(solution)/shard_map/ppermute | solution.py:341
  81.5 8.5 %collective-permute-start.35 = (bf16[224,512]{1,0:T(8,128)(2,1)S(1)}, bf16[224,512]{1,0:T(8,128)(2,1)S(1)}, u32[]{:S(2)}, u32[]{:S(2)}) collective-permute-start(bf16[224,512]{1,0:T(8,128)(2,1)S(1)} %get-tuple-element.68), channel_id=1, source_target_pairs={{0,16},{16,0},{1,17},{17,1},{2,18},{18,2},{3,19},{19,3},{4,20},{20... | collective-permute-start | bytes 688136 | tf_op jit(solution)/shard_map/ppermute | solution.py:46
  83.5 10.5 %collective-permute-start.32 = (bf16[224,512]{1,0:T(8,128)(2,1)S(1)}, bf16[224,512]{1,0:T(8,128)(2,1)S(1)}, u32[]{:S(2)}, u32[]{:S(2)}) collective-permute-start(bf16[224,512]{1,0:T(8,128)(2,1)S(1)} %get-tuple-element.64), channel_id=1, source_target_pairs={{0,16},{16,0},{1,17},{17,1},{2,18},{18,2},{3,19},{19,3},{4,20},{20... | collective-permute-start | bytes 688136 | tf_op jit(solution)/shard_map/ppermute | solution.py:46
  (12 other events, 117.5 us)

commit v4 on v3

--- a/solution.py
+++ b/solution.py
@@ -254,8 +254,8 @@
         out_specs=[IN_VMEM] * 2 if gates else IN_VMEM,
         compiler_params=pltpu.CompilerParams(vmem_limit_bytes=16 * MIB),
         cost_estimate=pl.CostEstimate(
-            flops=3 * rows * width * depth * count,
-            bytes_accessed=2 * (rows * (depth * count + width) + count * depth * width),
+            flops=3 * rows * width * depth * count if gates or not column else 0,
+            bytes_accessed=2 * (rows * (depth * count + width) + count * depth * width) if gates or not column else 0,
             transcendentals=0,
         ),
         name="project",
@@ -411,7 +411,8 @@
         cross(slot - FLIGHT, *(arrived[other] if isinstance(other, int) else other for other in others))
         hop(slot, *waits.get(slot, []))
     if len(hops) > 2 * FLIGHT and len(widths) > 1:
-        needs[len(hops) - 1] = [project_strip(len(widths) - 1, strip, final=False) for strip in range(2)]
+        sums = [project_strip(len(widths) - 1, strip, final=False) for strip in range(2)]
+        needs[len(hops) - 2] = needs.get(len(hops) - 2, []) + sums
     for slot in range(max(len(hops) - FLIGHT, 0), len(hops)):
         cross(slot, *needs.get(slot, []))
     for piece in range(len(widths)):

time: 94.9 us -> 93.8 us (0.988)
  starting transfers between devices: 31.6 us -> 29.3 us
  waiting for transfers between devices: 34 us -> 35.3 us
    ppermute x14, starting transfers between devices: 22.8 us -> 16.8 us  [hop(): value = lax.ppermute(value, ('owner', 'slab'), ring)]
    ppermute x14, waiting for transfers between devices: 19.4 us -> 24.9 us  [hop(): value = lax.ppermute(value, ('owner', 'slab'), ring)]
    ppermute x22, waiting for transfers between devices: 14.6 us -> 10.4 us  [swap(): return lax.ppermute(value, axes, [(i, count - 1 - i) for i in range(count)])]
    ppermute x22, starting transfers between devices: 8.82 us -> 12.5 us  [swap(): return lax.ppermute(value, axes, [(i, count - 1 - i) for i in range(count)])]
  transfers between devices with their start and end apart: 36 -> 36, of which waited for: 12 -> 15; matrix products, arithmetic and copies ran while one was open for 0% -> 0% of each run, Pallas kernels for 28% -> 28%
where the time goes in v4:
time: 93.8 us; the launch traced here: 93.7 us
  waiting for transfers between devices  35.3 us (38%)
  starting transfers between devices  29.3 us (31%)
  Pallas kernels  28.8 us (31%)
    ppermute x14, waiting for transfers between devices, hop(): value = lax.ppermute(value, ('owner', 'slab'), ring)  24.9 us
    ppermute x14, starting transfers between devices, hop(): value = lax.ppermute(value, ('owner', 'slab'), ring)  16.8 us
    pallas_call x8, Pallas kernels, project(): pl.pallas_call(functools.partial(project_kernel, strip, column, total, bo...  16.1 us
    ppermute x22, starting transfers between devices, swap(): return lax.ppermute(value, axes, [(i, count - 1 - i) for i in range(count)])  12.5 us
    ppermute x22, waiting for transfers between devices, swap(): return lax.ppermute(value, axes, [(i, count - 1 - i) for i in range(count)])  10.4 us
    pallas_call x2, Pallas kernels, attend(): pl.pallas_call(functools.partial(attend_kernel, spots), grid=(steps,), ou...  6.73 us
    pallas_call x2, Pallas kernels, cut(): pl.pallas_call(functools.partial(cut_kernel, first, total, with_border),...  2.81 us
    pallas_call x2, Pallas kernels, place(): pl.pallas_call(functools.partial(place_kernel, len(blocks), columns, tota...  2.05 us
  transfers between devices with their start and end apart: 36, of which 15 were waited for; matrix products, arithmetic and copies ran while one was open for 0% of the time, Pallas kernels for 28%

profile of v4, /device:TPU:0, one launch (start us, length us, event | category | flops | bytes accessed | tf_op | source)
XLA Modules:
  0.0 93.7 jit_solution(6279405535532414679)
XLA Ops:
  0.0 1.7 %cut.2 = (bf16[320,768]{1,0:T(8,128)(2,1)S(1)}, bf16[320,768]{1,0:T(8,128)(2,1)S(1)}, bf16[2,1,112,1280]{3,2,1,0:T(8,128)(2,1)S(1)}, bf16[2,1,112,1280]{3,2,1,0:T(8,128)(2,1)S(1)}) custom-call(bf16[320,5120]{1,0:T(8,128)(2,1)} %weight_ref.3, bf16[2,1,2,112,2560]{4,3,2,1,0:T(8,128)(2,1)} %key_value_ref.3), custom_call_target="tpu_custom_call" | custom-call | bytes 1966080 | tf_op jit(solution)/shard_map/cut/pallas_call | solution.py:84
  2.3 2.9 %collective-permute-start.3 = (bf16[320,768]{1,0:T(8,128)(2,1)S(1)}, bf16[320,768]{1,0:T(8,128)(2,1)S(1)}, u32[]{:S(2)}, u32[]{:S(2)}) collective-permute-start(bf16[320,768]{1,0:T(8,128)(2,1)S(1)} %get-tuple-element.39.refs_0_), channel_id=1, source_target_pairs={{0,2},{1,5},{2,6},{3,1},{4,0},{5,9},{6,10},{7,3},{8,4},{9,13},{10,... | collective-permute-start | bytes 1474568 | tf_op jit(solution)/shard_map/ppermute | solution.py:341
  5.3 1.6 %collective-permute-start.6 = (bf16[320,768]{1,0:T(8,128)(2,1)S(1)}, bf16[320,768]{1,0:T(8,128)(2,1)S(1)}, u32[]{:S(2)}, u32[]{:S(2)}) collective-permute-start(bf16[320,768]{1,0:T(8,128)(2,1)S(1)} %get-tuple-element.42.refs_0_), channel_id=1, source_target_pairs={{0,2},{1,5},{2,6},{3,1},{4,0},{5,9},{6,10},{7,3},{8,4},{9,13},{10,... | collective-permute-start | bytes 1474568 | tf_op jit(solution)/shard_map/ppermute | solution.py:341
  6.9 3.4 %attend.2.refs_0_ = bf16[224,2560]{1,0:T(8,128)(2,1)S(1)} custom-call(s32[4,3]{1,0:T(4,128)S(1)} %copy-done.7, bf16[224,2560]{1,0:T(8,128)(2,1)} %bitcast.11, bf16[2,224,2560]{2,1,0:T(8,128)(2,1)S(1)} %bitcast.5, bf16[2,224,2560]{2,1,0:T(8,128)(2,1)S(1)} %bitcast.6, bf16[2,112,1280]{2,1,0:T(8,128)(2,1)S(1)} %collective-permute-done.1.k_halo_ref.v_halo_ref, ...), custom_call_target="tpu_custom_call" | custom-call | flops 3523215360 | bytes 3112960 | tf_op jit(solution)/shard_map/attend/pallas_call | solution.py:171
  10.2 3.4 %attend.3.near_ref = bf16[224,2560]{1,0:T(8,128)(2,1)S(1)} custom-call(s32[4,3]{1,0:T(4,128)S(1)} %copy-done.7, bf16[224,2560]{1,0:T(8,128)(2,1)} %bitcast.12, bf16[2,224,2560]{2,1,0:T(8,128)(2,1)S(1)} %bitcast.7, bf16[2,224,2560]{2,1,0:T(8,128)(2,1)S(1)} %bitcast.8, ...), custom_call_target="tpu_custom_call", output_to_operand_aliasing={{}: (6, {})} | custom-call | flops 3523215360 | bytes 3112960 | tf_op jit(solution)/shard_map/attend/pallas_call | solution.py:171
  13.7 1.6 %collective-permute-start.4 = (bf16[320,768]{1,0:T(8,128)(2,1)S(1)}, bf16[320,768]{1,0:T(8,128)(2,1)S(1)}, u32[]{:S(2)}, u32[]{:S(2)}) collective-permute-start(bf16[320,768]{1,0:T(8,128)(2,1)S(1)} %collective-permute-done.3.refs_1_), channel_id=1, source_target_pairs={{0,2},{1,5},{2,6},{3,1},{4,0},{5,9},{6,10},{7,3},{8,4},{9,13},{10,... | collective-permute-start | bytes 1474568 | tf_op jit(solution)/shard_map/ppermute | solution.py:341
  15.3 1.5 %collective-permute-start.2 = (bf16[224,2560]{1,0:T(8,128)(2,1)S(1)}, bf16[224,2560]{1,0:T(8,128)(2,1)S(1)}, u32[]{:S(2)}, u32[]{:S(2)}) collective-permute-start(bf16[224,2560]{1,0:T(8,128)(2,1)S(1)} %attend.3.near_ref), channel_id=1, source_target_pairs={{0,16},{16,0},{1,17},{17,1},{2,18},{18,2},{3,19},{19,3},{4,20},{20... | collective-permute-start | bytes 3440648 | tf_op jit(solution)/shard_map/ppermute | solution.py:46
  17.4 2.0 %collective-permute-start.9 = (bf16[320,768]{1,0:T(8,128)(2,1)S(1)}, bf16[320,768]{1,0:T(8,128)(2,1)S(1)}, u32[]{:S(2)}, u32[]{:S(2)}) collective-permute-start(bf16[320,768]{1,0:T(8,128)(2,1)S(1)} %collective-permute-done.6.refs_1_), channel_id=1, source_target_pairs={{0,2},{1,5},{2,6},{3,1},{4,0},{5,9},{6,10},{7,3},{8,4},{9,13},{10,... | collective-permute-start | bytes 1474568 | tf_op jit(solution)/shard_map/ppermute | solution.py:341
  21.0 1.6 %collective-permute-done.4.refs_2_ = bf16[320,768]{1,0:T(8,128)(2,1)S(1)} collective-permute-done((bf16[320,768]{1,0:T(8,128)(2,1)S(1)}, bf16[320,768]{1,0:T(8,128)(2,1)S(1)}, u32[]{:S(2)}, u32[]{:S(2)}) %collective-permute-start.4) | collective-permute-done | bytes 491552 | tf_op jit(solution)/shard_map/ppermute | solution.py:341
  22.7 2.0 %collective-permute-start.5 = (bf16[320,768]{1,0:T(8,128)(2,1)S(1)}, bf16[320,768]{1,0:T(8,128)(2,1)S(1)}, u32[]{:S(2)}, u32[]{:S(2)}) collective-permute-start(bf16[320,768]{1,0:T(8,128)(2,1)S(1)} %collective-permute-done.4.refs_2_), channel_id=1, source_target_pairs={{0,2},{1,5},{2,6},{3,1},{4,0},{5,9},{6,10},{7,3},{8,4},{9,13},{10,... | collective-permute-start | bytes 1474568 | tf_op jit(solution)/shard_map/ppermute | solution.py:341
  24.6 3.3 %collective-permute-done.9.refs_2_ = bf16[320,768]{1,0:T(8,128)(2,1)S(1)} collective-permute-done((bf16[320,768]{1,0:T(8,128)(2,1)S(1)}, bf16[320,768]{1,0:T(8,128)(2,1)S(1)}, u32[]{:S(2)}, u32[]{:S(2)}) %collective-permute-start.9) | collective-permute-done | bytes 491552 | tf_op jit(solution)/shard_map/ppermute | solution.py:341
  27.9 2.0 %collective-permute-start.11 = (bf16[320,768]{1,0:T(8,128)(2,1)S(1)}, bf16[320,768]{1,0:T(8,128)(2,1)S(1)}, u32[]{:S(2)}, u32[]{:S(2)}) collective-permute-start(bf16[320,768]{1,0:T(8,128)(2,1)S(1)} %collective-permute-done.9.refs_2_), channel_id=1, source_target_pairs={{0,2},{1,5},{2,6},{3,1},{4,0},{5,9},{6,10},{7,3},{8,4},{9,13},{10,... | collective-permute-start | bytes 1474568 | tf_op jit(solution)/shard_map/ppermute | solution.py:341
  29.9 3.3 %collective-permute-done.5.refs_3_ = bf16[320,768]{1,0:T(8,128)(2,1)S(1)} collective-permute-done((bf16[320,768]{1,0:T(8,128)(2,1)S(1)}, bf16[320,768]{1,0:T(8,128)(2,1)S(1)}, u32[]{:S(2)}, u32[]{:S(2)}) %collective-permute-start.5) | collective-permute-done | bytes 491552 | tf_op jit(solution)/shard_map/ppermute | solution.py:341
  33.2 2.0 %collective-permute-start.8 = (bf16[320,512]{1,0:T(8,128)(2,1)S(1)}, bf16[320,512]{1,0:T(8,128)(2,1)S(1)}, u32[]{:S(2)}, u32[]{:S(2)}) collective-permute-start(bf16[320,512]{1,0:T(8,128)(2,1)S(1)} %get-tuple-element.43.refs_0_), channel_id=1, source_target_pairs={{0,2},{1,5},{2,6},{3,1},{4,0},{5,9},{6,10},{7,3},{8,4},{9,13},{10,... | collective-permute-start | bytes 983048 | tf_op jit(solution)/shard_map/ppermute | solution.py:341
  35.8 2.7 %collective-permute-done.11.refs_3_ = bf16[320,768]{1,0:T(8,128)(2,1)S(1)} collective-permute-done((bf16[320,768]{1,0:T(8,128)(2,1)S(1)}, bf16[320,768]{1,0:T(8,128)(2,1)S(1)}, u32[]{:S(2)}, u32[]{:S(2)}) %collective-permute-start.11) | collective-permute-done | bytes 491552 | tf_op jit(solution)/shard_map/ppermute | solution.py:341
  38.5 1.9 %collective-permute-start.20 = (f32[1,5120]{1,0:T(1,128)S(1)}, f32[1,5120]{1,0:T(1,128)S(1)}, u32[]{:S(2)}, u32[]{:S(2)}) collective-permute-start(f32[1,5120]{1,0:T(1,128)S(1)} %scale_gate.1.refs_3_.refs_2_), channel_id=1, source_target_pairs={{0,16},{16,0},{1,17},{17,1},{2,18},{18,2},{3,19},{19,3},{4,20},{20... | collective-permute-start | bytes 61448 | tf_op jit(solution)/shard_map/ppermute | solution.py:46
  40.4 1.5 %collective-permute-done.2.far_ref = bf16[224,2560]{1,0:T(8,128)(2,1)S(1)} collective-permute-done((bf16[224,2560]{1,0:T(8,128)(2,1)S(1)}, bf16[224,2560]{1,0:T(8,128)(2,1)S(1)}, u32[]{:S(2)}, u32[]{:S(2)}) %collective-permute-start.2) | collective-permute-done | bytes 1146912 | tf_op jit(solution)/shard_map/ppermute | solution.py:46
  44.4 3.0 %project.8.refs_2_ = f32[448,768]{1,0:T(8,128)S(1)} custom-call(s32[2,8,6]{2,1,0:T(8,128)S(1)} %copy-done.5, bf16[8,448,320]{2,1,0:T(8,128)(2,1)S(1)} %arrange.1.rows_ref, bf16[320,768]{1,0:T(8,128)(2,1)S(1)} %get-tuple-element.39.refs_0_, bf16[320,768]{1,0:T(8,128)(2,1)S(1)} %collective-permute-done.3.refs_1_, ...), custom_call_target="tpu_custom_call" | custom-call | flops 1981808640 | bytes 5357568 | tf_op jit(solution)/shard_map/project/pallas_call | solution.py:250
  48.0 2.8 %collective-permute-done.13.refs_0_ = bf16[320,768]{1,0:T(8,128)(2,1)S(1)} collective-permute-done((bf16[320,768]{1,0:T(8,128)(2,1)S(1)}, bf16[320,768]{1,0:T(8,128)(2,1)S(1)}, u32[]{:S(2)}, u32[]{:S(2)}) %collective-permute-start.13) | collective-permute-done | bytes 491552 | tf_op jit(solution)/shard_map/ppermute | solution.py:341
  51.0 1.6 %project.9 = (bf16[224,768]{1,0:T(8,128)(2,1)S(1)}, bf16[224,768]{1,0:T(8,128)(2,1)S(1)}) custom-call(s32[2,8,2]{2,1,0:T(8,128)S(1)} %copy-done.3, bf16[8,448,320]{2,1,0:T(8,128)(2,1)S(1)} %arrange.1.rows_ref, bf16[320,768]{1,0:T(8,128)(2,1)S(1)} %collective-permute-done.13.refs_0_, bf16[320,768]{1,0:T(8,128)(2,1)S(1)} %collective-permute-done.21.refs_1_, ...), custom_call_target="tpu_custom_call" | custom-call | flops 660602880 | bytes 2244608 | tf_op jit(solution)/shard_map/project/pallas_call | solution.py:250
  52.6 1.7 %collective-permute-done.19.refs_1_ = bf16[320,512]{1,0:T(8,128)(2,1)S(1)} collective-permute-done((bf16[320,512]{1,0:T(8,128)(2,1)S(1)}, bf16[320,512]{1,0:T(8,128)(2,1)S(1)}, u32[]{:S(2)}, u32[]{:S(2)}) %collective-permute-start.19) | collective-permute-done | bytes 327712 | tf_op jit(solution)/shard_map/ppermute | solution.py:341
  54.5 1.5 %collective-permute-start.26 = (bf16[224,768]{1,0:T(8,128)(2,1)S(1)}, bf16[224,768]{1,0:T(8,128)(2,1)S(1)}, u32[]{:S(2)}, u32[]{:S(2)}) collective-permute-start(bf16[224,768]{1,0:T(8,128)(2,1)S(1)} %get-tuple-element.57), channel_id=1, source_target_pairs={{0,16},{16,0},{1,17},{17,1},{2,18},{18,2},{3,19},{19,3},{4,20},{20... | collective-permute-start | bytes 1032200 | tf_op jit(solution)/shard_map/ppermute | solution.py:46
  56.0 1.8 %collective-permute-done.15.refs_2_ = bf16[320,512]{1,0:T(8,128)(2,1)S(1)} collective-permute-done((bf16[320,512]{1,0:T(8,128)(2,1)S(1)}, bf16[320,512]{1,0:T(8,128)(2,1)S(1)}, u32[]{:S(2)}, u32[]{:S(2)}) %collective-permute-start.15) | collective-permute-done | bytes 327712 | tf_op jit(solution)/shard_map/ppermute | solution.py:341
  58.1 3.3 %collective-permute-done.25.refs_2_ = bf16[320,512]{1,0:T(8,128)(2,1)S(1)} collective-permute-done((bf16[320,512]{1,0:T(8,128)(2,1)S(1)}, bf16[320,512]{1,0:T(8,128)(2,1)S(1)}, u32[]{:S(2)}, u32[]{:S(2)}) %collective-permute-start.25) | collective-permute-done | bytes 327712 | tf_op jit(solution)/shard_map/ppermute | solution.py:341
  61.4 3.3 %project.10.refs_1_ = f32[448,768]{1,0:T(8,128)S(1)} custom-call(s32[2,8,7]{2,1,0:T(8,128)S(1)} %copy-done.4, bf16[8,448,320]{2,1,0:T(8,128)(2,1)S(1)} %arrange.1.rows_ref, bf16[320,768]{1,0:T(8,128)(2,1)S(1)} %get-tuple-element.42.refs_0_, bf16[320,768]{1,0:T(8,128)(2,1)S(1)} %collective-permute-done.6.refs_1_, ...), custom_call_target="tpu_custom_call" | custom-call | flops 2312110080 | bytes 6135808 | tf_op jit(solution)/shard_map/project/pallas_call | solution.py:250
  65.9 1.6 %collective-permute-start.32 = (bf16[224,768]{1,0:T(8,128)(2,1)S(1)}, bf16[224,768]{1,0:T(8,128)(2,1)S(1)}, u32[]{:S(2)}, u32[]{:S(2)}) collective-permute-start(bf16[224,768]{1,0:T(8,128)(2,1)S(1)} %get-tuple-element.63), channel_id=1, source_target_pairs={{0,16},{16,0},{1,17},{17,1},{2,18},{18,2},{3,19},{19,3},{4,20},{20... | collective-permute-start | bytes 1032200 | tf_op jit(solution)/shard_map/ppermute | solution.py:46
  69.7 2.2 %project.14.refs_2_ = f32[448,512]{1,0:T(8,128)S(1)} custom-call(s32[2,8,6]{2,1,0:T(8,128)S(1)} %copy-done.5, bf16[8,448,320]{2,1,0:T(8,128)(2,1)S(1)} %arrange.1.rows_ref, bf16[320,512]{1,0:T(8,128)(2,1)S(1)} %get-tuple-element.43.refs_0_, bf16[320,512]{1,0:T(8,128)(2,1)S(1)} %collective-permute-done.8.refs_1_, ...), custom_call_target="tpu_custom_call" | custom-call | tf_op jit(solution)/shard_map/project/pallas_call | solution.py:250
  72.0 2.8 %collective-permute-done.28.refs_3_ = bf16[320,512]{1,0:T(8,128)(2,1)S(1)} collective-permute-done((bf16[320,512]{1,0:T(8,128)(2,1)S(1)}, bf16[320,512]{1,0:T(8,128)(2,1)S(1)}, u32[]{:S(2)}, u32[]{:S(2)}) %collective-permute-start.28) | collective-permute-done | bytes 327712 | tf_op jit(solution)/shard_map/ppermute | solution.py:341
  74.8 2.5 %project.12.refs_1_ = f32[448,512]{1,0:T(8,128)S(1)} custom-call(s32[2,8,7]{2,1,0:T(8,128)S(1)} %copy-done.4, bf16[8,448,320]{2,1,0:T(8,128)(2,1)S(1)} %arrange.1.rows_ref, bf16[320,512]{1,0:T(8,128)(2,1)S(1)} %get-tuple-element.50.refs_0_, bf16[320,512]{1,0:T(8,128)(2,1)S(1)} %collective-permute-done.19.refs_1_, ...), custom_call_target="tpu_custom_call" | custom-call | tf_op jit(solution)/shard_map/project/pallas_call | solution.py:250
  82.0 1.5 %collective-permute-start.31 = (bf16[224,512]{1,0:T(8,128)(2,1)S(1)}, bf16[224,512]{1,0:T(8,128)(2,1)S(1)}, u32[]{:S(2)}, u32[]{:S(2)}) collective-permute-start(bf16[224,512]{1,0:T(8,128)(2,1)S(1)} %get-tuple-element.62), channel_id=1, source_target_pairs={{0,16},{16,0},{1,17},{17,1},{2,18},{18,2},{3,19},{19,3},{4,20},{20... | collective-permute-start | bytes 688136 | tf_op jit(solution)/shard_map/ppermute | solution.py:46
  83.5 5.3 %collective-permute-done.35.refs_5_ = bf16[224,512]{1,0:T(8,128)(2,1)S(1)} collective-permute-done((bf16[224,512]{1,0:T(8,128)(2,1)S(1)}, bf16[224,512]{1,0:T(8,128)(2,1)S(1)}, u32[]{:S(2)}, u32[]{:S(2)}) %collective-permute-start.35) | collective-permute-done | bytes 229408 | tf_op jit(solution)/shard_map/ppermute | solution.py:46
  90.1 2.8 %collective-permute-done.31.refs_1_ = bf16[224,512]{1,0:T(8,128)(2,1)S(1)} collective-permute-done((bf16[224,512]{1,0:T(8,128)(2,1)S(1)}, bf16[224,512]{1,0:T(8,128)(2,1)S(1)}, u32[]{:S(2)}, u32[]{:S(2)}) %collective-permute-start.31) | collective-permute-done | bytes 229408 | tf_op jit(solution)/shard_map/ppermute | solution.py:46
  (72 shorter events, 17.5 us)
Async XLA Ops:
  1.7 5.1 %collective-permute-start.1 = (bf16[2,112,1280]{2,1,0:T(8,128)(2,1)S(1)}, bf16[2,112,1280]{2,1,0:T(8,128)(2,1)S(1)}, u32[]{:S(2)}, u32[]{:S(2)}) collective-permute-start(bf16[2,112,1280]{2,1,0:T(8,128)(2,1)S(1)} %bitcast.10), channel_id=1, source_target_pairs={{0,1},{1,0},{2,3},{3,2},{4,5},{5,4},{6,7},{7,6},{8,9},{9,8},{10,11... | collective-permute-start | bytes 1720328 | tf_op jit(solution)/shard_map/ppermute | solution.py:46
  2.3 8.0 %collective-permute-start = (bf16[2,112,1280]{2,1,0:T(8,128)(2,1)S(1)}, bf16[2,112,1280]{2,1,0:T(8,128)(2,1)S(1)}, u32[]{:S(2)}, u32[]{:S(2)}) collective-permute-start(bf16[2,112,1280]{2,1,0:T(8,128)(2,1)S(1)} %bitcast.9), channel_id=1, source_target_pairs={{0,1},{1,0},{2,3},{3,2},{4,5},{5,4},{6,7},{7,6},{8,9},{9,8},{10,11... | collective-permute-start | bytes 1720328 | tf_op jit(solution)/shard_map/ppermute | solution.py:46
  2.3 11.3 %collective-permute-start.3 = (bf16[320,768]{1,0:T(8,128)(2,1)S(1)}, bf16[320,768]{1,0:T(8,128)(2,1)S(1)}, u32[]{:S(2)}, u32[]{:S(2)}) collective-permute-start(bf16[320,768]{1,0:T(8,128)(2,1)S(1)} %get-tuple-element.39.refs_0_), channel_id=1, source_target_pairs={{0,2},{1,5},{2,6},{3,1},{4,0},{5,9},{6,10},{7,3},{8,4},{9,13},{10,... | collective-permute-start | bytes 1474568 | tf_op jit(solution)/shard_map/ppermute | solution.py:341
  5.3 12.1 %collective-permute-start.6 = (bf16[320,768]{1,0:T(8,128)(2,1)S(1)}, bf16[320,768]{1,0:T(8,128)(2,1)S(1)}, u32[]{:S(2)}, u32[]{:S(2)}) collective-permute-start(bf16[320,768]{1,0:T(8,128)(2,1)S(1)} %get-tuple-element.42.refs_0_), channel_id=1, source_target_pairs={{0,2},{1,5},{2,6},{3,1},{4,0},{5,9},{6,10},{7,3},{8,4},{9,13},{10,... | collective-permute-start | bytes 1474568 | tf_op jit(solution)/shard_map/ppermute | solution.py:341
  13.7 9.0 %collective-permute-start.4 = (bf16[320,768]{1,0:T(8,128)(2,1)S(1)}, bf16[320,768]{1,0:T(8,128)(2,1)S(1)}, u32[]{:S(2)}, u32[]{:S(2)}) collective-permute-start(bf16[320,768]{1,0:T(8,128)(2,1)S(1)} %collective-permute-done.3.refs_1_), channel_id=1, source_target_pairs={{0,2},{1,5},{2,6},{3,1},{4,0},{5,9},{6,10},{7,3},{8,4},{9,13},{10,... | collective-permute-start | bytes 1474568 | tf_op jit(solution)/shard_map/ppermute | solution.py:341
  15.3 26.7 %collective-permute-start.2 = (bf16[224,2560]{1,0:T(8,128)(2,1)S(1)}, bf16[224,2560]{1,0:T(8,128)(2,1)S(1)}, u32[]{:S(2)}, u32[]{:S(2)}) collective-permute-start(bf16[224,2560]{1,0:T(8,128)(2,1)S(1)} %attend.3.near_ref), channel_id=1, source_target_pairs={{0,16},{16,0},{1,17},{17,1},{2,18},{18,2},{3,19},{19,3},{4,20},{20... | collective-permute-start | bytes 3440648 | tf_op jit(solution)/shard_map/ppermute | solution.py:46
  17.4 10.5 %collective-permute-start.9 = (bf16[320,768]{1,0:T(8,128)(2,1)S(1)}, bf16[320,768]{1,0:T(8,128)(2,1)S(1)}, u32[]{:S(2)}, u32[]{:S(2)}) collective-permute-start(bf16[320,768]{1,0:T(8,128)(2,1)S(1)} %collective-permute-done.6.refs_1_), channel_id=1, source_target_pairs={{0,2},{1,5},{2,6},{3,1},{4,0},{5,9},{6,10},{7,3},{8,4},{9,13},{10,... | collective-permute-start | bytes 1474568 | tf_op jit(solution)/shard_map/ppermute | solution.py:341
  19.4 8.6 %collective-permute-start.10 = (bf16[320,768]{1,0:T(8,128)(2,1)S(1)}, bf16[320,768]{1,0:T(8,128)(2,1)S(1)}, u32[]{:S(2)}, u32[]{:S(2)}) collective-permute-start(bf16[320,768]{1,0:T(8,128)(2,1)S(1)} %collective-permute-done.3.refs_1_), channel_id=1, source_target_pairs={{0,1},{1,0},{2,3},{3,2},{4,5},{5,4},{6,7},{7,6},{8,9},{9,8},{10,11... | collective-permute-start | bytes 1474568 | tf_op jit(solution)/shard_map/ppermute | solution.py:46
  20.5 9.4 %collective-permute-start.7 = (bf16[320,768]{1,0:T(8,128)(2,1)S(1)}, bf16[320,768]{1,0:T(8,128)(2,1)S(1)}, u32[]{:S(2)}, u32[]{:S(2)}) collective-permute-start(bf16[320,768]{1,0:T(8,128)(2,1)S(1)} %collective-permute-done.6.refs_1_), channel_id=1, source_target_pairs={{0,1},{1,0},{2,3},{3,2},{4,5},{5,4},{6,7},{7,6},{8,9},{9,8},{10,11... | collective-permute-start | bytes 1474568 | tf_op jit(solution)/shard_map/ppermute | solution.py:46
  22.7 10.5 %collective-permute-start.5 = (bf16[320,768]{1,0:T(8,128)(2,1)S(1)}, bf16[320,768]{1,0:T(8,128)(2,1)S(1)}, u32[]{:S(2)}, u32[]{:S(2)}) collective-permute-start(bf16[320,768]{1,0:T(8,128)(2,1)S(1)} %collective-permute-done.4.refs_2_), channel_id=1, source_target_pairs={{0,2},{1,5},{2,6},{3,1},{4,0},{5,9},{6,10},{7,3},{8,4},{9,13},{10,... | collective-permute-start | bytes 1474568 | tf_op jit(solution)/shard_map/ppermute | solution.py:341
  27.9 10.5 %collective-permute-start.11 = (bf16[320,768]{1,0:T(8,128)(2,1)S(1)}, bf16[320,768]{1,0:T(8,128)(2,1)S(1)}, u32[]{:S(2)}, u32[]{:S(2)}) collective-permute-start(bf16[320,768]{1,0:T(8,128)(2,1)S(1)} %collective-permute-done.9.refs_2_), channel_id=1, source_target_pairs={{0,2},{1,5},{2,6},{3,1},{4,0},{5,9},{6,10},{7,3},{8,4},{9,13},{10,... | collective-permute-start | bytes 1474568 | tf_op jit(solution)/shard_map/ppermute | solution.py:341
  29.9 10.5 %collective-permute-start.12 = (bf16[320,768]{1,0:T(8,128)(2,1)S(1)}, bf16[320,768]{1,0:T(8,128)(2,1)S(1)}, u32[]{:S(2)}, u32[]{:S(2)}) collective-permute-start(bf16[320,768]{1,0:T(8,128)(2,1)S(1)} %collective-permute-done.4.refs_2_), channel_id=1, source_target_pairs={{0,1},{1,0},{2,3},{3,2},{4,5},{5,4},{6,7},{7,6},{8,9},{9,8},{10,11... | collective-permute-start | bytes 1474568 | tf_op jit(solution)/shard_map/ppermute | solution.py:46
  33.2 9.6 %collective-permute-start.8 = (bf16[320,512]{1,0:T(8,128)(2,1)S(1)}, bf16[320,512]{1,0:T(8,128)(2,1)S(1)}, u32[]{:S(2)}, u32[]{:S(2)}) collective-permute-start(bf16[320,512]{1,0:T(8,128)(2,1)S(1)} %get-tuple-element.43.refs_0_), channel_id=1, source_target_pairs={{0,2},{1,5},{2,6},{3,1},{4,0},{5,9},{6,10},{7,3},{8,4},{9,13},{10,... | collective-permute-start | bytes 983048 | tf_op jit(solution)/shard_map/ppermute | solution.py:341
  35.2 8.1 %collective-permute-start.18 = (bf16[320,768]{1,0:T(8,128)(2,1)S(1)}, bf16[320,768]{1,0:T(8,128)(2,1)S(1)}, u32[]{:S(2)}, u32[]{:S(2)}) collective-permute-start(bf16[320,768]{1,0:T(8,128)(2,1)S(1)} %collective-permute-done.9.refs_2_), channel_id=1, source_target_pairs={{0,1},{1,0},{2,3},{3,2},{4,5},{5,4},{6,7},{7,6},{8,9},{9,8},{10,11... | collective-permute-start | bytes 1474568 | tf_op jit(solution)/shard_map/ppermute | solution.py:46
  40.4 7.5 %collective-permute-start.14 = (bf16[320,768]{1,0:T(8,128)(2,1)S(1)}, bf16[320,768]{1,0:T(8,128)(2,1)S(1)}, u32[]{:S(2)}, u32[]{:S(2)}) collective-permute-start(bf16[320,768]{1,0:T(8,128)(2,1)S(1)} %collective-permute-done.5.refs_3_), channel_id=1, source_target_pairs={{0,1},{1,0},{2,3},{3,2},{4,5},{5,4},{6,7},{7,6},{8,9},{9,8},{10,11... | collective-permute-start | bytes 1474568 | tf_op jit(solution)/shard_map/ppermute | solution.py:46
  42.0 8.8 %collective-permute-start.13 = (bf16[320,768]{1,0:T(8,128)(2,1)S(1)}, bf16[320,768]{1,0:T(8,128)(2,1)S(1)}, u32[]{:S(2)}, u32[]{:S(2)}) collective-permute-start(bf16[320,768]{1,0:T(8,128)(2,1)S(1)} %collective-permute-done.5.refs_3_), channel_id=1, source_target_pairs={{0,2},{1,5},{2,6},{3,1},{4,0},{5,9},{6,10},{7,3},{8,4},{9,13},{10,... | collective-permute-start | bytes 1474568 | tf_op jit(solution)/shard_map/ppermute | solution.py:341
  42.8 8.2 %collective-permute-start.21 = (bf16[320,768]{1,0:T(8,128)(2,1)S(1)}, bf16[320,768]{1,0:T(8,128)(2,1)S(1)}, u32[]{:S(2)}, u32[]{:S(2)}) collective-permute-start(bf16[320,768]{1,0:T(8,128)(2,1)S(1)} %collective-permute-done.11.refs_3_), channel_id=1, source_target_pairs={{0,1},{1,0},{2,3},{3,2},{4,5},{5,4},{6,7},{7,6},{8,9},{9,8},{10,11... | collective-permute-start | bytes 1474568 | tf_op jit(solution)/shard_map/ppermute | solution.py:46
  43.2 11.1 %collective-permute-start.19 = (bf16[320,512]{1,0:T(8,128)(2,1)S(1)}, bf16[320,512]{1,0:T(8,128)(2,1)S(1)}, u32[]{:S(2)}, u32[]{:S(2)}) collective-permute-start(bf16[320,512]{1,0:T(8,128)(2,1)S(1)} %get-tuple-element.50.refs_0_), channel_id=1, source_target_pairs={{0,2},{1,5},{2,6},{3,1},{4,0},{5,9},{6,10},{7,3},{8,4},{9,13},{10,... | collective-permute-start | bytes 983048 | tf_op jit(solution)/shard_map/ppermute | solution.py:341
  47.3 8.7 %collective-permute-start.16 = (bf16[320,512]{1,0:T(8,128)(2,1)S(1)}, bf16[320,512]{1,0:T(8,128)(2,1)S(1)}, u32[]{:S(2)}, u32[]{:S(2)}) collective-permute-start(bf16[320,512]{1,0:T(8,128)(2,1)S(1)} %collective-permute-done.8.refs_1_), channel_id=1, source_target_pairs={{0,1},{1,0},{2,3},{3,2},{4,5},{5,4},{6,7},{7,6},{8,9},{9,8},{10,11... | collective-permute-start | bytes 983048 | tf_op jit(solution)/shard_map/ppermute | solution.py:46
  50.8 7.1 %collective-permute-start.15 = (bf16[320,512]{1,0:T(8,128)(2,1)S(1)}, bf16[320,512]{1,0:T(8,128)(2,1)S(1)}, u32[]{:S(2)}, u32[]{:S(2)}) collective-permute-start(bf16[320,512]{1,0:T(8,128)(2,1)S(1)} %collective-permute-done.8.refs_1_), channel_id=1, source_target_pairs={{0,2},{1,5},{2,6},{3,1},{4,0},{5,9},{6,10},{7,3},{8,4},{9,13},{10,... | collective-permute-start | bytes 983048 | tf_op jit(solution)/shard_map/ppermute | solution.py:341
  54.3 7.1 %collective-permute-start.25 = (bf16[320,512]{1,0:T(8,128)(2,1)S(1)}, bf16[320,512]{1,0:T(8,128)(2,1)S(1)}, u32[]{:S(2)}, u32[]{:S(2)}) collective-permute-start(bf16[320,512]{1,0:T(8,128)(2,1)S(1)} %collective-permute-done.19.refs_1_), channel_id=1, source_target_pairs={{0,2},{1,5},{2,6},{3,1},{4,0},{5,9},{6,10},{7,3},{8,4},{9,13},{10,... | collective-permute-start | bytes 983048 | tf_op jit(solution)/shard_map/ppermute | solution.py:341
  54.5 10.2 %collective-permute-start.27 = (bf16[320,768]{1,0:T(8,128)(2,1)S(1)}, bf16[320,768]{1,0:T(8,128)(2,1)S(1)}, u32[]{:S(2)}, u32[]{:S(2)}) collective-permute-start(bf16[320,768]{1,0:T(8,128)(2,1)S(1)} %collective-permute-done.13.refs_0_), channel_id=1, source_target_pairs={{0,1},{1,0},{2,3},{3,2},{4,5},{5,4},{6,7},{7,6},{8,9},{9,8},{10,11... | collective-permute-start | bytes 1474568 | tf_op jit(solution)/shard_map/ppermute | solution.py:46
  54.5 12.9 %collective-permute-start.26 = (bf16[224,768]{1,0:T(8,128)(2,1)S(1)}, bf16[224,768]{1,0:T(8,128)(2,1)S(1)}, u32[]{:S(2)}, u32[]{:S(2)}) collective-permute-start(bf16[224,768]{1,0:T(8,128)(2,1)S(1)} %get-tuple-element.57), channel_id=1, source_target_pairs={{0,16},{16,0},{1,17},{17,1},{2,18},{18,2},{3,19},{19,3},{4,20},{20... | collective-permute-start | bytes 1032200 | tf_op jit(solution)/shard_map/ppermute | solution.py:46
  57.9 9.8 %collective-permute-start.17 = (bf16[320,512]{1,0:T(8,128)(2,1)S(1)}, bf16[320,512]{1,0:T(8,128)(2,1)S(1)}, u32[]{:S(2)}, u32[]{:S(2)}) collective-permute-start(bf16[320,512]{1,0:T(8,128)(2,1)S(1)} %collective-permute-done.15.refs_2_), channel_id=1, source_target_pairs={{0,2},{1,5},{2,6},{3,1},{4,0},{5,9},{6,10},{7,3},{8,4},{9,13},{10,... | collective-permute-start | bytes 983048 | tf_op jit(solution)/shard_map/ppermute | solution.py:341
  58.1 9.8 %collective-permute-start.22 = (bf16[320,512]{1,0:T(8,128)(2,1)S(1)}, bf16[320,512]{1,0:T(8,128)(2,1)S(1)}, u32[]{:S(2)}, u32[]{:S(2)}) collective-permute-start(bf16[320,512]{1,0:T(8,128)(2,1)S(1)} %collective-permute-done.19.refs_1_), channel_id=1, source_target_pairs={{0,1},{1,0},{2,3},{3,2},{4,5},{5,4},{6,7},{7,6},{8,9},{9,8},{10,11... | collective-permute-start | bytes 983048 | tf_op jit(solution)/shard_map/ppermute | solution.py:46
  61.4 7.9 %collective-permute-start.33 = (bf16[320,512]{1,0:T(8,128)(2,1)S(1)}, bf16[320,512]{1,0:T(8,128)(2,1)S(1)}, u32[]{:S(2)}, u32[]{:S(2)}) collective-permute-start(bf16[320,512]{1,0:T(8,128)(2,1)S(1)} %collective-permute-done.25.refs_2_), channel_id=1, source_target_pairs={{0,1},{1,0},{2,3},{3,2},{4,5},{5,4},{6,7},{7,6},{8,9},{9,8},{10,11... | collective-permute-start | bytes 983048 | tf_op jit(solution)/shard_map/ppermute | solution.py:46
  65.9 11.4 %collective-permute-start.32 = (bf16[224,768]{1,0:T(8,128)(2,1)S(1)}, bf16[224,768]{1,0:T(8,128)(2,1)S(1)}, u32[]{:S(2)}, u32[]{:S(2)}) collective-permute-start(bf16[224,768]{1,0:T(8,128)(2,1)S(1)} %get-tuple-element.63), channel_id=1, source_target_pairs={{0,16},{16,0},{1,17},{17,1},{2,18},{18,2},{3,19},{19,3},{4,20},{20... | collective-permute-start | bytes 1032200 | tf_op jit(solution)/shard_map/ppermute | solution.py:46
  67.7 7.1 %collective-permute-start.28 = (bf16[320,512]{1,0:T(8,128)(2,1)S(1)}, bf16[320,512]{1,0:T(8,128)(2,1)S(1)}, u32[]{:S(2)}, u32[]{:S(2)}) collective-permute-start(bf16[320,512]{1,0:T(8,128)(2,1)S(1)} %collective-permute-done.25.refs_2_), channel_id=1, source_target_pairs={{0,2},{1,5},{2,6},{3,1},{4,0},{5,9},{6,10},{7,3},{8,4},{9,13},{10,... | collective-permute-start | bytes 983048 | tf_op jit(solution)/shard_map/ppermute | solution.py:341
  67.9 6.9 %collective-permute-start.30 = (bf16[320,512]{1,0:T(8,128)(2,1)S(1)}, bf16[320,512]{1,0:T(8,128)(2,1)S(1)}, u32[]{:S(2)}, u32[]{:S(2)}) collective-permute-start(bf16[320,512]{1,0:T(8,128)(2,1)S(1)} %collective-permute-done.17.refs_3_), channel_id=1, source_target_pairs={{0,1},{1,0},{2,3},{3,2},{4,5},{5,4},{6,7},{7,6},{8,9},{9,8},{10,11... | collective-permute-start | bytes 983048 | tf_op jit(solution)/shard_map/ppermute | solution.py:46
  69.2 9.1 %collective-permute-start.23 = (bf16[320,512]{1,0:T(8,128)(2,1)S(1)}, bf16[320,512]{1,0:T(8,128)(2,1)S(1)}, u32[]{:S(2)}, u32[]{:S(2)}) collective-permute-start(bf16[320,512]{1,0:T(8,128)(2,1)S(1)} %collective-permute-done.17.refs_3_), channel_id=1, source_target_pairs={{0,2},{1,5},{2,6},{3,1},{4,0},{5,9},{6,10},{7,3},{8,4},{9,13},{10,... | collective-permute-start | bytes 983048 | tf_op jit(solution)/shard_map/ppermute | solution.py:341
  80.3 8.5 %collective-permute-start.35 = (bf16[224,512]{1,0:T(8,128)(2,1)S(1)}, bf16[224,512]{1,0:T(8,128)(2,1)S(1)}, u32[]{:S(2)}, u32[]{:S(2)}) collective-permute-start(bf16[224,512]{1,0:T(8,128)(2,1)S(1)} %get-tuple-element.66), channel_id=1, source_target_pairs={{0,16},{16,0},{1,17},{17,1},{2,18},{18,2},{3,19},{19,3},{4,20},{20... | collective-permute-start | bytes 688136 | tf_op jit(solution)/shard_map/ppermute | solution.py:46
  82.0 10.9 %collective-permute-start.31 = (bf16[224,512]{1,0:T(8,128)(2,1)S(1)}, bf16[224,512]{1,0:T(8,128)(2,1)S(1)}, u32[]{:S(2)}, u32[]{:S(2)}) collective-permute-start(bf16[224,512]{1,0:T(8,128)(2,1)S(1)} %get-tuple-element.62), channel_id=1, source_target_pairs={{0,16},{16,0},{1,17},{17,1},{2,18},{18,2},{3,19},{19,3},{4,20},{20... | collective-permute-start | bytes 688136 | tf_op jit(solution)/shard_map/ppermute | solution.py:46
  (12 other events, 110.6 us)

commit v5 on v4

--- a/solution.py
+++ b/solution.py
@@ -254,8 +254,8 @@
         out_specs=[IN_VMEM] * 2 if gates else IN_VMEM,
         compiler_params=pltpu.CompilerParams(vmem_limit_bytes=16 * MIB),
         cost_estimate=pl.CostEstimate(
-            flops=3 * rows * width * depth * count if gates or not column else 0,
-            bytes_accessed=2 * (rows * (depth * count + width) + count * depth * width) if gates or not column else 0,
+            flops=3 * rows * width * depth * count if gates else 0,
+            bytes_accessed=2 * (rows * (depth * count + width) + count * depth * width) if gates else 0,
             transcendentals=0,
         ),
         name="project",
@@ -407,6 +407,8 @@
             else:
                 needs[first_done + 1] = [results[0, strip][0]]
                 waits.setdefault(len(hops) - 2, []).append(results[0, strip][1])
+        if slot == first_done + FLIGHT - 1:
+            needs[first_done - 1] = [project_strip(0, 1, final=False)]
         others = needs.get(slot - FLIGHT, [])
         cross(slot - FLIGHT, *(arrived[other] if isinstance(other, int) else other for other in others))
         hop(slot, *waits.get(slot, []))

time: 93.8 us -> 92.2 us (0.983)
  waiting for transfers between devices: 35.3 us -> 30.9 us
  starting transfers between devices: 29.3 us -> 32 us
    ppermute x14, waiting for transfers between devices: 24.9 us -> 19.1 us  [hop(): value = lax.ppermute(value, ('owner', 'slab'), ring)]
    ppermute x14, starting transfers between devices: 16.8 us -> 21.1 us  [hop(): value = lax.ppermute(value, ('owner', 'slab'), ring)]
    ppermute x22, starting transfers between devices: 12.5 us -> 10.9 us  [swap(): return lax.ppermute(value, axes, [(i, count - 1 - i) for i in range(count)])]
    ppermute x22, waiting for transfers between devices: 10.4 us -> 11.8 us  [swap(): return lax.ppermute(value, axes, [(i, count - 1 - i) for i in range(count)])]
  transfers between devices with their start and end apart: 36 -> 36, of which waited for: 15 -> 15; matrix products, arithmetic and copies ran while one was open for 0% -> 0% of each run, Pallas kernels for 28% -> 29%
where the time goes in v5:
time: 92.2 us; the launch traced here: 92 us
  starting transfers between devices  32 us (35%)
  waiting for transfers between devices  30.9 us (34%)
  Pallas kernels  28.8 us (31%)
    ppermute x14, starting transfers between devices, hop(): value = lax.ppermute(value, ('owner', 'slab'), ring)  21.1 us
    ppermute x14, waiting for transfers between devices, hop(): value = lax.ppermute(value, ('owner', 'slab'), ring)  19.1 us
    pallas_call x8, Pallas kernels, project(): pl.pallas_call(functools.partial(project_kernel, strip, column, total, bo...  16.1 us
    ppermute x22, waiting for transfers between devices, swap(): return lax.ppermute(value, axes, [(i, count - 1 - i) for i in range(count)])  11.8 us
    ppermute x22, starting transfers between devices, swap(): return lax.ppermute(value, axes, [(i, count - 1 - i) for i in range(count)])  10.9 us
    pallas_call x2, Pallas kernels, attend(): pl.pallas_call(functools.partial(attend_kernel, spots), grid=(steps,), ou...  6.73 us
    pallas_call x2, Pallas kernels, cut(): pl.pallas_call(functools.partial(cut_kernel, first, total, with_border),...  2.81 us
    pallas_call x2, Pallas kernels, place(): pl.pallas_call(functools.partial(place_kernel, len(blocks), columns, tota...  2.05 us
  transfers between devices with their start and end apart: 36, of which 15 were waited for; matrix products, arithmetic and copies ran while one was open for 0% of the time, Pallas kernels for 29%

profile of v5, /device:TPU:0, one launch (start us, length us, event | category | flops | bytes accessed | tf_op | source)
XLA Modules:
  0.0 92.0 jit_solution(3768039589081809799)
XLA Ops:
  0.0 1.7 %cut.2 = (bf16[320,768]{1,0:T(8,128)(2,1)S(1)}, bf16[320,768]{1,0:T(8,128)(2,1)S(1)}, bf16[2,1,112,1280]{3,2,1,0:T(8,128)(2,1)S(1)}, bf16[2,1,112,1280]{3,2,1,0:T(8,128)(2,1)S(1)}) custom-call(bf16[320,5120]{1,0:T(8,128)(2,1)} %weight_ref.3, bf16[2,1,2,112,2560]{4,3,2,1,0:T(8,128)(2,1)} %key_value_ref.3), custom_call_target="tpu_custom_call" | custom-call | bytes 1966080 | tf_op jit(solution)/shard_map/cut/pallas_call | solution.py:84
  2.3 2.9 %collective-permute-start.3 = (bf16[320,768]{1,0:T(8,128)(2,1)S(1)}, bf16[320,768]{1,0:T(8,128)(2,1)S(1)}, u32[]{:S(2)}, u32[]{:S(2)}) collective-permute-start(bf16[320,768]{1,0:T(8,128)(2,1)S(1)} %get-tuple-element.40.refs_0_), channel_id=1, source_target_pairs={{0,2},{1,5},{2,6},{3,1},{4,0},{5,9},{6,10},{7,3},{8,4},{9,13},{10,... | collective-permute-start | bytes 1474568 | tf_op jit(solution)/shard_map/ppermute | solution.py:341
  5.3 1.6 %collective-permute-start.6 = (bf16[320,768]{1,0:T(8,128)(2,1)S(1)}, bf16[320,768]{1,0:T(8,128)(2,1)S(1)}, u32[]{:S(2)}, u32[]{:S(2)}) collective-permute-start(bf16[320,768]{1,0:T(8,128)(2,1)S(1)} %get-tuple-element.43.refs_0_), channel_id=1, source_target_pairs={{0,2},{1,5},{2,6},{3,1},{4,0},{5,9},{6,10},{7,3},{8,4},{9,13},{10,... | collective-permute-start | bytes 1474568 | tf_op jit(solution)/shard_map/ppermute | solution.py:341
  6.9 3.4 %attend.2.refs_0_ = bf16[224,2560]{1,0:T(8,128)(2,1)S(1)} custom-call(s32[4,3]{1,0:T(4,128)S(1)} %copy-done.7, bf16[224,2560]{1,0:T(8,128)(2,1)} %bitcast.11, bf16[2,224,2560]{2,1,0:T(8,128)(2,1)S(1)} %bitcast.5, bf16[2,224,2560]{2,1,0:T(8,128)(2,1)S(1)} %bitcast.6, bf16[2,112,1280]{2,1,0:T(8,128)(2,1)S(1)} %collective-permute-done.1.k_halo_ref.v_halo_ref, ...), custom_call_target="tpu_custom_call" | custom-call | flops 3523215360 | bytes 3112960 | tf_op jit(solution)/shard_map/attend/pallas_call | solution.py:171
  10.2 3.4 %attend.3.near_ref = bf16[224,2560]{1,0:T(8,128)(2,1)S(1)} custom-call(s32[4,3]{1,0:T(4,128)S(1)} %copy-done.7, bf16[224,2560]{1,0:T(8,128)(2,1)} %bitcast.12, bf16[2,224,2560]{2,1,0:T(8,128)(2,1)S(1)} %bitcast.7, bf16[2,224,2560]{2,1,0:T(8,128)(2,1)S(1)} %bitcast.8, ...), custom_call_target="tpu_custom_call", output_to_operand_aliasing={{}: (6, {})} | custom-call | flops 3523215360 | bytes 3112960 | tf_op jit(solution)/shard_map/attend/pallas_call | solution.py:171
  13.7 1.6 %collective-permute-start.4 = (bf16[320,768]{1,0:T(8,128)(2,1)S(1)}, bf16[320,768]{1,0:T(8,128)(2,1)S(1)}, u32[]{:S(2)}, u32[]{:S(2)}) collective-permute-start(bf16[320,768]{1,0:T(8,128)(2,1)S(1)} %collective-permute-done.3.refs_1_), channel_id=1, source_target_pairs={{0,2},{1,5},{2,6},{3,1},{4,0},{5,9},{6,10},{7,3},{8,4},{9,13},{10,... | collective-permute-start | bytes 1474568 | tf_op jit(solution)/shard_map/ppermute | solution.py:341
  15.3 1.5 %collective-permute-start.2 = (bf16[224,2560]{1,0:T(8,128)(2,1)S(1)}, bf16[224,2560]{1,0:T(8,128)(2,1)S(1)}, u32[]{:S(2)}, u32[]{:S(2)}) collective-permute-start(bf16[224,2560]{1,0:T(8,128)(2,1)S(1)} %attend.3.near_ref), channel_id=1, source_target_pairs={{0,16},{16,0},{1,17},{17,1},{2,18},{18,2},{3,19},{19,3},{4,20},{20... | collective-permute-start | bytes 3440648 | tf_op jit(solution)/shard_map/ppermute | solution.py:46
  17.4 2.0 %collective-permute-start.9 = (bf16[320,768]{1,0:T(8,128)(2,1)S(1)}, bf16[320,768]{1,0:T(8,128)(2,1)S(1)}, u32[]{:S(2)}, u32[]{:S(2)}) collective-permute-start(bf16[320,768]{1,0:T(8,128)(2,1)S(1)} %collective-permute-done.6.refs_1_), channel_id=1, source_target_pairs={{0,2},{1,5},{2,6},{3,1},{4,0},{5,9},{6,10},{7,3},{8,4},{9,13},{10,... | collective-permute-start | bytes 1474568 | tf_op jit(solution)/shard_map/ppermute | solution.py:341
  21.0 1.6 %collective-permute-done.4.refs_2_ = bf16[320,768]{1,0:T(8,128)(2,1)S(1)} collective-permute-done((bf16[320,768]{1,0:T(8,128)(2,1)S(1)}, bf16[320,768]{1,0:T(8,128)(2,1)S(1)}, u32[]{:S(2)}, u32[]{:S(2)}) %collective-permute-start.4) | collective-permute-done | bytes 491552 | tf_op jit(solution)/shard_map/ppermute | solution.py:341
  22.7 2.0 %collective-permute-start.5 = (bf16[320,768]{1,0:T(8,128)(2,1)S(1)}, bf16[320,768]{1,0:T(8,128)(2,1)S(1)}, u32[]{:S(2)}, u32[]{:S(2)}) collective-permute-start(bf16[320,768]{1,0:T(8,128)(2,1)S(1)} %collective-permute-done.4.refs_2_), channel_id=1, source_target_pairs={{0,2},{1,5},{2,6},{3,1},{4,0},{5,9},{6,10},{7,3},{8,4},{9,13},{10,... | collective-permute-start | bytes 1474568 | tf_op jit(solution)/shard_map/ppermute | solution.py:341
  24.6 3.3 %collective-permute-done.9.refs_2_ = bf16[320,768]{1,0:T(8,128)(2,1)S(1)} collective-permute-done((bf16[320,768]{1,0:T(8,128)(2,1)S(1)}, bf16[320,768]{1,0:T(8,128)(2,1)S(1)}, u32[]{:S(2)}, u32[]{:S(2)}) %collective-permute-start.9) | collective-permute-done | bytes 491552 | tf_op jit(solution)/shard_map/ppermute | solution.py:341
  27.9 2.0 %collective-permute-start.11 = (bf16[320,768]{1,0:T(8,128)(2,1)S(1)}, bf16[320,768]{1,0:T(8,128)(2,1)S(1)}, u32[]{:S(2)}, u32[]{:S(2)}) collective-permute-start(bf16[320,768]{1,0:T(8,128)(2,1)S(1)} %collective-permute-done.9.refs_2_), channel_id=1, source_target_pairs={{0,2},{1,5},{2,6},{3,1},{4,0},{5,9},{6,10},{7,3},{8,4},{9,13},{10,... | collective-permute-start | bytes 1474568 | tf_op jit(solution)/shard_map/ppermute | solution.py:341
  29.9 3.3 %collective-permute-done.5.refs_3_ = bf16[320,768]{1,0:T(8,128)(2,1)S(1)} collective-permute-done((bf16[320,768]{1,0:T(8,128)(2,1)S(1)}, bf16[320,768]{1,0:T(8,128)(2,1)S(1)}, u32[]{:S(2)}, u32[]{:S(2)}) %collective-permute-start.5) | collective-permute-done | bytes 491552 | tf_op jit(solution)/shard_map/ppermute | solution.py:341
  33.2 2.0 %collective-permute-start.8 = (bf16[320,512]{1,0:T(8,128)(2,1)S(1)}, bf16[320,512]{1,0:T(8,128)(2,1)S(1)}, u32[]{:S(2)}, u32[]{:S(2)}) collective-permute-start(bf16[320,512]{1,0:T(8,128)(2,1)S(1)} %get-tuple-element.44.refs_0_), channel_id=1, source_target_pairs={{0,2},{1,5},{2,6},{3,1},{4,0},{5,9},{6,10},{7,3},{8,4},{9,13},{10,... | collective-permute-start | bytes 983048 | tf_op jit(solution)/shard_map/ppermute | solution.py:341
  35.8 2.7 %collective-permute-done.11.refs_3_ = bf16[320,768]{1,0:T(8,128)(2,1)S(1)} collective-permute-done((bf16[320,768]{1,0:T(8,128)(2,1)S(1)}, bf16[320,768]{1,0:T(8,128)(2,1)S(1)}, u32[]{:S(2)}, u32[]{:S(2)}) %collective-permute-start.11) | collective-permute-done | bytes 491552 | tf_op jit(solution)/shard_map/ppermute | solution.py:341
  38.5 1.9 %collective-permute-start.20 = (f32[1,5120]{1,0:T(1,128)S(1)}, f32[1,5120]{1,0:T(1,128)S(1)}, u32[]{:S(2)}, u32[]{:S(2)}) collective-permute-start(f32[1,5120]{1,0:T(1,128)S(1)} %scale_gate.1.refs_3_.refs_2_), channel_id=1, source_target_pairs={{0,16},{16,0},{1,17},{17,1},{2,18},{18,2},{3,19},{19,3},{4,20},{20... | collective-permute-start | bytes 61448 | tf_op jit(solution)/shard_map/ppermute | solution.py:46
  40.4 1.5 %collective-permute-done.2.far_ref = bf16[224,2560]{1,0:T(8,128)(2,1)S(1)} collective-permute-done((bf16[224,2560]{1,0:T(8,128)(2,1)S(1)}, bf16[224,2560]{1,0:T(8,128)(2,1)S(1)}, u32[]{:S(2)}, u32[]{:S(2)}) %collective-permute-start.2) | collective-permute-done | bytes 1146912 | tf_op jit(solution)/shard_map/ppermute | solution.py:46
  44.4 3.0 %project.9.refs_2_ = f32[448,768]{1,0:T(8,128)S(1)} custom-call(s32[2,8,6]{2,1,0:T(8,128)S(1)} %copy-done.5, bf16[8,448,320]{2,1,0:T(8,128)(2,1)S(1)} %arrange.1.rows_ref, bf16[320,768]{1,0:T(8,128)(2,1)S(1)} %get-tuple-element.40.refs_0_, bf16[320,768]{1,0:T(8,128)(2,1)S(1)} %collective-permute-done.3.refs_1_, ...), custom_call_target="tpu_custom_call" | custom-call | tf_op jit(solution)/shard_map/project/pallas_call | solution.py:250
  47.3 3.3 %project.8.refs_1_ = f32[448,768]{1,0:T(8,128)S(1)} custom-call(s32[2,8,7]{2,1,0:T(8,128)S(1)} %copy-done.4, bf16[8,448,320]{2,1,0:T(8,128)(2,1)S(1)} %arrange.1.rows_ref, bf16[320,768]{1,0:T(8,128)(2,1)S(1)} %get-tuple-element.43.refs_0_, bf16[320,768]{1,0:T(8,128)(2,1)S(1)} %collective-permute-done.6.refs_1_, ...), custom_call_target="tpu_custom_call" | custom-call | tf_op jit(solution)/shard_map/project/pallas_call | solution.py:250
  52.4 1.6 %project.10 = (bf16[224,768]{1,0:T(8,128)(2,1)S(1)}, bf16[224,768]{1,0:T(8,128)(2,1)S(1)}) custom-call(s32[2,8,2]{2,1,0:T(8,128)S(1)} %copy-done.3, bf16[8,448,320]{2,1,0:T(8,128)(2,1)S(1)} %arrange.1.rows_ref, bf16[320,768]{1,0:T(8,128)(2,1)S(1)} %collective-permute-done.13.refs_0_, bf16[320,768]{1,0:T(8,128)(2,1)S(1)} %collective-permute-done.21.refs_1_, ...), custom_call_target="tpu_custom_call" | custom-call | flops 660602880 | bytes 2244608 | tf_op jit(solution)/shard_map/project/pallas_call | solution.py:250
  55.6 1.4 %collective-permute-start.26 = (bf16[224,768]{1,0:T(8,128)(2,1)S(1)}, bf16[224,768]{1,0:T(8,128)(2,1)S(1)}, u32[]{:S(2)}, u32[]{:S(2)}) collective-permute-start(bf16[224,768]{1,0:T(8,128)(2,1)S(1)} %get-tuple-element.59), channel_id=1, source_target_pairs={{0,16},{16,0},{1,17},{17,1},{2,18},{18,2},{3,19},{19,3},{4,20},{20... | collective-permute-start | bytes 1032200 | tf_op jit(solution)/shard_map/ppermute | solution.py:46
  57.0 1.3 %collective-permute-done.15.refs_2_ = bf16[320,512]{1,0:T(8,128)(2,1)S(1)} collective-permute-done((bf16[320,512]{1,0:T(8,128)(2,1)S(1)}, bf16[320,512]{1,0:T(8,128)(2,1)S(1)}, u32[]{:S(2)}, u32[]{:S(2)}) %collective-permute-start.15) | collective-permute-done | bytes 327712 | tf_op jit(solution)/shard_map/ppermute | solution.py:341
  59.5 2.4 %collective-permute-done.25.refs_2_ = bf16[320,512]{1,0:T(8,128)(2,1)S(1)} collective-permute-done((bf16[320,512]{1,0:T(8,128)(2,1)S(1)}, bf16[320,512]{1,0:T(8,128)(2,1)S(1)}, u32[]{:S(2)}, u32[]{:S(2)}) %collective-permute-start.25) | collective-permute-done | bytes 327712 | tf_op jit(solution)/shard_map/ppermute | solution.py:341
  63.1 1.6 %collective-permute-start.32 = (bf16[224,768]{1,0:T(8,128)(2,1)S(1)}, bf16[224,768]{1,0:T(8,128)(2,1)S(1)}, u32[]{:S(2)}, u32[]{:S(2)}) collective-permute-start(bf16[224,768]{1,0:T(8,128)(2,1)S(1)} %get-tuple-element.65), channel_id=1, source_target_pairs={{0,16},{16,0},{1,17},{17,1},{2,18},{18,2},{3,19},{19,3},{4,20},{20... | collective-permute-start | bytes 1032200 | tf_op jit(solution)/shard_map/ppermute | solution.py:46
  64.7 1.4 %collective-permute-done.26.refs_1_ = bf16[224,768]{1,0:T(8,128)(2,1)S(1)} collective-permute-done((bf16[224,768]{1,0:T(8,128)(2,1)S(1)}, bf16[224,768]{1,0:T(8,128)(2,1)S(1)}, u32[]{:S(2)}, u32[]{:S(2)}) %collective-permute-start.26) | collective-permute-done | bytes 344096 | tf_op jit(solution)/shard_map/ppermute | solution.py:46
  66.1 1.7 %collective-permute-start.28 = (bf16[320,512]{1,0:T(8,128)(2,1)S(1)}, bf16[320,512]{1,0:T(8,128)(2,1)S(1)}, u32[]{:S(2)}, u32[]{:S(2)}) collective-permute-start(bf16[320,512]{1,0:T(8,128)(2,1)S(1)} %collective-permute-done.25.refs_2_), channel_id=1, source_target_pairs={{0,2},{1,5},{2,6},{3,1},{4,0},{5,9},{6,10},{7,3},{8,4},{9,13},{10,... | collective-permute-start | bytes 983048 | tf_op jit(solution)/shard_map/ppermute | solution.py:341
  68.4 2.2 %project.14.refs_2_ = f32[448,512]{1,0:T(8,128)S(1)} custom-call(s32[2,8,6]{2,1,0:T(8,128)S(1)} %copy-done.5, bf16[8,448,320]{2,1,0:T(8,128)(2,1)S(1)} %arrange.1.rows_ref, bf16[320,512]{1,0:T(8,128)(2,1)S(1)} %get-tuple-element.44.refs_0_, bf16[320,512]{1,0:T(8,128)(2,1)S(1)} %collective-permute-done.8.refs_1_, ...), custom_call_target="tpu_custom_call" | custom-call | tf_op jit(solution)/shard_map/project/pallas_call | solution.py:250
  70.6 2.5 %collective-permute-done.28.refs_3_ = bf16[320,512]{1,0:T(8,128)(2,1)S(1)} collective-permute-done((bf16[320,512]{1,0:T(8,128)(2,1)S(1)}, bf16[320,512]{1,0:T(8,128)(2,1)S(1)}, u32[]{:S(2)}, u32[]{:S(2)}) %collective-permute-start.28) | collective-permute-done | bytes 327712 | tf_op jit(solution)/shard_map/ppermute | solution.py:341
  73.2 2.5 %project.12.refs_1_ = f32[448,512]{1,0:T(8,128)S(1)} custom-call(s32[2,8,7]{2,1,0:T(8,128)S(1)} %copy-done.4, bf16[8,448,320]{2,1,0:T(8,128)(2,1)S(1)} %arrange.1.rows_ref, bf16[320,512]{1,0:T(8,128)(2,1)S(1)} %get-tuple-element.52.refs_0_, bf16[320,512]{1,0:T(8,128)(2,1)S(1)} %collective-permute-done.19.refs_1_, ...), custom_call_target="tpu_custom_call" | custom-call | tf_op jit(solution)/shard_map/project/pallas_call | solution.py:250
  78.6 1.5 %collective-permute-start.35 = (bf16[224,512]{1,0:T(8,128)(2,1)S(1)}, bf16[224,512]{1,0:T(8,128)(2,1)S(1)}, u32[]{:S(2)}, u32[]{:S(2)}) collective-permute-start(bf16[224,512]{1,0:T(8,128)(2,1)S(1)} %get-tuple-element.68), channel_id=1, source_target_pairs={{0,16},{16,0},{1,17},{17,1},{2,18},{18,2},{3,19},{19,3},{4,20},{20... | collective-permute-start | bytes 688136 | tf_op jit(solution)/shard_map/ppermute | solution.py:46
  81.9 5.3 %collective-permute-done.35.refs_5_ = bf16[224,512]{1,0:T(8,128)(2,1)S(1)} collective-permute-done((bf16[224,512]{1,0:T(8,128)(2,1)S(1)}, bf16[224,512]{1,0:T(8,128)(2,1)S(1)}, u32[]{:S(2)}, u32[]{:S(2)}) %collective-permute-start.35) | collective-permute-done | bytes 229408 | tf_op jit(solution)/shard_map/ppermute | solution.py:46
  88.4 2.8 %collective-permute-done.31.refs_1_ = bf16[224,512]{1,0:T(8,128)(2,1)S(1)} collective-permute-done((bf16[224,512]{1,0:T(8,128)(2,1)S(1)}, bf16[224,512]{1,0:T(8,128)(2,1)S(1)}, u32[]{:S(2)}, u32[]{:S(2)}) %collective-permute-start.31) | collective-permute-done | bytes 229408 | tf_op jit(solution)/shard_map/ppermute | solution.py:46
  (72 shorter events, 18.9 us)
Async XLA Ops:
  1.7 5.1 %collective-permute-start.1 = (bf16[2,112,1280]{2,1,0:T(8,128)(2,1)S(1)}, bf16[2,112,1280]{2,1,0:T(8,128)(2,1)S(1)}, u32[]{:S(2)}, u32[]{:S(2)}) collective-permute-start(bf16[2,112,1280]{2,1,0:T(8,128)(2,1)S(1)} %bitcast.10), channel_id=1, source_target_pairs={{0,1},{1,0},{2,3},{3,2},{4,5},{5,4},{6,7},{7,6},{8,9},{9,8},{10,11... | collective-permute-start | bytes 1720328 | tf_op jit(solution)/shard_map/ppermute | solution.py:46
  2.3 8.0 %collective-permute-start = (bf16[2,112,1280]{2,1,0:T(8,128)(2,1)S(1)}, bf16[2,112,1280]{2,1,0:T(8,128)(2,1)S(1)}, u32[]{:S(2)}, u32[]{:S(2)}) collective-permute-start(bf16[2,112,1280]{2,1,0:T(8,128)(2,1)S(1)} %bitcast.9), channel_id=1, source_target_pairs={{0,1},{1,0},{2,3},{3,2},{4,5},{5,4},{6,7},{7,6},{8,9},{9,8},{10,11... | collective-permute-start | bytes 1720328 | tf_op jit(solution)/shard_map/ppermute | solution.py:46
  2.3 11.3 %collective-permute-start.3 = (bf16[320,768]{1,0:T(8,128)(2,1)S(1)}, bf16[320,768]{1,0:T(8,128)(2,1)S(1)}, u32[]{:S(2)}, u32[]{:S(2)}) collective-permute-start(bf16[320,768]{1,0:T(8,128)(2,1)S(1)} %get-tuple-element.40.refs_0_), channel_id=1, source_target_pairs={{0,2},{1,5},{2,6},{3,1},{4,0},{5,9},{6,10},{7,3},{8,4},{9,13},{10,... | collective-permute-start | bytes 1474568 | tf_op jit(solution)/shard_map/ppermute | solution.py:341
  5.3 12.1 %collective-permute-start.6 = (bf16[320,768]{1,0:T(8,128)(2,1)S(1)}, bf16[320,768]{1,0:T(8,128)(2,1)S(1)}, u32[]{:S(2)}, u32[]{:S(2)}) collective-permute-start(bf16[320,768]{1,0:T(8,128)(2,1)S(1)} %get-tuple-element.43.refs_0_), channel_id=1, source_target_pairs={{0,2},{1,5},{2,6},{3,1},{4,0},{5,9},{6,10},{7,3},{8,4},{9,13},{10,... | collective-permute-start | bytes 1474568 | tf_op jit(solution)/shard_map/ppermute | solution.py:341
  13.7 9.0 %collective-permute-start.4 = (bf16[320,768]{1,0:T(8,128)(2,1)S(1)}, bf16[320,768]{1,0:T(8,128)(2,1)S(1)}, u32[]{:S(2)}, u32[]{:S(2)}) collective-permute-start(bf16[320,768]{1,0:T(8,128)(2,1)S(1)} %collective-permute-done.3.refs_1_), channel_id=1, source_target_pairs={{0,2},{1,5},{2,6},{3,1},{4,0},{5,9},{6,10},{7,3},{8,4},{9,13},{10,... | collective-permute-start | bytes 1474568 | tf_op jit(solution)/shard_map/ppermute | solution.py:341
  15.3 26.7 %collective-permute-start.2 = (bf16[224,2560]{1,0:T(8,128)(2,1)S(1)}, bf16[224,2560]{1,0:T(8,128)(2,1)S(1)}, u32[]{:S(2)}, u32[]{:S(2)}) collective-permute-start(bf16[224,2560]{1,0:T(8,128)(2,1)S(1)} %attend.3.near_ref), channel_id=1, source_target_pairs={{0,16},{16,0},{1,17},{17,1},{2,18},{18,2},{3,19},{19,3},{4,20},{20... | collective-permute-start | bytes 3440648 | tf_op jit(solution)/shard_map/ppermute | solution.py:46
  17.4 10.5 %collective-permute-start.9 = (bf16[320,768]{1,0:T(8,128)(2,1)S(1)}, bf16[320,768]{1,0:T(8,128)(2,1)S(1)}, u32[]{:S(2)}, u32[]{:S(2)}) collective-permute-start(bf16[320,768]{1,0:T(8,128)(2,1)S(1)} %collective-permute-done.6.refs_1_), channel_id=1, source_target_pairs={{0,2},{1,5},{2,6},{3,1},{4,0},{5,9},{6,10},{7,3},{8,4},{9,13},{10,... | collective-permute-start | bytes 1474568 | tf_op jit(solution)/shard_map/ppermute | solution.py:341
  19.4 8.6 %collective-permute-start.10 = (bf16[320,768]{1,0:T(8,128)(2,1)S(1)}, bf16[320,768]{1,0:T(8,128)(2,1)S(1)}, u32[]{:S(2)}, u32[]{:S(2)}) collective-permute-start(bf16[320,768]{1,0:T(8,128)(2,1)S(1)} %collective-permute-done.3.refs_1_), channel_id=1, source_target_pairs={{0,1},{1,0},{2,3},{3,2},{4,5},{5,4},{6,7},{7,6},{8,9},{9,8},{10,11... | collective-permute-start | bytes 1474568 | tf_op jit(solution)/shard_map/ppermute | solution.py:46
  20.5 9.4 %collective-permute-start.7 = (bf16[320,768]{1,0:T(8,128)(2,1)S(1)}, bf16[320,768]{1,0:T(8,128)(2,1)S(1)}, u32[]{:S(2)}, u32[]{:S(2)}) collective-permute-start(bf16[320,768]{1,0:T(8,128)(2,1)S(1)} %collective-permute-done.6.refs_1_), channel_id=1, source_target_pairs={{0,1},{1,0},{2,3},{3,2},{4,5},{5,4},{6,7},{7,6},{8,9},{9,8},{10,11... | collective-permute-start | bytes 1474568 | tf_op jit(solution)/shard_map/ppermute | solution.py:46
  22.7 10.5 %collective-permute-start.5 = (bf16[320,768]{1,0:T(8,128)(2,1)S(1)}, bf16[320,768]{1,0:T(8,128)(2,1)S(1)}, u32[]{:S(2)}, u32[]{:S(2)}) collective-permute-start(bf16[320,768]{1,0:T(8,128)(2,1)S(1)} %collective-permute-done.4.refs_2_), channel_id=1, source_target_pairs={{0,2},{1,5},{2,6},{3,1},{4,0},{5,9},{6,10},{7,3},{8,4},{9,13},{10,... | collective-permute-start | bytes 1474568 | tf_op jit(solution)/shard_map/ppermute | solution.py:341
  27.9 10.5 %collective-permute-start.11 = (bf16[320,768]{1,0:T(8,128)(2,1)S(1)}, bf16[320,768]{1,0:T(8,128)(2,1)S(1)}, u32[]{:S(2)}, u32[]{:S(2)}) collective-permute-start(bf16[320,768]{1,0:T(8,128)(2,1)S(1)} %collective-permute-done.9.refs_2_), channel_id=1, source_target_pairs={{0,2},{1,5},{2,6},{3,1},{4,0},{5,9},{6,10},{7,3},{8,4},{9,13},{10,... | collective-permute-start | bytes 1474568 | tf_op jit(solution)/shard_map/ppermute | solution.py:341
  29.9 10.5 %collective-permute-start.12 = (bf16[320,768]{1,0:T(8,128)(2,1)S(1)}, bf16[320,768]{1,0:T(8,128)(2,1)S(1)}, u32[]{:S(2)}, u32[]{:S(2)}) collective-permute-start(bf16[320,768]{1,0:T(8,128)(2,1)S(1)} %collective-permute-done.4.refs_2_), channel_id=1, source_target_pairs={{0,1},{1,0},{2,3},{3,2},{4,5},{5,4},{6,7},{7,6},{8,9},{9,8},{10,11... | collective-permute-start | bytes 1474568 | tf_op jit(solution)/shard_map/ppermute | solution.py:46
  33.2 9.6 %collective-permute-start.8 = (bf16[320,512]{1,0:T(8,128)(2,1)S(1)}, bf16[320,512]{1,0:T(8,128)(2,1)S(1)}, u32[]{:S(2)}, u32[]{:S(2)}) collective-permute-start(bf16[320,512]{1,0:T(8,128)(2,1)S(1)} %get-tuple-element.44.refs_0_), channel_id=1, source_target_pairs={{0,2},{1,5},{2,6},{3,1},{4,0},{5,9},{6,10},{7,3},{8,4},{9,13},{10,... | collective-permute-start | bytes 983048 | tf_op jit(solution)/shard_map/ppermute | solution.py:341
  35.2 8.1 %collective-permute-start.18 = (bf16[320,768]{1,0:T(8,128)(2,1)S(1)}, bf16[320,768]{1,0:T(8,128)(2,1)S(1)}, u32[]{:S(2)}, u32[]{:S(2)}) collective-permute-start(bf16[320,768]{1,0:T(8,128)(2,1)S(1)} %collective-permute-done.9.refs_2_), channel_id=1, source_target_pairs={{0,1},{1,0},{2,3},{3,2},{4,5},{5,4},{6,7},{7,6},{8,9},{9,8},{10,11... | collective-permute-start | bytes 1474568 | tf_op jit(solution)/shard_map/ppermute | solution.py:46
  40.4 6.9 %collective-permute-start.14 = (bf16[320,768]{1,0:T(8,128)(2,1)S(1)}, bf16[320,768]{1,0:T(8,128)(2,1)S(1)}, u32[]{:S(2)}, u32[]{:S(2)}) collective-permute-start(bf16[320,768]{1,0:T(8,128)(2,1)S(1)} %collective-permute-done.5.refs_3_), channel_id=1, source_target_pairs={{0,1},{1,0},{2,3},{3,2},{4,5},{5,4},{6,7},{7,6},{8,9},{9,8},{10,11... | collective-permute-start | bytes 1474568 | tf_op jit(solution)/shard_map/ppermute | solution.py:46
  42.0 9.3 %collective-permute-start.13 = (bf16[320,768]{1,0:T(8,128)(2,1)S(1)}, bf16[320,768]{1,0:T(8,128)(2,1)S(1)}, u32[]{:S(2)}, u32[]{:S(2)}) collective-permute-start(bf16[320,768]{1,0:T(8,128)(2,1)S(1)} %collective-permute-done.5.refs_3_), channel_id=1, source_target_pairs={{0,2},{1,5},{2,6},{3,1},{4,0},{5,9},{6,10},{7,3},{8,4},{9,13},{10,... | collective-permute-start | bytes 1474568 | tf_op jit(solution)/shard_map/ppermute | solution.py:341
  42.8 9.6 %collective-permute-start.21 = (bf16[320,768]{1,0:T(8,128)(2,1)S(1)}, bf16[320,768]{1,0:T(8,128)(2,1)S(1)}, u32[]{:S(2)}, u32[]{:S(2)}) collective-permute-start(bf16[320,768]{1,0:T(8,128)(2,1)S(1)} %collective-permute-done.11.refs_3_), channel_id=1, source_target_pairs={{0,1},{1,0},{2,3},{3,2},{4,5},{5,4},{6,7},{7,6},{8,9},{9,8},{10,11... | collective-permute-start | bytes 1474568 | tf_op jit(solution)/shard_map/ppermute | solution.py:46
  43.2 11.1 %collective-permute-start.19 = (bf16[320,512]{1,0:T(8,128)(2,1)S(1)}, bf16[320,512]{1,0:T(8,128)(2,1)S(1)}, u32[]{:S(2)}, u32[]{:S(2)}) collective-permute-start(bf16[320,512]{1,0:T(8,128)(2,1)S(1)} %get-tuple-element.52.refs_0_), channel_id=1, source_target_pairs={{0,2},{1,5},{2,6},{3,1},{4,0},{5,9},{6,10},{7,3},{8,4},{9,13},{10,... | collective-permute-start | bytes 983048 | tf_op jit(solution)/shard_map/ppermute | solution.py:341
  50.7 6.4 %collective-permute-start.16 = (bf16[320,512]{1,0:T(8,128)(2,1)S(1)}, bf16[320,512]{1,0:T(8,128)(2,1)S(1)}, u32[]{:S(2)}, u32[]{:S(2)}) collective-permute-start(bf16[320,512]{1,0:T(8,128)(2,1)S(1)} %collective-permute-done.8.refs_1_), channel_id=1, source_target_pairs={{0,1},{1,0},{2,3},{3,2},{4,5},{5,4},{6,7},{7,6},{8,9},{9,8},{10,11... | collective-permute-start | bytes 983048 | tf_op jit(solution)/shard_map/ppermute | solution.py:46
  51.3 7.1 %collective-permute-start.15 = (bf16[320,512]{1,0:T(8,128)(2,1)S(1)}, bf16[320,512]{1,0:T(8,128)(2,1)S(1)}, u32[]{:S(2)}, u32[]{:S(2)}) collective-permute-start(bf16[320,512]{1,0:T(8,128)(2,1)S(1)} %collective-permute-done.8.refs_1_), channel_id=1, source_target_pairs={{0,2},{1,5},{2,6},{3,1},{4,0},{5,9},{6,10},{7,3},{8,4},{9,13},{10,... | collective-permute-start | bytes 983048 | tf_op jit(solution)/shard_map/ppermute | solution.py:341
  54.3 7.6 %collective-permute-start.25 = (bf16[320,512]{1,0:T(8,128)(2,1)S(1)}, bf16[320,512]{1,0:T(8,128)(2,1)S(1)}, u32[]{:S(2)}, u32[]{:S(2)}) collective-permute-start(bf16[320,512]{1,0:T(8,128)(2,1)S(1)} %collective-permute-done.19.refs_1_), channel_id=1, source_target_pairs={{0,2},{1,5},{2,6},{3,1},{4,0},{5,9},{6,10},{7,3},{8,4},{9,13},{10,... | collective-permute-start | bytes 983048 | tf_op jit(solution)/shard_map/ppermute | solution.py:341
  55.6 6.3 %collective-permute-start.27 = (bf16[320,768]{1,0:T(8,128)(2,1)S(1)}, bf16[320,768]{1,0:T(8,128)(2,1)S(1)}, u32[]{:S(2)}, u32[]{:S(2)}) collective-permute-start(bf16[320,768]{1,0:T(8,128)(2,1)S(1)} %collective-permute-done.13.refs_0_), channel_id=1, source_target_pairs={{0,1},{1,0},{2,3},{3,2},{4,5},{5,4},{6,7},{7,6},{8,9},{9,8},{10,11... | collective-permute-start | bytes 1474568 | tf_op jit(solution)/shard_map/ppermute | solution.py:46
  55.6 10.5 %collective-permute-start.26 = (bf16[224,768]{1,0:T(8,128)(2,1)S(1)}, bf16[224,768]{1,0:T(8,128)(2,1)S(1)}, u32[]{:S(2)}, u32[]{:S(2)}) collective-permute-start(bf16[224,768]{1,0:T(8,128)(2,1)S(1)} %get-tuple-element.59), channel_id=1, source_target_pairs={{0,16},{16,0},{1,17},{17,1},{2,18},{18,2},{3,19},{19,3},{4,20},{20... | collective-permute-start | bytes 1032200 | tf_op jit(solution)/shard_map/ppermute | solution.py:46
  58.4 7.7 %collective-permute-start.17 = (bf16[320,512]{1,0:T(8,128)(2,1)S(1)}, bf16[320,512]{1,0:T(8,128)(2,1)S(1)}, u32[]{:S(2)}, u32[]{:S(2)}) collective-permute-start(bf16[320,512]{1,0:T(8,128)(2,1)S(1)} %collective-permute-done.15.refs_2_), channel_id=1, source_target_pairs={{0,2},{1,5},{2,6},{3,1},{4,0},{5,9},{6,10},{7,3},{8,4},{9,13},{10,... | collective-permute-start | bytes 983048 | tf_op jit(solution)/shard_map/ppermute | solution.py:341
  59.5 8.3 %collective-permute-start.22 = (bf16[320,512]{1,0:T(8,128)(2,1)S(1)}, bf16[320,512]{1,0:T(8,128)(2,1)S(1)}, u32[]{:S(2)}, u32[]{:S(2)}) collective-permute-start(bf16[320,512]{1,0:T(8,128)(2,1)S(1)} %collective-permute-done.19.refs_1_), channel_id=1, source_target_pairs={{0,1},{1,0},{2,3},{3,2},{4,5},{5,4},{6,7},{7,6},{8,9},{9,8},{10,11... | collective-permute-start | bytes 983048 | tf_op jit(solution)/shard_map/ppermute | solution.py:46
  61.9 5.9 %collective-permute-start.33 = (bf16[320,512]{1,0:T(8,128)(2,1)S(1)}, bf16[320,512]{1,0:T(8,128)(2,1)S(1)}, u32[]{:S(2)}, u32[]{:S(2)}) collective-permute-start(bf16[320,512]{1,0:T(8,128)(2,1)S(1)} %collective-permute-done.25.refs_2_), channel_id=1, source_target_pairs={{0,1},{1,0},{2,3},{3,2},{4,5},{5,4},{6,7},{7,6},{8,9},{9,8},{10,11... | collective-permute-start | bytes 983048 | tf_op jit(solution)/shard_map/ppermute | solution.py:46
  63.1 12.5 %collective-permute-start.32 = (bf16[224,768]{1,0:T(8,128)(2,1)S(1)}, bf16[224,768]{1,0:T(8,128)(2,1)S(1)}, u32[]{:S(2)}, u32[]{:S(2)}) collective-permute-start(bf16[224,768]{1,0:T(8,128)(2,1)S(1)} %get-tuple-element.65), channel_id=1, source_target_pairs={{0,16},{16,0},{1,17},{17,1},{2,18},{18,2},{3,19},{19,3},{4,20},{20... | collective-permute-start | bytes 1032200 | tf_op jit(solution)/shard_map/ppermute | solution.py:46
  66.1 7.1 %collective-permute-start.28 = (bf16[320,512]{1,0:T(8,128)(2,1)S(1)}, bf16[320,512]{1,0:T(8,128)(2,1)S(1)}, u32[]{:S(2)}, u32[]{:S(2)}) collective-permute-start(bf16[320,512]{1,0:T(8,128)(2,1)S(1)} %collective-permute-done.25.refs_2_), channel_id=1, source_target_pairs={{0,2},{1,5},{2,6},{3,1},{4,0},{5,9},{6,10},{7,3},{8,4},{9,13},{10,... | collective-permute-start | bytes 983048 | tf_op jit(solution)/shard_map/ppermute | solution.py:341
  67.8 5.4 %collective-permute-start.30 = (bf16[320,512]{1,0:T(8,128)(2,1)S(1)}, bf16[320,512]{1,0:T(8,128)(2,1)S(1)}, u32[]{:S(2)}, u32[]{:S(2)}) collective-permute-start(bf16[320,512]{1,0:T(8,128)(2,1)S(1)} %collective-permute-done.17.refs_3_), channel_id=1, source_target_pairs={{0,1},{1,0},{2,3},{3,2},{4,5},{5,4},{6,7},{7,6},{8,9},{9,8},{10,11... | collective-permute-start | bytes 983048 | tf_op jit(solution)/shard_map/ppermute | solution.py:46
  67.8 8.9 %collective-permute-start.23 = (bf16[320,512]{1,0:T(8,128)(2,1)S(1)}, bf16[320,512]{1,0:T(8,128)(2,1)S(1)}, u32[]{:S(2)}, u32[]{:S(2)}) collective-permute-start(bf16[320,512]{1,0:T(8,128)(2,1)S(1)} %collective-permute-done.17.refs_3_), channel_id=1, source_target_pairs={{0,2},{1,5},{2,6},{3,1},{4,0},{5,9},{6,10},{7,3},{8,4},{9,13},{10,... | collective-permute-start | bytes 983048 | tf_op jit(solution)/shard_map/ppermute | solution.py:341
  78.6 8.5 %collective-permute-start.35 = (bf16[224,512]{1,0:T(8,128)(2,1)S(1)}, bf16[224,512]{1,0:T(8,128)(2,1)S(1)}, u32[]{:S(2)}, u32[]{:S(2)}) collective-permute-start(bf16[224,512]{1,0:T(8,128)(2,1)S(1)} %get-tuple-element.68), channel_id=1, source_target_pairs={{0,16},{16,0},{1,17},{17,1},{2,18},{18,2},{3,19},{19,3},{4,20},{20... | collective-permute-start | bytes 688136 | tf_op jit(solution)/shard_map/ppermute | solution.py:46
  81.2 10.0 %collective-permute-start.31 = (bf16[224,512]{1,0:T(8,128)(2,1)S(1)}, bf16[224,512]{1,0:T(8,128)(2,1)S(1)}, u32[]{:S(2)}, u32[]{:S(2)}) collective-permute-start(bf16[224,512]{1,0:T(8,128)(2,1)S(1)} %get-tuple-element.64), channel_id=1, source_target_pairs={{0,16},{16,0},{1,17},{17,1},{2,18},{18,2},{3,19},{19,3},{4,20},{20... | collective-permute-start | bytes 688136 | tf_op jit(solution)/shard_map/ppermute | solution.py:46
  (12 other events, 99.9 us)
